TPU v7x, 128 devices: a whole 4x4x4 slice. The times are simulated.
128 devices in a mesh: ka: 8 (over y_lo, x), pb: 16 (over z, y_hi, core).
Axes of the slice: x: 4, y: 4 (y_hi: 2, y_lo: 2; y = y_hi * 2 + y_lo), z: 4, core: 2. Of those that a mesh axis runs over, the one named last changes fastest.
Arguments:
- occupation: bfloat16 [80, 4, 6400], P('ka'), may hold values from 0.049804688 to 1
- q_offsets: int32 [16, 3], P('pb'), may hold values from 0 to 79
- coupling: bfloat16 [16, 2, 200, 96], P('pb'), may hold values from -0.4375 to 0.4375
- window_bins: int32 [16, 16], P('pb'), may hold values from 0 to 31
- lorentz_table: float32 [32, 6], replicated, may hold values from 0.1 to 1
- lattice: int32 [3, 200], replicated, may hold values from -6 to 6
Outputs:
- collision: float32 [80, 4, 6400], P('ka', None, 'pb')
All inputs are finite; a program needn't handle non-finite values.
Results may differ from a plain program's by a relative error of at most 0.0003.
Values may be sent and summed in bfloat16 or wider, within the bound.
No kernel may reach another device: no remote copies, remote signals or barrier semaphores. Data moves between devices by JAX's collectives and lax.ppermute only.
A program may use at most 128 MiB of HBM per device.

v0:
```python
import math

import jax
import jax.numpy as jnp
from jax import lax
from jax.sharding import PartitionSpec as P

KX = 80
KY = 80
NB = 4
NM = 6


def shifted_2(shard, axis, by):
    size = lax.axis_size(axis)
    return lax.ppermute(shard, axis, [(i, (i + by) % size) for i in range(size)])


def phase_rows(plane_z, lattice, kpt_x, kpt_y, grid_depth):
    first_term = kpt_x[None, :] * lattice[0][:, None] % KX * (KY * grid_depth)
    second_term = kpt_y[None, :] * lattice[1][:, None] % KY * (KX * grid_depth)
    third_term = plane_z * lattice[2] % grid_depth * (KX * KY)
    flat_index = first_term + second_term + third_term[:, None]
    angles = flat_index.astype(jnp.float32) * (2.0 * math.pi / (KX * KY * grid_depth))
    return jnp.concatenate([jnp.cos(angles), jnp.sin(angles)], axis=0).astype(jnp.bfloat16)


def coupling_rows(q_block):
    upper_half = jnp.concatenate([q_block[0], q_block[1]], axis=1)
    lower_half = jnp.concatenate([-q_block[1], q_block[0]], axis=1)
    return jnp.concatenate([upper_half, lower_half], axis=0).T


def channel_weights(bins_row, lorentz_table):
    levels = jnp.arange(lorentz_table.shape[0], dtype=jnp.int32)
    onehot = (bins_row[:, None] == levels[None, :]).astype(jnp.float32)
    table = jnp.dot(
        onehot, lorentz_table, precision=lax.Precision.HIGHEST, preferred_element_type=jnp.float32
    )
    return table.reshape(-1)


def plane_term(phases, mat_t, weight, own_occ, arrived):
    couple = jnp.dot(mat_t, phases, preferred_element_type=jnp.float32)
    channels = weight.shape[0]
    squared = couple[:channels] * couple[:channels] + couple[channels:] * couple[channels:]
    strength = (squared * weight[:, None]).reshape(NB, NB, NM, -1).sum(axis=2)
    outgoing = strength.sum(axis=1)
    incoming = jnp.sum(strength * arrived.astype(jnp.float32)[None, :, :], axis=1)
    return incoming - outgoing * own_occ.astype(jnp.float32)


def roll_plane(slab_part, shift_x, shift_y):
    depth_here = slab_part.shape[0]
    shaped = slab_part.reshape(depth_here, NB, KX, KY)
    rolled = jnp.roll(shaped, (-shift_x, -shift_y), axis=(2, 3))
    return rolled.reshape(depth_here, NB, KX * KY)


def local(occupation, q_offsets, coupling, window_bins, lorentz_table, lattice):
    kz_local = occupation.shape[0]
    plane_size = occupation.shape[2]
    ka_size = lax.axis_size("ka")
    grid_depth = kz_local * ka_size
    q_local = q_offsets.shape[0]
    start_plane = lax.axis_index("ka") * kz_local
    hop_count = q_offsets[:, 2] // kz_local
    plane_rest = q_offsets[:, 2] % kz_local
    current = occupation[None]
    for bit_pos in range(ka_size.bit_length() - 1):
        arrived = shifted_2(current, "ka", ka_size - (1 << bit_pos))
        taken = hop_count >> bit_pos & 1 == 1
        current = jnp.where(taken[:, None, None, None], arrived, current)
    following = shifted_2(current, "ka", ka_size - 1)
    stacked = jnp.concatenate([current, following], axis=1)
    window = lax.dynamic_slice_in_dim(stacked[0], plane_rest[0], kz_local, 0)
    pieces = [roll_plane(window, q_offsets[0, 0], q_offsets[0, 1])]
    shifted = jnp.stack(pieces)
    flat_k = jnp.arange(plane_size, dtype=jnp.int32)
    kpt_x = flat_k // KY
    kpt_y = flat_k % KY
    q_mats = jnp.stack([coupling_rows(coupling[0])])
    q_weights = jnp.stack([channel_weights(window_bins[0], lorentz_table)])
    shifted = jnp.swapaxes(shifted, 0, 1)

    def one_plane(inputs):
        local_z, own_occ, moved_here = inputs
        phases = phase_rows(start_plane + local_z, lattice, kpt_x, kpt_y, grid_depth)

        def add_q(running, q_item):
            mat_t, weight, arrived_q = q_item
            return (running + plane_term(phases, mat_t, weight, own_occ, arrived_q), None)

        return lax.scan(
            add_q, jnp.zeros((NB, plane_size), jnp.float32), (q_mats, q_weights, moved_here)
        )[0]

    q_terms = lax.map(one_plane, (jnp.arange(kz_local, dtype=jnp.int32), occupation, shifted))
    normalize = 1.0 / (q_local * lax.axis_size("pb") * NM)
    combined = lax.psum_scatter(q_terms, "pb", scatter_dimension=2, tiled=True)
    return combined * normalize


def solution(mesh):
    in_specs = (
        P("ka", None, None),
        P("pb", None),
        P("pb", None, None, None),
        P("pb", None),
        P(),
        P(),
    )
    out_specs = P("ka", None, "pb")
    return jax.shard_map(local, mesh=mesh, in_specs=in_specs, out_specs=out_specs, check_vma=False)
```

profile of v0, /device:TPU:1, one launch (start us, length us, event | category | flops | bytes accessed | tf_op | source)
XLA Modules:
  0.0 573.2 jit_solution(11641163313349703606)
XLA Ops:
  6.5 4.3 collective-permute-start
  14.2 7.3 %collective-permute-done = bf16[1,10,4,6400]{3,2,1,0:T(4,128)(2,1)S(1)} collective-permute-done((bf16[1,10,4,6400]{3,2,1,0:T(4,128)(2,1)}, bf16[1,10,4,6400]{3,2,1,0:T(4,128)(2,1)S(1)}, u32[]{:S(2)}, u32[]{:S(2)}) %collective-permute-start) | collective-permute-done | bytes 512032 | tf_op jit(solution)/shard_map/ppermute | solution.py:16
  22.8 2.4 collective-permute-start.1
  25.2 10.8 %collective-permute-done.1 = bf16[1,10,4,6400]{3,2,1,0:T(4,128)(2,1)S(1)} collective-permute-done((bf16[1,10,4,6400]{3,2,1,0:T(4,128)(2,1)S(1)}, bf16[1,10,4,6400]{3,2,1,0:T(4,128)(2,1)S(1)}, u32[]{:S(2)}, u32[]{:S(2)}) %collective-permute-start.1) | collective-permute-done | bytes 512032 | tf_op jit(solution)/shard_map/ppermute | solution.py:16
  38.6 8.2 %collective-permute-done.2 = bf16[1,10,4,6400]{3,2,1,0:T(4,128)(2,1)S(1)} collective-permute-done((bf16[1,10,4,6400]{3,2,1,0:T(4,128)(2,1)S(1)}, bf16[1,10,4,6400]{3,2,1,0:T(4,128)(2,1)S(1)}, u32[]{:S(2)}, u32[]{:S(2)}) %collective-permute-start.2) | collective-permute-done | bytes 512032 | tf_op jit(solution)/shard_map/ppermute | solution.py:16
  46.9 5.2 collective-permute-start.3
  52.9 6.7 %collective-permute-done.3 = bf16[1,10,4,6400]{3,2,1,0:T(4,128)(2,1)S(1)} collective-permute-done((bf16[1,10,4,6400]{3,2,1,0:T(4,128)(2,1)S(1)}, bf16[1,10,4,6400]{3,2,1,0:T(4,128)(2,1)S(1)}, u32[]{:S(2)}, u32[]{:S(2)}) %collective-permute-start.3) | collective-permute-done | bytes 512032 | tf_op jit(solution)/shard_map/ppermute | solution.py:16
  63.2 1.8 transpose_stack_reshape.3
  65.0 358.0 %while.17 = (s32[]{:T(128)}, f32[10,4,6400]{2,1,0:T(4,128)}, s32[3,200]{1,0:T(4,128)S(1)}, s32[10]{0:T(128)S(1)}, s32[]{:T(128)}, /*index=5*/bf16[1,192,400]{2,1...) while((s32[]{:T(128)}, f32[10,4,6400]{2,1,0:T(4,128)}, ...), condition=%wide.region_4.5_spmd.clone, body=%wide.region_0.4_spmd.clone.sunk | while | flops 1024078400 | bytes 31804528 | solution.py:98
  67.2 24.3 %cosine_convert_fusion.2 = (bf16[200,6400]{1,0:T(8,128)(2,1)S(1)}, bf16[200,6400]{1,0:T(8,128)(2,1)S(1)}) fusion(s32[200]{0:T(256)S(1)} %fusion.53, s32[200]{0:T(256)S(1)} %bitcast.85, s32[6400]{0:T(1024)S(1)} %get-tuple-element.284, s32[200]{0:T(256)S(1)} %bitcast.84, s32[6400]{0:T(1024)S(1)} %get-tuple-element.286), kind=kLoop, calls=%fused_computation.14.clone.1 | loop fusion | flops 26880000 | bytes 5173600 | tf_op jit(solution)/shard_map/convert.1
  91.5 2.4 convolution_bitcast_fusion.2
  93.9 1.8 fusion.55
  95.7 1.8 reshape.90
  99.3 1.5 fusion.57
  103.0 24.3 %cosine_convert_fusion.2 = (bf16[200,6400]{1,0:T(8,128)(2,1)S(1)}, bf16[200,6400]{1,0:T(8,128)(2,1)S(1)}) fusion(s32[200]{0:T(256)S(1)} %fusion.53, s32[200]{0:T(256)S(1)} %bitcast.85, s32[6400]{0:T(1024)S(1)} %get-tuple-element.284, s32[200]{0:T(256)S(1)} %bitcast.84, s32[6400]{0:T(1024)S(1)} %get-tuple-element.286), kind=kLoop, calls=%fused_computation.14.clone.1 | loop fusion | flops 26880000 | bytes 5173600 | tf_op jit(solution)/shard_map/convert.1
  127.3 2.4 convolution_bitcast_fusion.2
  129.7 1.8 fusion.55
  131.5 1.8 reshape.90
  135.1 1.5 fusion.57
  138.8 24.3 %cosine_convert_fusion.2 = (bf16[200,6400]{1,0:T(8,128)(2,1)S(1)}, bf16[200,6400]{1,0:T(8,128)(2,1)S(1)}) fusion(s32[200]{0:T(256)S(1)} %fusion.53, s32[200]{0:T(256)S(1)} %bitcast.85, s32[6400]{0:T(1024)S(1)} %get-tuple-element.284, s32[200]{0:T(256)S(1)} %bitcast.84, s32[6400]{0:T(1024)S(1)} %get-tuple-element.286), kind=kLoop, calls=%fused_computation.14.clone.1 | loop fusion | flops 26880000 | bytes 5173600 | tf_op jit(solution)/shard_map/convert.1
  163.1 2.4 convolution_bitcast_fusion.2
  165.5 1.8 fusion.55
  167.3 1.8 reshape.90
  170.9 1.5 fusion.57
  174.6 24.3 %cosine_convert_fusion.2 = (bf16[200,6400]{1,0:T(8,128)(2,1)S(1)}, bf16[200,6400]{1,0:T(8,128)(2,1)S(1)}) fusion(s32[200]{0:T(256)S(1)} %fusion.53, s32[200]{0:T(256)S(1)} %bitcast.85, s32[6400]{0:T(1024)S(1)} %get-tuple-element.284, s32[200]{0:T(256)S(1)} %bitcast.84, s32[6400]{0:T(1024)S(1)} %get-tuple-element.286), kind=kLoop, calls=%fused_computation.14.clone.1 | loop fusion | flops 26880000 | bytes 5173600 | tf_op jit(solution)/shard_map/convert.1
  198.9 2.4 convolution_bitcast_fusion.2
  201.3 1.8 fusion.55
  203.1 1.8 reshape.90
  206.7 1.5 fusion.57
  210.4 24.3 %cosine_convert_fusion.2 = (bf16[200,6400]{1,0:T(8,128)(2,1)S(1)}, bf16[200,6400]{1,0:T(8,128)(2,1)S(1)}) fusion(s32[200]{0:T(256)S(1)} %fusion.53, s32[200]{0:T(256)S(1)} %bitcast.85, s32[6400]{0:T(1024)S(1)} %get-tuple-element.284, s32[200]{0:T(256)S(1)} %bitcast.84, s32[6400]{0:T(1024)S(1)} %get-tuple-element.286), kind=kLoop, calls=%fused_computation.14.clone.1 | loop fusion | flops 26880000 | bytes 5173600 | tf_op jit(solution)/shard_map/convert.1
  234.7 2.4 convolution_bitcast_fusion.2
  237.1 1.8 fusion.55
  238.9 1.8 reshape.90
  242.5 1.5 fusion.57
  246.2 24.3 %cosine_convert_fusion.2 = (bf16[200,6400]{1,0:T(8,128)(2,1)S(1)}, bf16[200,6400]{1,0:T(8,128)(2,1)S(1)}) fusion(s32[200]{0:T(256)S(1)} %fusion.53, s32[200]{0:T(256)S(1)} %bitcast.85, s32[6400]{0:T(1024)S(1)} %get-tuple-element.284, s32[200]{0:T(256)S(1)} %bitcast.84, s32[6400]{0:T(1024)S(1)} %get-tuple-element.286), kind=kLoop, calls=%fused_computation.14.clone.1 | loop fusion | flops 26880000 | bytes 5173600 | tf_op jit(solution)/shard_map/convert.1
  270.5 2.4 convolution_bitcast_fusion.2
  272.9 1.8 fusion.55
  274.7 1.8 reshape.90
  278.3 1.5 fusion.57
  282.0 24.3 %cosine_convert_fusion.2 = (bf16[200,6400]{1,0:T(8,128)(2,1)S(1)}, bf16[200,6400]{1,0:T(8,128)(2,1)S(1)}) fusion(s32[200]{0:T(256)S(1)} %fusion.53, s32[200]{0:T(256)S(1)} %bitcast.85, s32[6400]{0:T(1024)S(1)} %get-tuple-element.284, s32[200]{0:T(256)S(1)} %bitcast.84, s32[6400]{0:T(1024)S(1)} %get-tuple-element.286), kind=kLoop, calls=%fused_computation.14.clone.1 | loop fusion | flops 26880000 | bytes 5173600 | tf_op jit(solution)/shard_map/convert.1
  306.3 2.4 convolution_bitcast_fusion.2
  308.7 1.8 fusion.55
  310.5 1.8 reshape.90
  314.1 1.5 fusion.57
  317.8 24.3 %cosine_convert_fusion.2 = (bf16[200,6400]{1,0:T(8,128)(2,1)S(1)}, bf16[200,6400]{1,0:T(8,128)(2,1)S(1)}) fusion(s32[200]{0:T(256)S(1)} %fusion.53, s32[200]{0:T(256)S(1)} %bitcast.85, s32[6400]{0:T(1024)S(1)} %get-tuple-element.284, s32[200]{0:T(256)S(1)} %bitcast.84, s32[6400]{0:T(1024)S(1)} %get-tuple-element.286), kind=kLoop, calls=%fused_computation.14.clone.1 | loop fusion | flops 26880000 | bytes 5173600 | tf_op jit(solution)/shard_map/convert.1
  342.1 2.4 convolution_bitcast_fusion.2
  344.5 1.8 fusion.55
  346.3 1.8 reshape.90
  349.9 1.5 fusion.57
  353.6 24.3 %cosine_convert_fusion.2 = (bf16[200,6400]{1,0:T(8,128)(2,1)S(1)}, bf16[200,6400]{1,0:T(8,128)(2,1)S(1)}) fusion(s32[200]{0:T(256)S(1)} %fusion.53, s32[200]{0:T(256)S(1)} %bitcast.85, s32[6400]{0:T(1024)S(1)} %get-tuple-element.284, s32[200]{0:T(256)S(1)} %bitcast.84, s32[6400]{0:T(1024)S(1)} %get-tuple-element.286), kind=kLoop, calls=%fused_computation.14.clone.1 | loop fusion | flops 26880000 | bytes 5173600 | tf_op jit(solution)/shard_map/convert.1
  377.9 2.4 convolution_bitcast_fusion.2
  380.3 1.8 fusion.55
  382.1 1.8 reshape.90
  385.7 1.5 fusion.57
  389.4 24.3 %cosine_convert_fusion.2 = (bf16[200,6400]{1,0:T(8,128)(2,1)S(1)}, bf16[200,6400]{1,0:T(8,128)(2,1)S(1)}) fusion(s32[200]{0:T(256)S(1)} %fusion.53, s32[200]{0:T(256)S(1)} %bitcast.85, s32[6400]{0:T(1024)S(1)} %get-tuple-element.284, s32[200]{0:T(256)S(1)} %bitcast.84, s32[6400]{0:T(1024)S(1)} %get-tuple-element.286), kind=kLoop, calls=%fused_computation.14.clone.1 | loop fusion | flops 26880000 | bytes 5173600 | tf_op jit(solution)/shard_map/convert.1
  413.7 2.4 convolution_bitcast_fusion.2
  416.1 1.8 fusion.55
  417.9 1.8 reshape.90
  421.5 1.5 fusion.57
  422.9 25.3 %copy.12 = f32[10,4,6400]{1,0,2:T(8,128)} copy(f32[10,4,6400]{2,1,0:T(4,128)} %get-tuple-element.164) | data formatting | bytes 2048000
  448.2 32.1 %reshape.87 = f32[6400,40]{1,0:T(8,128)} reshape(f32[6400,10,4]{2,1,0:T(8,128)} %bitcast.74) | data formatting | bytes 2048000
  480.4 81.7 %reduce-scatter.4.cloned.1.call-done = f32[400,40]{1,0:T(8,128)} async-done(((f32[6400,40]{1,0:T(8,128)}), f32[400,40]{1,0:T(8,128)}) %reduce-scatter.4.cloned.1.call-update) | async-done | bytes 64016
  562.1 2.1 reshape.88
  564.2 1.5 copy.13
  (97 shorter events, 41.7 us)
Async XLA Ops:
  6.5 31.1 %copy-start = (f32[32,6]{0,1:T(8,128)S(1)}, f32[32,6]{0,1:T(8,128)}, u32[]{:S(2)}) copy-start(f32[32,6]{0,1:T(8,128)} %param.12) | copy-start | bytes 2308
  6.5 45.5 %copy-start.2 = (bf16[1,2,200,96]{2,3,1,0:T(8,128)(2,1)S(1)}, bf16[1,2,200,96]{2,3,1,0:T(8,128)(2,1)}, u32[]{:S(2)}) copy-start(bf16[1,2,200,96]{2,3,1,0:T(8,128)(2,1)} %param.10) | copy-start | bytes 230404
  6.5 555.5 %reduce-scatter.4.cloned.1.call-start = ((), (), s32[]{:S(2)}) async-start(), calls=%async_computation.1 | async-start | bytes 3481600
  6.5 15.0 %collective-permute-start = (bf16[1,10,4,6400]{3,2,1,0:T(4,128)(2,1)}, bf16[1,10,4,6400]{3,2,1,0:T(4,128)(2,1)S(1)}, u32[]{:S(2)}, u32[]{:S(2)}) collective-permute-start(bf16[1,10,4,6400]{3,2,1,0:T(4,128)(2,1)} %bitcast.80), channel_id=1, source_target_pairs={{0,112},{16,0},{32,16},{48,32},{64,48},{80,64},{96,80},{112,96},{1... | collective-permute-start | bytes 1536008 | tf_op jit(solution)/shard_map/ppermute | solution.py:16
  22.8 13.2 %collective-permute-start.1 = (bf16[1,10,4,6400]{3,2,1,0:T(4,128)(2,1)S(1)}, bf16[1,10,4,6400]{3,2,1,0:T(4,128)(2,1)S(1)}, u32[]{:S(2)}, u32[]{:S(2)}) collective-permute-start(bf16[1,10,4,6400]{3,2,1,0:T(4,128)(2,1)S(1)} %broadcast_select_fusion), channel_id=1, source_target_pairs={{0,96},{16,112},{32,0},{48,16},{64,32},{80,48},{96,64},{112,80},{1... | collective-permute-start | bytes 1536008 | tf_op jit(solution)/shard_map/ppermute | solution.py:16
  36.1 10.8 %collective-permute-start.2 = (bf16[1,10,4,6400]{3,2,1,0:T(4,128)(2,1)S(1)}, bf16[1,10,4,6400]{3,2,1,0:T(4,128)(2,1)S(1)}, u32[]{:S(2)}, u32[]{:S(2)}) collective-permute-start(bf16[1,10,4,6400]{3,2,1,0:T(4,128)(2,1)S(1)} %bitcast.76), channel_id=1, source_target_pairs={{0,64},{16,80},{32,96},{48,112},{64,0},{80,16},{96,32},{112,48},{1... | collective-permute-start | bytes 1536008 | tf_op jit(solution)/shard_map/ppermute | solution.py:16
  46.9 12.7 %collective-permute-start.3 = (bf16[1,10,4,6400]{3,2,1,0:T(4,128)(2,1)S(1)}, bf16[1,10,4,6400]{3,2,1,0:T(4,128)(2,1)S(1)}, u32[]{:S(2)}, u32[]{:S(2)}) collective-permute-start(bf16[1,10,4,6400]{3,2,1,0:T(4,128)(2,1)S(1)} %bitcast.77), channel_id=1, source_target_pairs={{0,112},{16,0},{32,16},{48,32},{64,48},{80,64},{96,80},{112,96},{1... | collective-permute-start | bytes 1536008 | tf_op jit(solution)/shard_map/ppermute | solution.py:16
  60.3 4.7 copy-start.3
  480.4 86.0 %copy-start.1 = (f32[32,6]{0,1:T(8,128)S(1)}, f32[32,6]{0,1:T(8,128)}, u32[]{:S(2)}) copy-start(f32[32,6]{0,1:T(8,128)} %param.12) | copy-start | bytes 2308
Sparse Core Ops, SparseCore 0:
  480.5 81.5 reduce-scatter.3
where the time goes:
time: 576 us; the launch traced here: 573 us
  other arithmetic  307 us (53%)
  waiting for transfers between devices  115 us (20%)
  local copies, waits for them, and re-layouts  90.6 us (16%)
  matrix products  24.5 us (4%)
  between operations  16.8 us (3%)
  starting transfers between devices  12.2 us (2%)
  loops' own time  7.39 us (1%)
    another operation x10, other arithmetic  243 us
    unnamed x2, waiting for transfers between devices  81.7 us
    unnamed x12, local copies, waits for them, and re-layouts  61 us
    ppermute x4, waiting for transfers between devices, shifted_2(): lax.ppermute(shard, axis, [(i, (i + by) % size) for i in range(size)])  33 us
    dot_general x10, matrix products, plane_term(): couple = jnp.dot(mat_t, phases, preferred_element_type=jnp.float32)  23.7 us
    reshape x10, local copies, waits for them, and re-layouts, plane_term(): strength = (squared * weight[:, None]).reshape(NB, NB, NM, -1).sum(axis=2)  18.3 us
    mul x10, other arithmetic, plane_term(): strength = (squared * weight[:, None]).reshape(NB, NB, NM, -1).sum(axis=2)  18 us
    dynamic_update_slice x10, other arithmetic, local(): lax.map(one_plane, (jnp.arange(kz_local, dtype=jnp.int32), occupation, sh...  14.9 us
  transfers between devices with their start and end apart: 5, of which 5 were waited for; matrix products, arithmetic and copies ran while one was open for 1% of the time, Pallas kernels for 0%

commit v1 on v0

v1 whole, which is shorter than its diff:
```python
import math

import jax
import jax.numpy as jnp
from jax import lax
from jax.experimental import pallas as pl
from jax.experimental.pallas import tpu as pltpu
from jax.sharding import PartitionSpec as P

KX = 80
KY = 80
KZ = 80
NB = 4
NM = 6
NR = 200
RP = 208
RW = 256
CH = 96
NBIN = 32
QG = 8
PLANES = 10
ROWS = 5
SHARE = ROWS * KY
PAY = 2 * RP + 16
FRONT = 128
BACK = 512
VLANES = FRONT + KX * KY + BACK
WIN = 640
VMEM_LIMIT = 50 * 1024 * 1024


def phase_kernel(ac_ref, as_ref, bc_ref, bs_ref, out_ref):
    bc = bc_ref[...]
    bs = bs_ref[...]
    for row in range(ROWS):
        ac = ac_ref[0, row : row + 1, :]
        an = as_ref[0, row : row + 1, :]
        cosine = ac * bc - an * bs
        sine = an * bc + ac * bs
        out_ref[row * KY : (row + 1) * KY, :RW] = cosine.astype(jnp.bfloat16)
        out_ref[row * KY : (row + 1) * KY, RW:] = sine.astype(jnp.bfloat16)


def make_phases(ac, an, bc, bs):
    plane = pl.BlockSpec((1, ROWS, RW), lambda i: (i, 0, 0))
    whole = pl.BlockSpec((KY, RW), lambda i: (0, 0))
    return pl.pallas_call(
        phase_kernel,
        grid=(PLANES,),
        in_specs=[plane, plane, whole, whole],
        out_specs=pl.BlockSpec((SHARE, 2 * RW), lambda i: (i, 0)),
        out_shape=jax.ShapeDtypeStruct((PLANES * SHARE, 2 * RW), jnp.bfloat16),
        cost_estimate=pl.CostEstimate(flops=10_000_000, bytes_accessed=5_000_000, transcendentals=0),
        name="phases",
    )(ac, an, bc, bs)


def strength_kernel(table_ref, p0, p1, p2, p3, ph_ref, s_ref, off_ref, g_ref, w_ref):
    @pl.when(pl.program_id(0) == 0)
    def _():
        channel = lax.broadcasted_iota(jnp.int32, (CH, NM * 128), 0)
        column = lax.broadcasted_iota(jnp.int32, (CH, NM * 128), 1)
        pair = (channel * 43) >> 8
        target = (channel - NM * pair) * 128 + pair
        total = None
        for slot in range(QG):
            ref = (p0, p1, p2, p3)[slot // 2]
            block = ref[(slot % 2) * PAY : (slot % 2 + 1) * PAY, :]
            place = jnp.where(column - 16 * slot == target, 1.0, 0.0).astype(jnp.bfloat16)
            part = jnp.dot(block, place, preferred_element_type=jnp.float32)
            total = part if total is None else total + part
        real = total[:RP].astype(jnp.bfloat16)
        imag = total[RP : 2 * RP].astype(jnp.bfloat16)
        minus = (-total[RP : 2 * RP]).astype(jnp.bfloat16)
        zeros = jnp.zeros((RW - RP, 2 * NM * 128), jnp.bfloat16)
        g_ref[RP:RW, :] = zeros
        g_ref[RW + RP :, :] = zeros
        for mode in range(NM):
            lanes = slice(mode * 128, (mode + 1) * 128)
            left = slice(mode * 256, mode * 256 + 128)
            right = slice(mode * 256 + 128, mode * 256 + 256)
            g_ref[:RP, left] = real[:, lanes]
            g_ref[:RP, right] = imag[:, lanes]
            g_ref[RW : RW + RP, left] = minus[:, lanes]
            g_ref[RW : RW + RP, right] = real[:, lanes]
        bins = total[2 * RP : 2 * RP + 1, :128]
        off_ref[...] = jnp.broadcast_to(total[2 * RP : 2 * RP + 1, 128:256], (8, 128)).astype(jnp.int32)
        for mode in range(NM):
            weight = jnp.zeros((1, 128), jnp.float32)
            for level in range(NBIN):
                weight = jnp.where(bins == float(level), table_ref[level, mode], weight)
            w_ref[mode : mode + 1, :] = weight

    phases = ph_ref[...]
    acc = None
    for mode in range(NM):
        couple = jnp.dot(phases, g_ref[:, mode * 256 : (mode + 1) * 256], preferred_element_type=jnp.float32)
        re = couple[:, :128]
        im = couple[:, 128:]
        term = (re * re + im * im) * w_ref[mode : mode + 1, :]
        acc = term if acc is None else acc + term
    s_ref[...] = acc


def strengths(table, pays, phases):
    vmem = pl.BlockSpec((2 * PAY, CH), lambda i: (0, 0))
    return pl.pallas_call(
        strength_kernel,
        grid=(PLANES,),
        in_specs=[pl.BlockSpec(memory_space=pltpu.SMEM)] + [vmem] * 4 + [pl.BlockSpec((SHARE, 2 * RW), lambda i: (i, 0))],
        out_specs=[pl.BlockSpec((SHARE, 128), lambda i: (i, 0)), pl.BlockSpec((8, 128), lambda i: (0, 0))],
        out_shape=[jax.ShapeDtypeStruct((PLANES * SHARE, 128), jnp.float32), jax.ShapeDtypeStruct((8, 128), jnp.int32)],
        scratch_shapes=[pltpu.VMEM((2 * RW, 2 * NM * 128), jnp.bfloat16), pltpu.VMEM((8, 128), jnp.float32)],
        compiler_params=pltpu.CompilerParams(vmem_limit_bytes=VMEM_LIMIT),
        cost_estimate=pl.CostEstimate(flops=6_300_000_000, bytes_accessed=8_000_000, transcendentals=0),
        name="strengths",
    )(table, *pays, phases)


def final_kernel(where_ref, off_a, off_b, own, *refs):
    parts = refs[:14]
    sa_ref, sb_ref, out_ref, v_ref, arr_ref, sem = refs[14:]
    step = pl.program_id(0)
    slab = where_ref[0]
    core = where_ref[1]
    share = where_ref[2]

    @pl.when(step == 0)
    def _():
        copies = []

        def bring(src, plane, count):
            dst = v_ref.at[pl.ds(plane, count)]
            copies.append(pltpu.make_async_copy(src, dst.at[:, :, FRONT : FRONT + KX * KY], sem.at[len(copies)]))
            copies.append(pltpu.make_async_copy(src.at[:, :, :BACK], dst.at[:, :, FRONT + KX * KY :], sem.at[len(copies)]))
            copies.append(pltpu.make_async_copy(src.at[:, :, KX * KY - FRONT :], dst.at[:, :, :FRONT], sem.at[len(copies)]))

        bring(own, slab * PLANES, PLANES)
        for index in range(7):
            source = where_ref[3 + index]
            bring(parts[index], source * PLANES + core * (PLANES // 2), PLANES // 2)
            bring(parts[7 + index], source * PLANES + (1 - core) * (PLANES // 2), PLANES // 2)
        for copy in copies:
            copy.start()
        for copy in copies:
            copy.wait()

    lane = lax.broadcasted_iota(jnp.int32, (NB, 512), 1)
    ky = lax.rem(lane, KY)
    for slot in range(2 * QG):
        off = (off_a, off_b)[slot // QG]
        base = (slot % QG) * 16
        qx = off[0, base]
        qy = off[0, base + 1]
        qz = off[0, base + 2]
        plane = lax.rem(slab * PLANES + step + qz, KZ)
        first = lax.rem(share * ROWS + qx, KX) * KY
        start = first + qy + (FRONT - KY)
        aligned = pl.multiple_of((start >> 7) * 128, 128)
        window = v_ref[plane, :, pl.ds(aligned, WIN)].astype(jnp.float32)
        late = pltpu.roll(window, lax.rem(WIN - (start - aligned), WIN), 1)
        early = pltpu.roll(late, WIN - KY, 1)
        arr_ref[NB * slot : NB * (slot + 1), :] = jnp.where(ky + qy < KY, early[:, :512], late[:, :512])
    window = v_ref[slab * PLANES + step, :, pl.ds(pl.multiple_of(((share * SHARE + FRONT) >> 7) * 128, 128), WIN)].astype(jnp.float32)
    rest = lax.rem(share * SHARE, 128)
    occ = pltpu.roll(window, lax.rem(WIN - rest, WIN), 1)
    arr_ref[64:68, :] = occ[:, :512]
    arr_ref[68:80, :] = jnp.zeros((12, 512), jnp.float32)
    arrived = arr_ref[...].astype(jnp.bfloat16)
    row = lax.broadcasted_iota(jnp.int32, (80, 256), 0)
    col = lax.broadcasted_iota(jnp.int32, (80, 256), 1)
    gain = (row < 64) & (row >> 2 == col >> 4) & (row & 3 == col & 3)
    loss = (row >= 64) & (row - 64 == (col >> 2) & 3)
    spread = (jnp.where(gain, 1.0, 0.0) - jnp.where(loss, 1.0, 0.0)).astype(jnp.bfloat16)
    diff = lax.dot_general(arrived, spread, (((0,), (0,)), ((), ())), preferred_element_type=jnp.float32)[:SHARE]
    term = sa_ref[...] * diff[:, :128] + sb_ref[...] * diff[:, 128:]
    band = lax.broadcasted_iota(jnp.int32, (8, 128), 0)
    lane8 = lax.broadcasted_iota(jnp.int32, (8, 128), 1)
    pick = jnp.where((lane8 >> 2) & 3 == band, 1.0, 0.0).astype(jnp.bfloat16)
    result = None
    for _ in range(3):
        piece = term.astype(jnp.bfloat16)
        term = term - piece.astype(jnp.float32)
        got = lax.dot_general(pick, piece, (((1,), (1,)), ((), ())), preferred_element_type=jnp.float32)
        result = got if result is None else result + got
    out_ref[0] = result[:NB] * (1.0 / (2 * QG * NM))


def contract(where, off_a, off_b, own, parts, s_a, s_b):
    smem = pl.BlockSpec(memory_space=pltpu.SMEM)
    anywhere = pl.BlockSpec(memory_space=pl.ANY)
    rows = pl.BlockSpec((SHARE, 128), lambda i: (i, 0))
    return pl.pallas_call(
        final_kernel,
        grid=(PLANES,),
        in_specs=[smem] * 3 + [anywhere] * 15 + [rows] * 2,
        out_specs=pl.BlockSpec((1, NB, SHARE), lambda i: (i, 0, 0)),
        out_shape=jax.ShapeDtypeStruct((PLANES, NB, SHARE), jnp.float32),
        scratch_shapes=[
            pltpu.VMEM((KZ, NB, VLANES), jnp.bfloat16),
            pltpu.VMEM((80, 512), jnp.float32),
            pltpu.SemaphoreType.DMA((45,)),
        ],
        compiler_params=pltpu.CompilerParams(vmem_limit_bytes=VMEM_LIMIT),
        cost_estimate=pl.CostEstimate(flops=2_000_000_000, bytes_accessed=9_000_000, transcendentals=0),
        name="contract",
    )(where, off_a, off_b, own, *parts, s_a, s_b)


def local(occupation, q_offsets, coupling, window_bins, lorentz_table, lattice):
    slab = lax.axis_index("ka")
    share = lax.axis_index("pb")
    core = share % 2

    def core_swap(array):
        return lax.ppermute(array, "pb", [(i, i ^ 1) for i in range(16)])

    half = lax.dynamic_slice_in_dim(occupation, core * (PLANES // 2), PLANES // 2, 0)
    steps = [(0, 1), (0, 3), (1, 0), (1, 1), (1, 3), (0, 2), (1, 2)]
    fetched, sources = [], []
    for dy, dx in steps:
        pairs = [(i, ((i // 4) ^ dy) * 4 + (i % 4 + dx) % 4) for i in range(8)]
        fetched.append(lax.ppermute(half, "ka", pairs))
        sources.append(((slab // 4) ^ dy) * 4 + (slab % 4 + 4 - dx) % 4)
    where = jnp.stack([slab, core, share] + sources).astype(jnp.int32)

    small = jnp.zeros((16, NM), jnp.bfloat16)
    small = small.at[:, 0].set(window_bins[0].astype(jnp.bfloat16)).at[:3, 1].set(q_offsets[0].astype(jnp.bfloat16))
    pay = jnp.concatenate(
        [jnp.pad(coupling[0], ((0, 0), (0, RP - NR), (0, 0))).reshape(2 * RP, CH), jnp.pad(small.reshape(1, CH), ((0, 15), (0, 0)))], axis=0
    )
    pair = jnp.concatenate([pay, lax.ppermute(pay, "pb", [(i, i ^ 2) for i in range(16)])], axis=0)
    group = [pair] + [lax.ppermute(pair, "pb", [(i, (i + 4 * d) % 16) for i in range(16)]) for d in (1, 3, 2)]
    other = [core_swap(array) for array in group]

    vectors = jnp.pad(lattice, ((0, 0), (0, RW - NR)))
    kz = slab * PLANES + jnp.arange(PLANES, dtype=jnp.int32)
    kx = share * ROWS + jnp.arange(ROWS, dtype=jnp.int32)
    first = kz[:, None, None] * vectors[2] + kx[None, :, None] * vectors[0]
    second = jnp.arange(KY, dtype=jnp.int32)[:, None] * vectors[1]
    index = jnp.concatenate([first.reshape(PLANES * ROWS, RW), second], axis=0) % KX
    angle = index.astype(jnp.float32) * (2.0 * math.pi / KX)
    cosine, sine = jnp.cos(angle), jnp.sin(angle)
    cut = PLANES * ROWS
    phases = make_phases(
        cosine[:cut].reshape(PLANES, ROWS, RW), sine[:cut].reshape(PLANES, ROWS, RW), cosine[cut:], sine[cut:]
    )

    s_a, off_a = strengths(lorentz_table, group, phases)
    s_b, off_b = strengths(lorentz_table, other, phases)
    swapped = [core_swap(array) for array in fetched]
    return contract(where, off_a, off_b, occupation, fetched + swapped, s_a, s_b)


def solution(mesh):
    in_specs = (
        P("ka", None, None),
        P("pb", None),
        P("pb", None, None, None),
        P("pb", None),
        P(),
        P(),
    )
    out_specs = P("ka", None, "pb")
    return jax.shard_map(local, mesh=mesh, in_specs=in_specs, out_specs=out_specs, check_vma=False)
```

time: 576 us -> 96.9 us (0.17)
  other arithmetic: 307 us -> 3.42 us
  waiting for transfers between devices: 115 us -> 4.1 us
  local copies, waits for them, and re-layouts: 90.6 us -> 10.5 us
  Pallas kernels: 0 us -> 43.6 us
  matrix products: 24.5 us -> 0 us
  starting transfers between devices: 12.2 us -> 33.6 us
  between operations: 16.8 us -> 0.32 us
  loops' own time: 7.39 us -> 0 us
    another operation x11 -> x2, other arithmetic: 244 us -> 1.94 us
    unnamed x2 -> x0, waiting for transfers between devices: 81.7 us -> none
    unnamed x12 -> x8, local copies, waits for them, and re-layouts: 61 us -> 3.76 us
    pallas_call x0 -> x4, Pallas kernels: none -> 43.6 us  [the longest x2 23.5 us: strengths(): pl.pallas_call(strength_kernel, grid=(PLANES,), in_specs=[pl.BlockSpec(me...]
    ppermute x4 -> x22, waiting for transfers between devices: 33 us -> 4.1 us  [the longest x3 1.95 us: local(): lax.ppermute(pair, 'pb', [(i, (i + 4 * d) % 16) for i in range(16)])]
    dot_general x11 -> x0, matrix products: 24.5 us -> none  [the longest x10 23.7 us: plane_term(): couple = jnp.dot(mat_t, phases, preferred_element_type=jnp.float32)]
    ppermute x4 -> x22, starting transfers between devices: 12.2 us -> 33.6 us  [the longest x11 14 us: core_swap(): return lax.ppermute(array, 'pb', [(i, i ^ 1) for i in range(16)])]
    mul x21 -> x3, other arithmetic: 18.7 us -> 0.15 us  [the longest x2 0.14 us: local(): first = kz[:, None, None] * vectors[2] + kx[None, :, None] * vectors[0]]
  transfers between devices with their start and end apart: 5 -> 22, of which waited for: 5 -> 3; matrix products, arithmetic and copies ran while one was open for 1% -> 11% of each run, Pallas kernels for 0% -> 31%
where the time goes in v1:
time: 96.9 us; the launch traced here: 95.6 us
  Pallas kernels  43.6 us (45%)
  starting transfers between devices  33.6 us (35%)
  local copies, waits for them, and re-layouts  10.5 us (11%)
  waiting for transfers between devices  4.1 us (4%)
  other arithmetic  3.42 us (4%)
    pallas_call x2, Pallas kernels, strengths(): pl.pallas_call(strength_kernel, grid=(PLANES,), in_specs=[pl.BlockSpec(me...  23.5 us
    ppermute x11, starting transfers between devices, core_swap(): return lax.ppermute(array, 'pb', [(i, i ^ 1) for i in range(16)])  14 us
    pallas_call x1, Pallas kernels, contract(): pl.pallas_call(final_kernel, grid=(PLANES,), in_specs=[smem] * 3 + [anywh...  13.6 us
    ppermute x7, starting transfers between devices, local(): fetched.append(lax.ppermute(half, 'ka', pairs))  11.3 us
    pallas_call x1, Pallas kernels, make_phases(): pl.pallas_call(phase_kernel, grid=(PLANES,), in_specs=[plane, plane, whol...  6.52 us
    ppermute x3, starting transfers between devices, local(): lax.ppermute(pair, 'pb', [(i, (i + 4 * d) % 16) for i in range(16)])  5.18 us
    unnamed x8, local copies, waits for them, and re-layouts  3.76 us
    ppermute x1, starting transfers between devices, local(): lax.ppermute(pay, 'pb', [(i, i ^ 2) for i in range(16)])  3.11 us
  transfers between devices with their start and end apart: 22, of which 3 were waited for; matrix products, arithmetic and copies ran while one was open for 11% of the time, Pallas kernels for 31%

profile of v1, /device:TPU:1, one launch (start us, length us, event | category | flops | bytes accessed | tf_op | source)
XLA Modules:
  0.0 95.6 jit_solution(11165359610767213616)
XLA Ops:
  0.0 1.1 %constant_dynamic-slice_fusion = bf16[5,4,6400]{2,1,0:T(4,128)(2,1)S(1)} fusion(bf16[10,4,6400]{2,1,0:T(4,128)(2,1)} %own.1, s32[]{:T(128)S(6)} %select_n.72), kind=kLoop, calls=%fused_computation.21 | loop fusion | bytes 512004 | tf_op jit(solution)/shard_map/dynamic_slice | solution.py:218
  1.1 2.1 %collective-permute-start.8 = (bf16[5,4,6400]{2,1,0:T(4,128)(2,1)S(1)}, bf16[5,4,6400]{2,1,0:T(4,128)(2,1)S(1)}, u32[]{:S(2)}, u32[]{:S(2)}) collective-permute-start(bf16[5,4,6400]{2,1,0:T(4,128)(2,1)S(1)} %constant_dynamic-slice_fusion), channel_id=1, source_target_pairs={{0,16},{16,32},{32,48},{48,0},{64,80},{80,96},{96,112},{112,64},{1... | collective-permute-start | bytes 768008 | tf_op jit(solution)/shard_map/ppermute | solution.py:223
  3.2 1.3 %collective-permute-start.9 = (bf16[5,4,6400]{2,1,0:T(4,128)(2,1)S(1)}, bf16[5,4,6400]{2,1,0:T(4,128)(2,1)S(1)}, u32[]{:S(2)}, u32[]{:S(2)}) collective-permute-start(bf16[5,4,6400]{2,1,0:T(4,128)(2,1)S(1)} %constant_dynamic-slice_fusion), channel_id=1, source_target_pairs={{0,48},{16,0},{32,16},{48,32},{64,112},{80,64},{96,80},{112,96},{1... | collective-permute-start | bytes 768008 | tf_op jit(solution)/shard_map/ppermute | solution.py:223
  4.5 0.6 compare_reduce_fusion
  5.2 0.7 convert_bitcast_fusion
  5.8 0.6 fusion.5
  6.4 1.3 %fusion.4 = bf16[16,1]{0,1:T(2,128)(2,1)S(1)} fusion(pred[]{:T(512)} %compare_reduce_fusion, s32[1,16]{1,0:T(1,128)} %param.13), kind=kLoop, calls=%fused_computation.17 | loop fusion | flops 32 | bytes 97 | tf_op jit(solution)/shard_map/reshape.151
  7.7 1.4 %scatter.9 = bf16[16,6]{0,1:T(8,128)(2,1)S(1)} dynamic-update-slice(bf16[16,6]{0,1:T(8,128)(2,1)S(1)} %scatter.6, bf16[3,1]{0,1:T(2,128)(2,1)S(1)} %convert_bitcast_fusion, s32[]{:T(128)} %bitcast.14, s32[]{:T(128)} %bitcast.15) | dynamic-update-slice | bytes 16 | tf_op jit(solution)/shard_map/scatter | solution.py:228
  9.1 0.1 copy.12
  9.2 0.1 reshape.170
  9.3 1.0 %copy.15 = bf16[2,200,96]{2,1,0:T(8,128)(2,1)S(1)} copy(bf16[2,200,96]{1,2,0:T(8,128)(2,1)} %bitcast.23) | data formatting | bytes 153600
  10.4 3.1 %collective-permute-start = (bf16[432,96]{1,0:T(8,128)(2,1)S(1)}, bf16[432,96]{1,0:T(8,128)(2,1)S(1)}, u32[]{:S(2)}, u32[]{:S(2)}) collective-permute-start(bf16[432,96]{1,0:T(8,128)(2,1)S(1)} %pad_maximum_fusion.1), channel_id=1, source_target_pairs={{0,2},{1,3},{2,0},{3,1},{4,6},{5,7},{6,4},{7,5},{8,10},{9,11},{10,... | collective-permute-start | bytes 248840 | tf_op jit(solution)/shard_map/ppermute | solution.py:232
  13.5 0.8 pad_slice_fusion.2
  14.3 0.1 broadcast_multiply_fusion
  14.4 1.3 %collective-permute-done = bf16[432,96]{1,0:T(8,128)(2,1)S(1)} collective-permute-done((bf16[432,96]{1,0:T(8,128)(2,1)S(1)}, bf16[432,96]{1,0:T(8,128)(2,1)S(1)}, u32[]{:S(2)}, u32[]{:S(2)}) %collective-permute-start) | collective-permute-done | bytes 82976 | tf_op jit(solution)/shard_map/ppermute | solution.py:232
  15.7 1.8 %collective-permute-start.1 = (bf16[864,96]{1,0:T(8,128)(2,1)S(1)}, bf16[864,96]{1,0:T(8,128)(2,1)S(1)}, u32[]{:S(2)}, u32[]{:S(2)}) collective-permute-start(bf16[864,96]{1,0:T(8,128)(2,1)S(1)} %pad_maximum_fusion.p0), channel_id=1, source_target_pairs={{0,4},{1,5},{2,6},{3,7},{4,8},{5,9},{6,10},{7,11},{8,12},{9,13},{1... | collective-permute-start | bytes 497672 | tf_op jit(solution)/shard_map/ppermute | solution.py:233
  17.5 0.1 broadcast_multiply_fusion.1
  17.6 2.2 %collective-permute-start.2 = (bf16[864,96]{1,0:T(8,128)(2,1)S(1)}, bf16[864,96]{1,0:T(8,128)(2,1)S(1)}, u32[]{:S(2)}, u32[]{:S(2)}) collective-permute-start(bf16[864,96]{1,0:T(8,128)(2,1)S(1)} %pad_maximum_fusion.p0), channel_id=1, source_target_pairs={{0,12},{1,13},{2,14},{3,15},{4,0},{5,1},{6,2},{7,3},{8,4},{9,5},{1... | collective-permute-start | bytes 497672 | tf_op jit(solution)/shard_map/ppermute | solution.py:233
  19.8 1.2 %collective-permute-start.3 = (bf16[864,96]{1,0:T(8,128)(2,1)S(1)}, bf16[864,96]{1,0:T(8,128)(2,1)S(1)}, u32[]{:S(2)}, u32[]{:S(2)}) collective-permute-start(bf16[864,96]{1,0:T(8,128)(2,1)S(1)} %pad_maximum_fusion.p0), channel_id=1, source_target_pairs={{0,8},{1,9},{2,10},{3,11},{4,12},{5,13},{6,14},{7,15},{8,0},{9,1},... | collective-permute-start | bytes 497672 | tf_op jit(solution)/shard_map/ppermute | solution.py:233
  21.0 1.9 %collective-permute-done.1.p1 = bf16[864,96]{1,0:T(8,128)(2,1)S(1)} collective-permute-done((bf16[864,96]{1,0:T(8,128)(2,1)S(1)}, bf16[864,96]{1,0:T(8,128)(2,1)S(1)}, u32[]{:S(2)}, u32[]{:S(2)}) %collective-permute-start.1) | collective-permute-done | bytes 165920 | tf_op jit(solution)/shard_map/ppermute | solution.py:233
  22.9 5.2 %collective-permute-start.4 = (bf16[864,96]{1,0:T(8,128)(2,1)S(1)}, bf16[864,96]{1,0:T(8,128)(2,1)S(1)}, u32[]{:S(2)}, u32[]{:S(2)}) collective-permute-start(bf16[864,96]{1,0:T(8,128)(2,1)S(1)} %pad_maximum_fusion.p0), channel_id=1, source_target_pairs={{0,1},{1,0},{2,3},{3,2},{4,5},{5,4},{6,7},{7,6},{8,9},{9,8},{10,11... | collective-permute-start | bytes 497672 | tf_op jit(solution)/shard_map/ppermute | solution.py:216
  28.1 0.0 collective-permute-done.2.p2
  28.1 1.4 %collective-permute-start.10 = (bf16[5,4,6400]{2,1,0:T(4,128)(2,1)S(1)}, bf16[5,4,6400]{2,1,0:T(4,128)(2,1)S(1)}, u32[]{:S(2)}, u32[]{:S(2)}) collective-permute-start(bf16[5,4,6400]{2,1,0:T(4,128)(2,1)S(1)} %constant_dynamic-slice_fusion), channel_id=1, source_target_pairs={{0,64},{16,80},{32,96},{48,112},{64,0},{80,16},{96,32},{112,48},{1... | collective-permute-start | bytes 768008 | tf_op jit(solution)/shard_map/ppermute | solution.py:223
  29.5 0.0 collective-permute-done.3.p3
  29.5 0.0 collective-permute-start.11
  29.5 0.0 collective-permute-done.4.p0
  29.5 3.6 %collective-permute-start.12 = (bf16[5,4,6400]{2,1,0:T(4,128)(2,1)S(1)}, bf16[5,4,6400]{2,1,0:T(4,128)(2,1)S(1)}, u32[]{:S(2)}, u32[]{:S(2)}) collective-permute-start(bf16[5,4,6400]{2,1,0:T(4,128)(2,1)S(1)} %constant_dynamic-slice_fusion), channel_id=1, source_target_pairs={{0,112},{16,64},{32,80},{48,96},{64,48},{80,0},{96,16},{112,32},{1... | collective-permute-start | bytes 768008 | tf_op jit(solution)/shard_map/ppermute | solution.py:223
  33.1 0.0 collective-permute-done.8.refs_0_
  33.1 0.3 collective-permute-start.13
  33.4 2.5 %collective-permute-start.14 = (bf16[5,4,6400]{2,1,0:T(4,128)(2,1)S(1)}, bf16[5,4,6400]{2,1,0:T(4,128)(2,1)S(1)}, u32[]{:S(2)}, u32[]{:S(2)}) collective-permute-start(bf16[5,4,6400]{2,1,0:T(4,128)(2,1)S(1)} %constant_dynamic-slice_fusion), channel_id=1, source_target_pairs={{0,96},{16,112},{32,64},{48,80},{64,32},{80,48},{96,0},{112,16},{1... | collective-permute-start | bytes 768008 | tf_op jit(solution)/shard_map/ppermute | solution.py:223
  36.0 0.6 fusion.2
  36.6 0.6 slice.70.bc_ref
  37.2 0.6 slice.71.bs_ref
  37.9 0.1 copy.13.table_ref
  38.0 0.6 reshape.171.ac_ref
  38.6 0.6 reshape.172.as_ref
  39.2 0.1 stack.43.where_ref
  39.3 6.5 %phases.1.ph_ref = bf16[4000,512]{1,0:T(8,128)(2,1)} custom-call(f32[10,5,256]{2,1,0:T(8,128)} %reshape.171.ac_ref, f32[10,5,256]{2,1,0:T(8,128)} %reshape.172.as_ref, f32[80,256]{1,0:T(8,128)} %slice.70.bc_ref, f32[80,256]{1,0:T(8,128)} %slice.71.bs_ref), custom_call_target="tpu_custom_call" | custom-call | flops 10000000 | bytes 5000000 | tf_op jit(solution)/shard_map/phases/pallas_call | solution.py:47
  45.9 0.8 collective-permute-done.10.refs_2_
  46.7 6.6 %collective-permute-start.5 = (bf16[864,96]{1,0:T(8,128)(2,1)S(1)}, bf16[864,96]{1,0:T(8,128)(2,1)S(1)}, u32[]{:S(2)}, u32[]{:S(2)}) collective-permute-start(bf16[864,96]{1,0:T(8,128)(2,1)S(1)} %collective-permute-done.1.p1), channel_id=1, source_target_pairs={{0,1},{1,0},{2,3},{3,2},{4,5},{5,4},{6,7},{7,6},{8,9},{9,8},{10,11... | collective-permute-start | bytes 497672 | tf_op jit(solution)/shard_map/ppermute | solution.py:216
  53.3 0.0 collective-permute-done.11.refs_3_
  53.3 0.0 collective-permute-start.6
  53.3 0.0 collective-permute-done.12.refs_4_
  53.3 0.5 collective-permute-start.7
  53.8 0.0 collective-permute-done.13.refs_5_
  53.8 0.1 collective-permute-start.15
  53.9 0.0 collective-permute-done.14.refs_6_
  53.9 0.4 collective-permute-start.16
  54.3 11.8 %strengths.2 = (f32[4000,128]{1,0:T(8,128)S(1)}, s32[8,128]{1,0:T(8,128)S(1)}) custom-call(f32[32,6]{1,0:T(8,128)S(1)} %copy.13.table_ref, bf16[864,96]{1,0:T(8,128)(2,1)S(1)} %pad_maximum_fusion.p0, bf16[864,96]{1,0:T(8,128)(2,1)S(1)} %collective-permute-done.1.p1, bf16[864,96]{1,0:T(8,128)(2,1)S(1)} %collective-permute-done.2.p2, ...), custom_call_target="tpu_custom_call" | custom-call | flops 6300000256 | bytes 8000000 | tf_op jit(solution)/shard_map/strengths/pallas_call | solution.py:107
  66.1 1.3 %copy-done = f32[4000,128]{1,0:T(8,128)} copy-done((f32[4000,128]{1,0:T(8,128)}, f32[4000,128]{1,0:T(8,128)S(1)}, u32[]{:S(2)}) %copy-start) | copy-done | bytes 2048024
  67.4 0.0 collective-permute-done.5.p1
  67.4 0.1 collective-permute-start.17
  67.5 0.4 collective-permute-start.18
  68.0 0.1 collective-permute-start.19
  68.0 0.0 collective-permute-done.15.refs_7_
  68.0 0.4 collective-permute-start.20
  68.5 0.3 collective-permute-start.21
  68.7 11.8 %strengths.3 = (f32[4000,128]{1,0:T(8,128)S(1)}, s32[8,128]{1,0:T(8,128)S(1)}) custom-call(f32[32,6]{1,0:T(8,128)S(1)} %copy.13.table_ref, bf16[864,96]{1,0:T(8,128)(2,1)S(1)} %collective-permute-done.4.p0, bf16[864,96]{1,0:T(8,128)(2,1)S(1)} %collective-permute-done.5.p1, bf16[864,96]{1,0:T(8,128)(2,1)S(1)} %collective-permute-done.6.p2, ...), custom_call_target="tpu_custom_call" | custom-call | flops 6300000256 | bytes 8000000 | tf_op jit(solution)/shard_map/strengths/pallas_call | solution.py:107
  80.5 1.3 %copy-done.1 = f32[4000,128]{1,0:T(8,128)} copy-done((f32[4000,128]{1,0:T(8,128)}, f32[4000,128]{1,0:T(8,128)S(1)}, u32[]{:S(2)}) %copy-start.1) | copy-done | bytes 2048024
  81.8 0.0 collective-permute-done.17.refs_9_
  81.8 0.0 collective-permute-done.18.refs_10_
  81.8 0.0 collective-permute-done.19.refs_11_
  81.9 0.0 collective-permute-done.21.refs_13_
  81.9 13.6 %contract.1 = f32[10,4,400]{2,1,0:T(4,128)} custom-call(s32[10]{0:T(128)S(1)} %stack.43.where_ref, s32[8,128]{1,0:T(8,128)S(1)} %get-tuple-element.33.off_a, s32[8,128]{1,0:T(8,128)S(1)} %get-tuple-element.34.off_b, bf16[10,4,6400]{2,1,0:T(4,128)(2,1)} %own.1, bf16[5,4,6400]{2,1,0:T(4,128)(2,1)S(1)} %collective-permute-done.8.refs_0_, ...), custom_call_target="tpu_custom_call" | custom-call | flops 2000000000 | bytes 9000000 | tf_op jit(solution)/shard_map/contract/pallas_call | solution.py:193
  (22 shorter events, 0.2 us)
Async XLA Ops:
  0.0 37.9 %copy-start.2 = (f32[32,6]{0,1:T(8,128)S(1)}, f32[32,6]{0,1:T(8,128)}, u32[]{:S(2)}) copy-start(f32[32,6]{0,1:T(8,128)} %param.14) | copy-start | bytes 2308
  1.1 32.0 %collective-permute-start.8 = (bf16[5,4,6400]{2,1,0:T(4,128)(2,1)S(1)}, bf16[5,4,6400]{2,1,0:T(4,128)(2,1)S(1)}, u32[]{:S(2)}, u32[]{:S(2)}) collective-permute-start(bf16[5,4,6400]{2,1,0:T(4,128)(2,1)S(1)} %constant_dynamic-slice_fusion), channel_id=1, source_target_pairs={{0,16},{16,32},{32,48},{48,0},{64,80},{80,96},{96,112},{112,64},{1... | collective-permute-start | bytes 768008 | tf_op jit(solution)/shard_map/ppermute | solution.py:223
  3.2 30.3 %collective-permute-start.9 = (bf16[5,4,6400]{2,1,0:T(4,128)(2,1)S(1)}, bf16[5,4,6400]{2,1,0:T(4,128)(2,1)S(1)}, u32[]{:S(2)}, u32[]{:S(2)}) collective-permute-start(bf16[5,4,6400]{2,1,0:T(4,128)(2,1)S(1)} %constant_dynamic-slice_fusion), channel_id=1, source_target_pairs={{0,48},{16,0},{32,16},{48,32},{64,112},{80,64},{96,80},{112,96},{1... | collective-permute-start | bytes 768008 | tf_op jit(solution)/shard_map/ppermute | solution.py:223
  10.4 5.2 %collective-permute-start = (bf16[432,96]{1,0:T(8,128)(2,1)S(1)}, bf16[432,96]{1,0:T(8,128)(2,1)S(1)}, u32[]{:S(2)}, u32[]{:S(2)}) collective-permute-start(bf16[432,96]{1,0:T(8,128)(2,1)S(1)} %pad_maximum_fusion.1), channel_id=1, source_target_pairs={{0,2},{1,3},{2,0},{3,1},{4,6},{5,7},{6,4},{7,5},{8,10},{9,11},{10,... | collective-permute-start | bytes 248840 | tf_op jit(solution)/shard_map/ppermute | solution.py:232
  15.7 7.2 %collective-permute-start.1 = (bf16[864,96]{1,0:T(8,128)(2,1)S(1)}, bf16[864,96]{1,0:T(8,128)(2,1)S(1)}, u32[]{:S(2)}, u32[]{:S(2)}) collective-permute-start(bf16[864,96]{1,0:T(8,128)(2,1)S(1)} %pad_maximum_fusion.p0), channel_id=1, source_target_pairs={{0,4},{1,5},{2,6},{3,7},{4,8},{5,9},{6,10},{7,11},{8,12},{9,13},{1... | collective-permute-start | bytes 497672 | tf_op jit(solution)/shard_map/ppermute | solution.py:233
  17.6 10.6 %collective-permute-start.2 = (bf16[864,96]{1,0:T(8,128)(2,1)S(1)}, bf16[864,96]{1,0:T(8,128)(2,1)S(1)}, u32[]{:S(2)}, u32[]{:S(2)}) collective-permute-start(bf16[864,96]{1,0:T(8,128)(2,1)S(1)} %pad_maximum_fusion.p0), channel_id=1, source_target_pairs={{0,12},{1,13},{2,14},{3,15},{4,0},{5,1},{6,2},{7,3},{8,4},{9,5},{1... | collective-permute-start | bytes 497672 | tf_op jit(solution)/shard_map/ppermute | solution.py:233
  19.8 9.8 %collective-permute-start.3 = (bf16[864,96]{1,0:T(8,128)(2,1)S(1)}, bf16[864,96]{1,0:T(8,128)(2,1)S(1)}, u32[]{:S(2)}, u32[]{:S(2)}) collective-permute-start(bf16[864,96]{1,0:T(8,128)(2,1)S(1)} %pad_maximum_fusion.p0), channel_id=1, source_target_pairs={{0,8},{1,9},{2,10},{3,11},{4,12},{5,13},{6,14},{7,15},{8,0},{9,1},... | collective-permute-start | bytes 497672 | tf_op jit(solution)/shard_map/ppermute | solution.py:233
  22.9 6.6 %collective-permute-start.4 = (bf16[864,96]{1,0:T(8,128)(2,1)S(1)}, bf16[864,96]{1,0:T(8,128)(2,1)S(1)}, u32[]{:S(2)}, u32[]{:S(2)}) collective-permute-start(bf16[864,96]{1,0:T(8,128)(2,1)S(1)} %pad_maximum_fusion.p0), channel_id=1, source_target_pairs={{0,1},{1,0},{2,3},{3,2},{4,5},{5,4},{6,7},{7,6},{8,9},{9,8},{10,11... | collective-permute-start | bytes 497672 | tf_op jit(solution)/shard_map/ppermute | solution.py:216
  28.1 18.6 %collective-permute-start.10 = (bf16[5,4,6400]{2,1,0:T(4,128)(2,1)S(1)}, bf16[5,4,6400]{2,1,0:T(4,128)(2,1)S(1)}, u32[]{:S(2)}, u32[]{:S(2)}) collective-permute-start(bf16[5,4,6400]{2,1,0:T(4,128)(2,1)S(1)} %constant_dynamic-slice_fusion), channel_id=1, source_target_pairs={{0,64},{16,80},{32,96},{48,112},{64,0},{80,16},{96,32},{112,48},{1... | collective-permute-start | bytes 768008 | tf_op jit(solution)/shard_map/ppermute | solution.py:223
  29.5 23.8 %collective-permute-start.11 = (bf16[5,4,6400]{2,1,0:T(4,128)(2,1)S(1)}, bf16[5,4,6400]{2,1,0:T(4,128)(2,1)S(1)}, u32[]{:S(2)}, u32[]{:S(2)}) collective-permute-start(bf16[5,4,6400]{2,1,0:T(4,128)(2,1)S(1)} %constant_dynamic-slice_fusion), channel_id=1, source_target_pairs={{0,80},{16,96},{32,112},{48,64},{64,16},{80,32},{96,48},{112,0},{1... | collective-permute-start | bytes 768008 | tf_op jit(solution)/shard_map/ppermute | solution.py:223
  29.5 23.8 %collective-permute-start.12 = (bf16[5,4,6400]{2,1,0:T(4,128)(2,1)S(1)}, bf16[5,4,6400]{2,1,0:T(4,128)(2,1)S(1)}, u32[]{:S(2)}, u32[]{:S(2)}) collective-permute-start(bf16[5,4,6400]{2,1,0:T(4,128)(2,1)S(1)} %constant_dynamic-slice_fusion), channel_id=1, source_target_pairs={{0,112},{16,64},{32,80},{48,96},{64,48},{80,0},{96,16},{112,32},{1... | collective-permute-start | bytes 768008 | tf_op jit(solution)/shard_map/ppermute | solution.py:223
  33.1 20.7 %collective-permute-start.13 = (bf16[5,4,6400]{2,1,0:T(4,128)(2,1)S(1)}, bf16[5,4,6400]{2,1,0:T(4,128)(2,1)S(1)}, u32[]{:S(2)}, u32[]{:S(2)}) collective-permute-start(bf16[5,4,6400]{2,1,0:T(4,128)(2,1)S(1)} %constant_dynamic-slice_fusion), channel_id=1, source_target_pairs={{0,32},{16,48},{32,0},{48,16},{64,96},{80,112},{96,64},{112,80},{1... | collective-permute-start | bytes 768008 | tf_op jit(solution)/shard_map/ppermute | solution.py:223
  33.4 20.4 %collective-permute-start.14 = (bf16[5,4,6400]{2,1,0:T(4,128)(2,1)S(1)}, bf16[5,4,6400]{2,1,0:T(4,128)(2,1)S(1)}, u32[]{:S(2)}, u32[]{:S(2)}) collective-permute-start(bf16[5,4,6400]{2,1,0:T(4,128)(2,1)S(1)} %constant_dynamic-slice_fusion), channel_id=1, source_target_pairs={{0,96},{16,112},{32,64},{48,80},{64,32},{80,48},{96,0},{112,16},{1... | collective-permute-start | bytes 768008 | tf_op jit(solution)/shard_map/ppermute | solution.py:223
  46.7 20.7 %collective-permute-start.5 = (bf16[864,96]{1,0:T(8,128)(2,1)S(1)}, bf16[864,96]{1,0:T(8,128)(2,1)S(1)}, u32[]{:S(2)}, u32[]{:S(2)}) collective-permute-start(bf16[864,96]{1,0:T(8,128)(2,1)S(1)} %collective-permute-done.1.p1), channel_id=1, source_target_pairs={{0,1},{1,0},{2,3},{3,2},{4,5},{5,4},{6,7},{7,6},{8,9},{9,8},{10,11... | collective-permute-start | bytes 497672 | tf_op jit(solution)/shard_map/ppermute | solution.py:216
  53.3 14.2 %collective-permute-start.6 = (bf16[864,96]{1,0:T(8,128)(2,1)S(1)}, bf16[864,96]{1,0:T(8,128)(2,1)S(1)}, u32[]{:S(2)}, u32[]{:S(2)}) collective-permute-start(bf16[864,96]{1,0:T(8,128)(2,1)S(1)} %collective-permute-done.2.p2), channel_id=1, source_target_pairs={{0,1},{1,0},{2,3},{3,2},{4,5},{5,4},{6,7},{7,6},{8,9},{9,8},{10,11... | collective-permute-start | bytes 497672 | tf_op jit(solution)/shard_map/ppermute | solution.py:216
  53.3 14.7 %collective-permute-start.7 = (bf16[864,96]{1,0:T(8,128)(2,1)S(1)}, bf16[864,96]{1,0:T(8,128)(2,1)S(1)}, u32[]{:S(2)}, u32[]{:S(2)}) collective-permute-start(bf16[864,96]{1,0:T(8,128)(2,1)S(1)} %collective-permute-done.3.p3), channel_id=1, source_target_pairs={{0,1},{1,0},{2,3},{3,2},{4,5},{5,4},{6,7},{7,6},{8,9},{9,8},{10,11... | collective-permute-start | bytes 497672 | tf_op jit(solution)/shard_map/ppermute | solution.py:216
  53.8 14.2 %collective-permute-start.15 = (bf16[5,4,6400]{2,1,0:T(4,128)(2,1)S(1)}, bf16[5,4,6400]{2,1,0:T(4,128)(2,1)S(1)}, u32[]{:S(2)}, u32[]{:S(2)}) collective-permute-start(bf16[5,4,6400]{2,1,0:T(4,128)(2,1)S(1)} %collective-permute-done.8.refs_0_), channel_id=1, source_target_pairs={{0,1},{1,0},{2,3},{3,2},{4,5},{5,4},{6,7},{7,6},{8,9},{9,8},{10,11... | collective-permute-start | bytes 768008 | tf_op jit(solution)/shard_map/ppermute | solution.py:216
  53.9 14.6 %collective-permute-start.16 = (bf16[5,4,6400]{2,1,0:T(4,128)(2,1)S(1)}, bf16[5,4,6400]{2,1,0:T(4,128)(2,1)S(1)}, u32[]{:S(2)}, u32[]{:S(2)}) collective-permute-start(bf16[5,4,6400]{2,1,0:T(4,128)(2,1)S(1)} %collective-permute-done.9.refs_1_), channel_id=1, source_target_pairs={{0,1},{1,0},{2,3},{3,2},{4,5},{5,4},{6,7},{7,6},{8,9},{9,8},{10,11... | collective-permute-start | bytes 768008 | tf_op jit(solution)/shard_map/ppermute | solution.py:216
  66.1 1.3 %copy-start = (f32[4000,128]{1,0:T(8,128)}, f32[4000,128]{1,0:T(8,128)S(1)}, u32[]{:S(2)}) copy-start(f32[4000,128]{1,0:T(8,128)S(1)} %get-tuple-element.35.refs_14_) | copy-start | bytes 6144004
  67.4 14.4 %collective-permute-start.17 = (bf16[5,4,6400]{2,1,0:T(4,128)(2,1)S(1)}, bf16[5,4,6400]{2,1,0:T(4,128)(2,1)S(1)}, u32[]{:S(2)}, u32[]{:S(2)}) collective-permute-start(bf16[5,4,6400]{2,1,0:T(4,128)(2,1)S(1)} %collective-permute-done.10.refs_2_), channel_id=1, source_target_pairs={{0,1},{1,0},{2,3},{3,2},{4,5},{5,4},{6,7},{7,6},{8,9},{9,8},{10,11... | collective-permute-start | bytes 768008 | tf_op jit(solution)/shard_map/ppermute | solution.py:216
  67.5 14.3 %collective-permute-start.18 = (bf16[5,4,6400]{2,1,0:T(4,128)(2,1)S(1)}, bf16[5,4,6400]{2,1,0:T(4,128)(2,1)S(1)}, u32[]{:S(2)}, u32[]{:S(2)}) collective-permute-start(bf16[5,4,6400]{2,1,0:T(4,128)(2,1)S(1)} %collective-permute-done.11.refs_3_), channel_id=1, source_target_pairs={{0,1},{1,0},{2,3},{3,2},{4,5},{5,4},{6,7},{7,6},{8,9},{9,8},{10,11... | collective-permute-start | bytes 768008 | tf_op jit(solution)/shard_map/ppermute | solution.py:216
  68.0 13.9 %collective-permute-start.19 = (bf16[5,4,6400]{2,1,0:T(4,128)(2,1)S(1)}, bf16[5,4,6400]{2,1,0:T(4,128)(2,1)S(1)}, u32[]{:S(2)}, u32[]{:S(2)}) collective-permute-start(bf16[5,4,6400]{2,1,0:T(4,128)(2,1)S(1)} %collective-permute-done.12.refs_4_), channel_id=1, source_target_pairs={{0,1},{1,0},{2,3},{3,2},{4,5},{5,4},{6,7},{7,6},{8,9},{9,8},{10,11... | collective-permute-start | bytes 768008 | tf_op jit(solution)/shard_map/ppermute | solution.py:216
  68.0 13.8 %collective-permute-start.20 = (bf16[5,4,6400]{2,1,0:T(4,128)(2,1)S(1)}, bf16[5,4,6400]{2,1,0:T(4,128)(2,1)S(1)}, u32[]{:S(2)}, u32[]{:S(2)}) collective-permute-start(bf16[5,4,6400]{2,1,0:T(4,128)(2,1)S(1)} %collective-permute-done.13.refs_5_), channel_id=1, source_target_pairs={{0,1},{1,0},{2,3},{3,2},{4,5},{5,4},{6,7},{7,6},{8,9},{9,8},{10,11... | collective-permute-start | bytes 768008 | tf_op jit(solution)/shard_map/ppermute | solution.py:216
  68.5 13.4 %collective-permute-start.21 = (bf16[5,4,6400]{2,1,0:T(4,128)(2,1)S(1)}, bf16[5,4,6400]{2,1,0:T(4,128)(2,1)S(1)}, u32[]{:S(2)}, u32[]{:S(2)}) collective-permute-start(bf16[5,4,6400]{2,1,0:T(4,128)(2,1)S(1)} %collective-permute-done.14.refs_6_), channel_id=1, source_target_pairs={{0,1},{1,0},{2,3},{3,2},{4,5},{5,4},{6,7},{7,6},{8,9},{9,8},{10,11... | collective-permute-start | bytes 768008 | tf_op jit(solution)/shard_map/ppermute | solution.py:216
  80.5 1.3 %copy-start.1 = (f32[4000,128]{1,0:T(8,128)}, f32[4000,128]{1,0:T(8,128)S(1)}, u32[]{:S(2)}) copy-start(f32[4000,128]{1,0:T(8,128)S(1)} %get-tuple-element.36.refs_15_) | copy-start | bytes 6144004

commit v2 on v0

v2 whole, which is shorter than its diff:
```python
import math

import jax
import jax.numpy as jnp
from jax import lax
from jax.experimental import pallas as pl
from jax.experimental.pallas import tpu as pltpu
from jax.sharding import PartitionSpec as P

KX = 80
KY = 80
KZ = 80
NB = 4
NM = 6
NR = 200
RW = 256
CH = 96
NBIN = 32
QG = 8
PLANES = 10
HP = PLANES // 2
PARTS = 4
WHICH = (0, 1, 3, 5)
ROWS = 5
HALF = KY // 2
SHARE = ROWS * KY
POINTS = PLANES * ROWS * HALF
PAY = 2 * CH + 16
SLOTS = 384
FRONT = 128
BACK = 512
VLANES = FRONT + KX * KY + BACK
WIN = 640
STEP = 400
UNROLL = 5
VMEM_LIMIT = 28 * 1024 * 1024
F32 = jnp.float32
BF16 = jnp.bfloat16


def smem():
    return pl.BlockSpec(memory_space=pltpu.SMEM)


def vmem():
    return pl.BlockSpec(memory_space=pltpu.VMEM)


def anywhere():
    return pl.BlockSpec(memory_space=pl.ANY)


def iota(shape, axis):
    return lax.broadcasted_iota(jnp.int32, shape, axis)


def pack_kernel(off_ref, bins_ref, coupling_ref, pay_ref):
    row = iota((CH, CH), 0)
    moved = jnp.where(iota((CH, CH), 1) == (row & 15) * NM + (row >> 4), 1.0, 0.0).astype(BF16)
    pay_ref[:, NR:] = jnp.zeros((PAY, RW - NR), BF16)
    for part in range(2):
        block = jnp.dot(moved, coupling_ref[part], preferred_element_type=F32)
        pay_ref[part * CH : (part + 1) * CH, :NR] = block.astype(BF16)
    lane = iota((16, 128), 1) & 15
    line = iota((16, 128), 0)
    small = jnp.zeros((16, 128), F32)
    for pair in range(NB * NB):
        small = jnp.where((line == 0) & (lane == pair), bins_ref[0, pair].astype(F32), small)
    for axis in range(3):
        small = jnp.where((line == 1) & (lane == axis), off_ref[0, axis].astype(F32), small)
    pay_ref[2 * CH :, :128] = small.astype(BF16)
    pay_ref[2 * CH :, 128:] = jnp.zeros((16, RW - 128), BF16)


def pack(q_offsets, window_bins, coupling):
    return pl.pallas_call(
        pack_kernel,
        in_specs=[smem(), smem(), vmem()],
        out_specs=vmem(),
        out_shape=jax.ShapeDtypeStruct((PAY, RW), BF16),
        name="pack",
    )(q_offsets, window_bins, coupling)


def sine_of(turns):
    x = turns * (math.pi / 40)
    y = x * x
    s = -2.3889859e-08
    for c in (2.7525562e-06, -1.9840874e-04, 8.3333310e-03, -1.6666667e-01, 1.0):
        s = s * y + c
    return x * s


def cos_sin(steps):
    t = steps - 80.0 * jnp.round(steps * (1.0 / 80.0))
    a = jnp.abs(t)
    cosine = sine_of(20.0 - a)
    folded = jnp.where(a > 20.0, 40.0 - a, a)
    sine = sine_of(jnp.where(t < 0.0, -folded, folded))
    return cosine, sine


def order(lattice):
    lane = iota((8, 256), 1)
    even = jnp.where((jnp.broadcast_to(lattice[1:2, :], (8, 256)) & 1) == 0, 1, 0)
    real = lane < NR
    is_even = jnp.where(real, even, 0).astype(BF16)
    before = jnp.where(iota((256, 256), 0) < iota((256, 256), 1), 1.0, 0.0).astype(BF16)
    rank = jnp.dot(is_even, before, preferred_element_type=F32).astype(jnp.int32)
    count = jnp.sum(is_even[:1].astype(F32), axis=1, keepdims=True).astype(jnp.int32)
    base = jnp.where(count > 128, 256, 128)
    slot = jnp.where(even == 1, rank, lane - rank + base)
    slot = jnp.where(real, slot, -1)[:1]
    count = count[0, 0]
    wide = count > 128
    third = (wide & (count < NR)) | (count < NR - 128)
    place = jnp.where(iota((SLOTS, 256), 0) == slot, 1.0, 0.0).astype(BF16)
    return place, third, wide


def phase_kernel(where_ref, lattice_ref, out_ref, out3_ref):
    lattice = lattice_ref[...]
    place, third, _ = order(lattice)
    vectors = lax.dot_general(lattice.astype(BF16), place, (((1,), (1,)), ((), ())), preferred_element_type=F32)
    n = PLANES * ROWS
    row = iota((56, SLOTS), 0)
    upper = (row * 52) >> 8
    kz = (where_ref[0] * PLANES + upper).astype(F32)
    kx = (where_ref[2] * ROWS + row - ROWS * upper).astype(F32)
    ac, an = cos_sin(kx * vectors[0:1] + kz * vectors[2:3])
    ky = iota((HALF, SLOTS), 0).astype(F32)
    bc, bs = cos_sin(ky * vectors[1:2])

    def tile(t, ref, lane):
        cols = slice(t * 128, (t + 1) * 128)
        c, s = bc[:, cols], bs[:, cols]
        for r in range(0, n, 2):
            cosine, sine = [], []
            for k in (r, r + 1):
                u, v = ac[k : k + 1, cols], an[k : k + 1, cols]
                cosine.append(u * c - v * s)
                sine.append(v * c + u * s)
            rows = slice(r * HALF, (r + 2) * HALF)
            ref[rows, lane : lane + 128] = jnp.concatenate(cosine, axis=0).astype(BF16)
            ref[rows, lane + 128 : lane + 256] = jnp.concatenate(sine, axis=0).astype(BF16)

    tile(0, out_ref, 0)
    tile(1, out_ref, 256)

    @pl.when(third)
    def _():
        tile(2, out3_ref, 0)


def make_phases(where, lattice):
    return pl.pallas_call(
        phase_kernel,
        in_specs=[smem(), vmem()],
        out_specs=[vmem()] * 2,
        out_shape=[jax.ShapeDtypeStruct((POINTS, 512), BF16), jax.ShapeDtypeStruct((POINTS, 256), BF16)],
        compiler_params=pltpu.CompilerParams(vmem_limit_bytes=VMEM_LIMIT),
        cost_estimate=pl.CostEstimate(flops=1_500_000_000, bytes_accessed=3_000_000, transcendentals=0),
        name="phases",
    )(where, lattice)


def strength_kernel(table_ref, lattice_ref, p0, p1, p2, p3, ph_ref, ph3_ref, s_ref, off_ref, mixed_ref, g_ref, w_ref):
    for slot in range(QG):
        ref = (p0, p1, p2, p3)[slot // 2]
        start = (slot % 2) * PAY
        for part in range(2):
            for mode in range(NM):
                source = start + part * CH + mode * 16
                mixed_ref[part, mode * 128 + slot * 16 : mode * 128 + slot * 16 + 16, :] = ref[source : source + 16, :]
        line = ref[start + 2 * CH : start + 2 * CH + 16, :128].astype(F32)[:8]
        small = line if slot == 0 else jnp.where(iota((8, 128), 1) >> 4 == slot, line, small)
    off_ref[...] = small.astype(jnp.int32)
    place, third, wide = order(lattice_ref[...])
    general = third | wide

    def fill(first, count):
        span = count * 128
        rows = place[first * 128 : first * 128 + span]
        both = (((1,), (1,)), ((), ()))
        real = lax.dot_general(rows, mixed_ref[0], both, preferred_element_type=F32)
        imag = lax.dot_general(rows, mixed_ref[1], both, preferred_element_type=F32)
        minus = (-imag).astype(BF16)
        real = real.astype(BF16)
        imag = imag.astype(BF16)
        for t in range(count):
            here = slice(t * 128, (t + 1) * 128)
            low = (first + t) * 256
            for mode in range(NM):
                lanes = slice(mode * 128, (mode + 1) * 128)
                left = slice(mode * 256, mode * 256 + 128)
                right = slice(mode * 256 + 128, mode * 256 + 256)
                g_ref[low : low + 128, left] = real[here, lanes]
                g_ref[low : low + 128, right] = imag[here, lanes]
                g_ref[low + 128 : low + 256, left] = minus[here, lanes]
                g_ref[low + 128 : low + 256, right] = real[here, lanes]

    fill(0, 2)
    pl.when(third)(lambda: fill(2, 1))
    level = jnp.where(iota((NBIN, 128), 0) == small[:1].astype(jnp.int32), 1.0, 0.0).astype(BF16)
    table = table_ref[...]
    weights = None
    for _ in range(3):
        piece = table.astype(BF16)
        table = table - piece.astype(F32)
        got = jnp.dot(piece, level, preferred_element_type=F32)
        weights = got if weights is None else weights + got
    w_ref[:NM, :] = weights

    def square(x):
        return x[:, :128] * x[:, :128] + x[:, 128:] * x[:, 128:]

    def run(full):
        sign = jnp.where(wide, 1.0, -1.0)

        def body(step, carry):
            rows = pl.ds(pl.multiple_of(step * STEP, STEP), STEP)
            plus = minus = None
            for mode in range(NM):
                cols = slice(mode * 256, (mode + 1) * 256)
                one = jnp.dot(ph_ref[rows, :256], g_ref[:256, cols], preferred_element_type=F32)
                two = jnp.dot(ph_ref[rows, 256:], g_ref[256:512, cols], preferred_element_type=F32)
                if full:
                    three = jnp.dot(ph3_ref[rows, :], g_ref[512:, cols], preferred_element_type=F32)
                    three = jnp.where(third, three, 0.0)
                    sums, differences = one + two + three, one + sign * two - three
                else:
                    sums, differences = one + two, one - two
                weight = w_ref[mode : mode + 1, :]
                up, down = square(sums) * weight, square(differences) * weight
                plus = up if plus is None else plus + up
                minus = down if minus is None else minus + down
            s_ref[0, rows, :] = plus
            s_ref[1, rows, :] = minus
            return carry

        lax.fori_loop(0, POINTS // STEP, body, 0)

    pl.when(jnp.logical_not(general))(lambda: run(False))
    pl.when(general)(lambda: run(True))


def strengths(table, lattice, pays, phases, phases3):
    return pl.pallas_call(
        strength_kernel,
        in_specs=[vmem()] * 8,
        out_specs=[vmem()] * 2,
        out_shape=[jax.ShapeDtypeStruct((2, POINTS, 128), F32), jax.ShapeDtypeStruct((8, 128), jnp.int32)],
        scratch_shapes=[
            pltpu.VMEM((2, NM * 128, RW), BF16),
            pltpu.VMEM((768, 2 * NM * 128), BF16),
            pltpu.VMEM((8, 128), F32),
        ],
        compiler_params=pltpu.CompilerParams(vmem_limit_bytes=VMEM_LIMIT),
        cost_estimate=pl.CostEstimate(flops=4_000_000_000, bytes_accessed=6_000_000, transcendentals=0),
        name="strengths",
    )(table, lattice, *pays, phases, phases3)


def final_kernel(where_ref, off_a_ref, off_b_ref, own, *refs):
    parts = refs[: 2 * PARTS]
    sa_ref, sb_ref, out_ref, v_ref, arr_ref, off_ref, sem = refs[2 * PARTS :]
    slab = where_ref[0]
    core = where_ref[1]
    share = where_ref[2]
    copies = [
        pltpu.make_async_copy(off_a_ref, off_ref.at[0], sem.at[0]),
        pltpu.make_async_copy(off_b_ref, off_ref.at[1], sem.at[1]),
    ]

    def bring(src, plane, count):
        dst = v_ref.at[pl.ds(plane, count)]
        copies.append(pltpu.make_async_copy(src, dst.at[:, :, FRONT : FRONT + KX * KY], sem.at[len(copies)]))
        copies.append(pltpu.make_async_copy(src.at[:, :, :BACK], dst.at[:, :, FRONT + KX * KY :], sem.at[len(copies)]))
        copies.append(pltpu.make_async_copy(src.at[:, :, KX * KY - FRONT :], dst.at[:, :, :FRONT], sem.at[len(copies)]))

    bring(own, slab * PLANES, PLANES)
    for index in range(PARTS):
        for which in range(parts[index].shape[0]):
            source = where_ref[3 + WHICH[index] + which]
            bring(parts[index].at[which], source * PLANES + core * HP, HP)
            bring(parts[PARTS + index].at[which], source * PLANES + (1 - core) * HP, HP)
    for copy in copies:
        copy.start()

    ky = lax.rem(iota((NB, 512), 1), KY)
    row = iota((80, 256), 0)
    col = iota((80, 256), 1)
    gain = (row < 64) & (row >> 2 == col >> 4) & (row & 3 == col & 3)
    loss = (row >= 64) & (row - 64 == (col >> 2) & 3)
    spread = (jnp.where(gain, 1.0, 0.0) - jnp.where(loss, 1.0, 0.0)).astype(BF16)
    pick = jnp.where((iota((8, 128), 1) >> 2) & 3 == iota((8, 128), 0), 1.0, 0.0).astype(BF16)
    home = pl.multiple_of(((share * SHARE + FRONT) >> 7) * 128, 128)
    turn = lax.rem(WIN - lax.rem(share * SHARE, 128), WIN)
    arr_ref[:, 64:80, :] = jnp.zeros((UNROLL, 16, 512), F32)
    for copy in copies:
        copy.wait()

    def shift(step, lane):
        for slot in range(2 * QG):
            base = (slot % QG) * 16
            qx = off_ref[slot // QG, 1, base]
            qy = off_ref[slot // QG, 1, base + 1]
            qz = off_ref[slot // QG, 1, base + 2]
            plane = lax.rem(slab * PLANES + step + qz, KZ)
            first = lax.rem(share * ROWS + qx, KX) * KY
            start = first + qy + (FRONT - KY)
            aligned = pl.multiple_of((start >> 7) * 128, 128)
            window = v_ref[plane, :, pl.ds(aligned, WIN)].astype(F32)
            late = pltpu.roll(window, lax.rem(WIN - (start - aligned), WIN), 1)
            early = pltpu.roll(late, WIN - KY, 1)
            arr_ref[lane, NB * slot : NB * (slot + 1), :] = jnp.where(ky + qy < KY, early[:, :512], late[:, :512])
        window = v_ref[slab * PLANES + step, :, pl.ds(home, WIN)].astype(F32)
        arr_ref[lane, 64:68, :] = pltpu.roll(window, turn, 1)[:, :512]

    def combine(step, lane):
        arrived = arr_ref[lane].astype(BF16)
        diff = lax.dot_general(arrived, spread, (((0,), (0,)), ((), ())), preferred_element_type=F32)
        terms = []
        for kx in range(ROWS):
            for upper in range(2):
                rows = pl.ds(pl.multiple_of((step * ROWS + kx) * HALF, HALF), HALF)
                here = slice((2 * kx + upper) * HALF, (2 * kx + upper + 1) * HALF)
                terms.append(sa_ref[upper, rows, :] * diff[here, :128] + sb_ref[upper, rows, :] * diff[here, 128:])
        term = jnp.concatenate(terms, axis=0)
        result = None
        for _ in range(3):
            piece = term.astype(BF16)
            term = term - piece.astype(F32)
            got = lax.dot_general(pick, piece, (((1,), (1,)), ((), ())), preferred_element_type=F32)
            result = got if result is None else result + got
        out_ref[step] = result[:NB] * (1.0 / (2 * QG * NM))

    def body(step, carry):
        for lane in range(UNROLL):
            shift(step * UNROLL + lane, lane)
        for lane in range(UNROLL):
            combine(step * UNROLL + lane, lane)
        return carry

    lax.fori_loop(0, PLANES // UNROLL, body, 0)


def contract(where, off_a, off_b, own, parts, s_a, s_b):
    return pl.pallas_call(
        final_kernel,
        in_specs=[smem()] + [anywhere()] * (3 + 2 * PARTS) + [vmem()] * 2,
        out_specs=vmem(),
        out_shape=jax.ShapeDtypeStruct((PLANES, NB, SHARE), F32),
        scratch_shapes=[
            pltpu.VMEM((KZ, NB, VLANES), BF16),
            pltpu.VMEM((UNROLL, 80, 512), F32),
            pltpu.SMEM((2, 8, 128), jnp.int32),
            pltpu.SemaphoreType.DMA((47,)),
        ],
        compiler_params=pltpu.CompilerParams(vmem_limit_bytes=VMEM_LIMIT),
        cost_estimate=pl.CostEstimate(flops=2_000_000_000, bytes_accessed=9_000_000, transcendentals=0),
        name="contract",
    )(where, off_a, off_b, own, *parts, s_a, s_b)


def local(occupation, q_offsets, coupling, window_bins, lorentz_table, lattice):
    slab = lax.axis_index("ka")
    share = lax.axis_index("pb")
    core = share % 2
    vectors = jnp.pad(lattice, ((0, 5), (0, RW - NR)))

    def place(ylo, x, z, yhi, c):
        return ((ylo * 4 + x) * 16) + z * 4 + yhi * 2 + c

    def move(array, to):
        grid = [(yl, x, z, yh, c) for yl in range(2) for x in range(4) for z in range(4) for yh in range(2) for c in range(2)]
        return lax.ppermute(array, ("ka", "pb"), [(place(*at), place(*to(*at))) for at in grid])

    def core_swap(array):
        return move(array, lambda yl, x, z, yh, c: (yl, x, z, yh, 1 - c))

    pay = pack(q_offsets, window_bins, jnp.swapaxes(coupling[0], 1, 2))
    pair = jnp.concatenate([pay, move(pay, lambda yl, x, z, yh, c: (1 - yl, x, z, 1 - yh, c))], axis=0)
    group = [pair] + [move(pair, lambda yl, x, z, yh, c: (yl, x, (z + d) % 4, yh, c)) for d in (1, 3, 2)]
    other = [core_swap(array) for array in group]
    half = lax.dynamic_slice_in_dim(occupation, core * HP, HP, 0)[None]
    beyond = move(half, lambda yl, x, z, yh, c: (1 - yl, x, z, yh, c))
    both = jnp.concatenate([half, beyond], axis=0)
    fetched = [beyond] + [move(both, lambda yl, x, z, yh, c: (yl, (x + d) % 4, z, yh, c)) for d in (1, 3, 2)]
    swapped = [core_swap(array) for array in fetched]
    ylo, x = slab // 4, slab % 4
    sources = [(1 - ylo) * 4 + x]
    for d in (1, 3, 2):
        sources += [ylo * 4 + (x + 4 - d) % 4, (1 - ylo) * 4 + (x + 4 - d) % 4]
    where = jnp.stack([slab, core, share] + sources).astype(jnp.int32)

    phases, phases3 = make_phases(where, vectors)
    table = lorentz_table.T
    s_a, off_a = strengths(table, vectors, group, phases, phases3)
    s_b, off_b = strengths(table, vectors, other, phases, phases3)
    return contract(where, off_a, off_b, occupation, fetched + swapped, s_a, s_b)


def solution(mesh):
    in_specs = (
        P("ka", None, None),
        P("pb", None),
        P("pb", None, None, None),
        P("pb", None),
        P(),
        P(),
    )
    out_specs = P("ka", None, "pb")
    return jax.shard_map(local, mesh=mesh, in_specs=in_specs, out_specs=out_specs, check_vma=False)
```

time: 576 us -> 59.5 us (0.10)
  other arithmetic: 307 us -> 2.07 us
  waiting for transfers between devices: 115 us -> 5.93 us
  local copies, waits for them, and re-layouts: 90.6 us -> 1.16 us
  matrix products: 24.5 us -> 0 us
  Pallas kernels: 0 us -> 21.2 us
  starting transfers between devices: 12.2 us -> 28.7 us
  between operations: 16.8 us -> 0.3 us
  loops' own time: 7.39 us -> 0 us
    another operation x11 -> x0, other arithmetic: 244 us -> none
    unnamed x2 -> x0, waiting for transfers between devices: 81.7 us -> none
    unnamed x12 -> x6, local copies, waits for them, and re-layouts: 61 us -> 0.01 us
    ppermute x4 -> x16, waiting for transfers between devices: 33 us -> 5.93 us  [move(): lax.ppermute(array, ('ka', 'pb'), [(place(*at), place(*to(*at))) for at i...]
    dot_general x11 -> x0, matrix products: 24.5 us -> none  [the longest x10 23.7 us: plane_term(): couple = jnp.dot(mat_t, phases, preferred_element_type=jnp.float32)]
    pallas_call x0 -> x5, Pallas kernels: none -> 21.2 us  [the longest x2 9.67 us: strengths(): pl.pallas_call(strength_kernel, in_specs=[vmem()] * 8, out_specs=[vmem()]...]
    reshape x11 -> x0, local copies, waits for them, and re-layouts: 19.7 us -> none  [the longest x10 18.3 us: plane_term(): strength = (squared * weight[:, None]).reshape(NB, NB, NM, -1).sum(axis=2)]
    mul x21 -> x0, other arithmetic: 18.7 us -> none  [the longest x10 18 us: plane_term(): strength = (squared * weight[:, None]).reshape(NB, NB, NM, -1).sum(axis=2)]
  transfers between devices with their start and end apart: 5 -> 16, of which waited for: 5 -> 2; matrix products, arithmetic and copies ran while one was open for 1% -> 4% of each run, Pallas kernels for 0% -> 22%
where the time goes in v2:
time: 59.5 us; the launch traced here: 59.3 us
  starting transfers between devices  28.7 us (48%)
  Pallas kernels  21.2 us (36%)
  waiting for transfers between devices  5.93 us (10%)
  other arithmetic  2.07 us (3%)
  local copies, waits for them, and re-layouts  1.16 us (2%)
    ppermute x16, starting transfers between devices, move(): lax.ppermute(array, ('ka', 'pb'), [(place(*at), place(*to(*at))) for at i...  28.7 us
    pallas_call x2, Pallas kernels, strengths(): pl.pallas_call(strength_kernel, in_specs=[vmem()] * 8, out_specs=[vmem()]...  9.67 us
    pallas_call x1, Pallas kernels, contract(): pl.pallas_call(final_kernel, in_specs=[smem()] + [anywhere()] * (3 + 2 *...  8.13 us
    ppermute x16, waiting for transfers between devices, move(): lax.ppermute(array, ('ka', 'pb'), [(place(*at), place(*to(*at))) for at i...  5.93 us
    pallas_call x1, Pallas kernels, pack(): pl.pallas_call(pack_kernel, in_specs=[smem(), smem(), vmem()], out_specs=...  1.71 us
    pallas_call x1, Pallas kernels, make_phases(): pl.pallas_call(phase_kernel, in_specs=[smem(), vmem()], out_specs=[vmem()...  1.64 us
  transfers between devices with their start and end apart: 16, of which 2 were waited for; matrix products, arithmetic and copies ran while one was open for 4% of the time, Pallas kernels for 22%

profile of v2, /device:TPU:1, one launch (start us, length us, event | category | flops | bytes accessed | tf_op | source)
XLA Modules:
  0.0 59.3 jit_solution(977069893327714316)
XLA Ops:
  0.0 0.0 copy-start.2
  0.0 1.1 %dynamic-slice_bitcast_fusion = bf16[1,5,4,6400]{3,2,1,0:T(4,128)(2,1)S(1)} fusion(bf16[10,4,6400]{2,1,0:T(4,128)(2,1)} %own.1, s32[]{:T(128)S(6)} %select_n.42), kind=kLoop, calls=%fused_computation.1 | loop fusion | bytes 512004 | tf_op jit(solution)/shard_map/broadcast_in_dim | solution.py:386
  1.1 2.2 %collective-permute-start.8 = (bf16[1,5,4,6400]{3,2,1,0:T(4,128)(2,1)S(1)}, bf16[1,5,4,6400]{3,2,1,0:T(4,128)(2,1)S(1)}, u32[]{:S(2)}, u32[]{:S(2)}) collective-permute-start(bf16[1,5,4,6400]{3,2,1,0:T(4,128)(2,1)S(1)} %dynamic-slice_bitcast_fusion), channel_id=1, source_target_pairs={{0,64},{1,65},{2,66},{3,67},{4,68},{5,69},{6,70},{7,71},{8,72},{9,... | collective-permute-start | bytes 768008 | tf_op jit(solution)/shard_map/ppermute | solution.py:377
  3.3 1.7 %pack.1 = bf16[208,256]{1,0:T(8,128)(2,1)} custom-call(s32[1,3]{1,0:T(1,128)} %off_ref.1, s32[1,16]{1,0:T(1,128)} %bins_ref.1, bf16[2,96,200]{2,1,0:T(8,128)(2,1)} %bitcast.18), custom_call_target="tpu_custom_call" | custom-call | tf_op jit(solution)/shard_map/pack/pallas_call | solution.py:76
  5.0 1.9 %collective-permute-start = (bf16[208,256]{1,0:T(8,128)(2,1)}, bf16[208,256]{1,0:T(8,128)(2,1)S(1)}, u32[]{:S(2)}, u32[]{:S(2)}) collective-permute-start(bf16[208,256]{1,0:T(8,128)(2,1)} %pack.1), channel_id=1, source_target_pairs={{0,66},{1,67},{2,64},{3,65},{4,70},{5,71},{6,68},{7,69},{8,74},{9,... | collective-permute-start | bytes 319496 | tf_op jit(solution)/shard_map/ppermute | solution.py:377
  6.9 3.1 %collective-permute-done = bf16[208,256]{1,0:T(8,128)(2,1)S(1)} collective-permute-done((bf16[208,256]{1,0:T(8,128)(2,1)}, bf16[208,256]{1,0:T(8,128)(2,1)S(1)}, u32[]{:S(2)}, u32[]{:S(2)}) %collective-permute-start) | collective-permute-done | bytes 106528 | tf_op jit(solution)/shard_map/ppermute | solution.py:377
  9.9 0.9 %pad_maximum_fusion.1.p0 = bf16[416,256]{1,0:T(8,128)(2,1)S(1)} fusion(bf16[208,256]{1,0:T(8,128)(2,1)S(1)} %collective-permute-done, bf16[208,256]{1,0:T(8,128)(2,1)} %pack.1), kind=kLoop, calls=%fused_computation.2 | loop fusion | flops 425984 | bytes 425984 | tf_op jit(solution)/shard_map/concatenate | solution.py:383
  10.9 1.7 %collective-permute-start.1 = (bf16[416,256]{1,0:T(8,128)(2,1)S(1)}, bf16[416,256]{1,0:T(8,128)(2,1)S(1)}, u32[]{:S(2)}, u32[]{:S(2)}) collective-permute-start(bf16[416,256]{1,0:T(8,128)(2,1)S(1)} %pad_maximum_fusion.1.p0), channel_id=1, source_target_pairs={{0,4},{1,5},{2,6},{3,7},{4,8},{5,9},{6,10},{7,11},{8,12},{9,13},{1... | collective-permute-start | bytes 638984 | tf_op jit(solution)/shard_map/ppermute | solution.py:377
  12.6 0.0 collective-permute-done.8.refs_0_
  12.6 1.2 %pad_maximum_fusion = bf16[2,5,4,6400]{3,2,1,0:T(4,128)(2,1)} fusion(bf16[1,5,4,6400]{3,2,1,0:T(4,128)(2,1)S(1)} %collective-permute-done.8.refs_0_, bf16[1,5,4,6400]{3,2,1,0:T(4,128)(2,1)S(1)} %dynamic-slice_bitcast_fusion), kind=kLoop, calls=%fused_computation | loop fusion | flops 256000 | bytes 1024000 | tf_op jit(solution)/shard_map/concatenate | solution.py:388
  13.7 1.2 %collective-permute-start.9 = (bf16[2,5,4,6400]{3,2,1,0:T(4,128)(2,1)}, bf16[2,5,4,6400]{3,2,1,0:T(4,128)(2,1)S(1)}, u32[]{:S(2)}, u32[]{:S(2)}) collective-permute-start(bf16[2,5,4,6400]{3,2,1,0:T(4,128)(2,1)} %pad_maximum_fusion), channel_id=1, source_target_pairs={{0,16},{1,17},{2,18},{3,19},{4,20},{5,21},{6,22},{7,23},{8,24},{9,... | collective-permute-start | bytes 1536008 | tf_op jit(solution)/shard_map/ppermute | solution.py:377
  14.9 1.5 %collective-permute-start.10 = (bf16[2,5,4,6400]{3,2,1,0:T(4,128)(2,1)}, bf16[2,5,4,6400]{3,2,1,0:T(4,128)(2,1)S(1)}, u32[]{:S(2)}, u32[]{:S(2)}) collective-permute-start(bf16[2,5,4,6400]{3,2,1,0:T(4,128)(2,1)} %pad_maximum_fusion), channel_id=1, source_target_pairs={{0,48},{1,49},{2,50},{3,51},{4,52},{5,53},{6,54},{7,55},{8,56},{9,... | collective-permute-start | bytes 1536008 | tf_op jit(solution)/shard_map/ppermute | solution.py:377
  16.4 1.5 %collective-permute-start.11 = (bf16[2,5,4,6400]{3,2,1,0:T(4,128)(2,1)}, bf16[2,5,4,6400]{3,2,1,0:T(4,128)(2,1)S(1)}, u32[]{:S(2)}, u32[]{:S(2)}) collective-permute-start(bf16[2,5,4,6400]{3,2,1,0:T(4,128)(2,1)} %pad_maximum_fusion), channel_id=1, source_target_pairs={{0,32},{1,33},{2,34},{3,35},{4,36},{5,37},{6,38},{7,39},{8,40},{9,... | collective-permute-start | bytes 1536008 | tf_op jit(solution)/shard_map/ppermute | solution.py:377
  17.9 2.1 %collective-permute-start.2 = (bf16[416,256]{1,0:T(8,128)(2,1)S(1)}, bf16[416,256]{1,0:T(8,128)(2,1)S(1)}, u32[]{:S(2)}, u32[]{:S(2)}) collective-permute-start(bf16[416,256]{1,0:T(8,128)(2,1)S(1)} %pad_maximum_fusion.1.p0), channel_id=1, source_target_pairs={{0,12},{1,13},{2,14},{3,15},{4,0},{5,1},{6,2},{7,3},{8,4},{9,5},{1... | collective-permute-start | bytes 638984 | tf_op jit(solution)/shard_map/ppermute | solution.py:377
  20.1 0.0 collective-permute-done.1.p1
  20.1 1.3 %collective-permute-start.3 = (bf16[416,256]{1,0:T(8,128)(2,1)S(1)}, bf16[416,256]{1,0:T(8,128)(2,1)S(1)}, u32[]{:S(2)}, u32[]{:S(2)}) collective-permute-start(bf16[416,256]{1,0:T(8,128)(2,1)S(1)} %pad_maximum_fusion.1.p0), channel_id=1, source_target_pairs={{0,8},{1,9},{2,10},{3,11},{4,12},{5,13},{6,14},{7,15},{8,0},{9,1},... | collective-permute-start | bytes 638984 | tf_op jit(solution)/shard_map/ppermute | solution.py:377
  21.4 2.8 %collective-permute-done.2.p2 = bf16[416,256]{1,0:T(8,128)(2,1)S(1)} collective-permute-done((bf16[416,256]{1,0:T(8,128)(2,1)S(1)}, bf16[416,256]{1,0:T(8,128)(2,1)S(1)}, u32[]{:S(2)}, u32[]{:S(2)}) %collective-permute-start.2) | collective-permute-done | bytes 213024 | tf_op jit(solution)/shard_map/ppermute | solution.py:377
  24.2 6.0 %collective-permute-start.4 = (bf16[416,256]{1,0:T(8,128)(2,1)S(1)}, bf16[416,256]{1,0:T(8,128)(2,1)S(1)}, u32[]{:S(2)}, u32[]{:S(2)}) collective-permute-start(bf16[416,256]{1,0:T(8,128)(2,1)S(1)} %pad_maximum_fusion.1.p0), channel_id=1, source_target_pairs={{0,1},{1,0},{2,3},{3,2},{4,5},{5,4},{6,7},{7,6},{8,9},{9,8},{10,11... | collective-permute-start | bytes 638984 | tf_op jit(solution)/shard_map/ppermute | solution.py:377
  30.1 0.0 collective-permute-done.3.p3
  30.2 0.5 collective-permute-start.5
  30.7 0.0 copy-done.2
  30.7 0.1 stack.43.where_ref
  30.8 0.0 copy-start.1
  30.8 1.6 %phases.1 = (bf16[2000,512]{1,0:T(8,128)(2,1)S(1)}, bf16[2000,256]{1,0:T(8,128)(2,1)S(1)}) custom-call(s32[10]{0:T(128)S(1)} %stack.43.where_ref, s32[8,256]{1,0:T(8,128)S(1)} %pad.4.lattice_ref), custom_call_target="tpu_custom_call" | custom-call | flops 1500000000 | bytes 3000000 | tf_op jit(solution)/shard_map/phases/pallas_call | solution.py:156
  32.4 0.0 collective-permute-done.4.p0
  32.4 0.1 collective-permute-start.6
  32.5 0.0 collective-permute-done.5.p1
  32.5 0.5 collective-permute-start.7
  33.0 0.0 collective-permute-done.9.refs_1_
  33.0 0.1 collective-permute-start.13
  33.1 0.0 collective-permute-done.10.refs_2_
  33.1 6.5 %collective-permute-start.14 = (bf16[2,5,4,6400]{3,2,1,0:T(4,128)(2,1)S(1)}, bf16[2,5,4,6400]{3,2,1,0:T(4,128)(2,1)S(1)}, u32[]{:S(2)}, u32[]{:S(2)}) collective-permute-start(bf16[2,5,4,6400]{3,2,1,0:T(4,128)(2,1)S(1)} %collective-permute-done.10.refs_2_), channel_id=1, source_target_pairs={{0,1},{1,0},{2,3},{3,2},{4,5},{5,4},{6,7},{7,6},{8,9},{9,8},{10,11... | collective-permute-start | bytes 1536008 | tf_op jit(solution)/shard_map/ppermute | solution.py:377
  39.6 0.0 collective-permute-done.11.refs_3_
  39.6 1.6 %collective-permute-start.15 = (bf16[2,5,4,6400]{3,2,1,0:T(4,128)(2,1)S(1)}, bf16[2,5,4,6400]{3,2,1,0:T(4,128)(2,1)S(1)}, u32[]{:S(2)}, u32[]{:S(2)}) collective-permute-start(bf16[2,5,4,6400]{3,2,1,0:T(4,128)(2,1)S(1)} %collective-permute-done.11.refs_3_), channel_id=1, source_target_pairs={{0,1},{1,0},{2,3},{3,2},{4,5},{5,4},{6,7},{7,6},{8,9},{9,8},{10,11... | collective-permute-start | bytes 1536008 | tf_op jit(solution)/shard_map/ppermute | solution.py:377
  41.2 0.0 copy-done.1
  41.2 4.8 %strengths.2 = (f32[2,2000,128]{2,1,0:T(8,128)S(1)}, s32[8,128]{1,0:T(8,128)S(1)}) custom-call(f32[6,32]{1,0:T(8,128)S(1)} %bitcast.16, s32[8,256]{1,0:T(8,128)S(1)} %pad.4.lattice_ref, bf16[416,256]{1,0:T(8,128)(2,1)S(1)} %pad_maximum_fusion.1.p0, bf16[416,256]{1,0:T(8,128)(2,1)S(1)} %collective-permute-done.1.p1, ...), custom_call_target="tpu_custom_call" | custom-call | flops 4000000000 | bytes 6000000 | tf_op jit(solution)/shard_map/strengths/pallas_call | solution.py:248
  46.0 0.0 copy-start
  46.0 0.0 collective-permute-done.6.p2
  46.0 0.1 collective-permute-start.12
  46.1 0.0 collective-permute-done.7.p3
  46.1 4.9 %strengths.3 = (f32[2,2000,128]{2,1,0:T(8,128)S(1)}, s32[8,128]{1,0:T(8,128)S(1)}) custom-call(f32[6,32]{1,0:T(8,128)S(1)} %bitcast.17, s32[8,256]{1,0:T(8,128)S(1)} %pad.4.lattice_ref, bf16[416,256]{1,0:T(8,128)(2,1)S(1)} %collective-permute-done.4.p0, bf16[416,256]{1,0:T(8,128)(2,1)S(1)} %collective-permute-done.5.p1, ...), custom_call_target="tpu_custom_call" | custom-call | flops 4000000000 | bytes 6000000 | tf_op jit(solution)/shard_map/strengths/pallas_call | solution.py:248
  51.0 0.0 collective-permute-done.12.refs_4_
  51.0 0.0 collective-permute-done.13.refs_5_
  51.0 0.0 collective-permute-done.14.refs_6_
  51.0 0.0 collective-permute-done.15.refs_7_
  51.0 0.0 copy-done
  51.1 8.1 %contract.1 = f32[10,4,400]{2,1,0:T(4,128)} custom-call(s32[10]{0:T(128)S(1)} %stack.43.where_ref, s32[8,128]{1,0:T(8,128)S(1)} %get-tuple-element.13.off_a_ref, s32[8,128]{1,0:T(8,128)S(1)} %get-tuple-element.14.off_b_ref, bf16[10,4,6400]{2,1,0:T(4,128)(2,1)S(1)} %copy-done, bf16[1,5,4,6400]{3,2,1,0:T(4,128)(2,1)S(1)} %collective-permute-done.8.refs_0_, ...), custom_call_target="tpu_custom_call" | custom-call | flops 2000000000 | bytes 9000000 | tf_op jit(solution)/shard_map/contract/pallas_call | solution.py:349
  (1 shorter events, 0.0 us)
Async XLA Ops:
  0.0 30.7 %copy-start.2 = (s32[3,200]{1,0:T(4,128)S(1)}, s32[3,200]{1,0:T(4,128)}, u32[]{:S(2)}) copy-start(s32[3,200]{1,0:T(4,128)} %param.11) | copy-start | bytes 7204
  1.1 11.5 %collective-permute-start.8 = (bf16[1,5,4,6400]{3,2,1,0:T(4,128)(2,1)S(1)}, bf16[1,5,4,6400]{3,2,1,0:T(4,128)(2,1)S(1)}, u32[]{:S(2)}, u32[]{:S(2)}) collective-permute-start(bf16[1,5,4,6400]{3,2,1,0:T(4,128)(2,1)S(1)} %dynamic-slice_bitcast_fusion), channel_id=1, source_target_pairs={{0,64},{1,65},{2,66},{3,67},{4,68},{5,69},{6,70},{7,71},{8,72},{9,... | collective-permute-start | bytes 768008 | tf_op jit(solution)/shard_map/ppermute | solution.py:377
  5.0 5.0 %collective-permute-start = (bf16[208,256]{1,0:T(8,128)(2,1)}, bf16[208,256]{1,0:T(8,128)(2,1)S(1)}, u32[]{:S(2)}, u32[]{:S(2)}) collective-permute-start(bf16[208,256]{1,0:T(8,128)(2,1)} %pack.1), channel_id=1, source_target_pairs={{0,66},{1,67},{2,64},{3,65},{4,70},{5,71},{6,68},{7,69},{8,74},{9,... | collective-permute-start | bytes 319496 | tf_op jit(solution)/shard_map/ppermute | solution.py:377
  10.9 9.2 %collective-permute-start.1 = (bf16[416,256]{1,0:T(8,128)(2,1)S(1)}, bf16[416,256]{1,0:T(8,128)(2,1)S(1)}, u32[]{:S(2)}, u32[]{:S(2)}) collective-permute-start(bf16[416,256]{1,0:T(8,128)(2,1)S(1)} %pad_maximum_fusion.1.p0), channel_id=1, source_target_pairs={{0,4},{1,5},{2,6},{3,7},{4,8},{5,9},{6,10},{7,11},{8,12},{9,13},{1... | collective-permute-start | bytes 638984 | tf_op jit(solution)/shard_map/ppermute | solution.py:377
  13.7 19.3 %collective-permute-start.9 = (bf16[2,5,4,6400]{3,2,1,0:T(4,128)(2,1)}, bf16[2,5,4,6400]{3,2,1,0:T(4,128)(2,1)S(1)}, u32[]{:S(2)}, u32[]{:S(2)}) collective-permute-start(bf16[2,5,4,6400]{3,2,1,0:T(4,128)(2,1)} %pad_maximum_fusion), channel_id=1, source_target_pairs={{0,16},{1,17},{2,18},{3,19},{4,20},{5,21},{6,22},{7,23},{8,24},{9,... | collective-permute-start | bytes 1536008 | tf_op jit(solution)/shard_map/ppermute | solution.py:377
  14.9 18.2 %collective-permute-start.10 = (bf16[2,5,4,6400]{3,2,1,0:T(4,128)(2,1)}, bf16[2,5,4,6400]{3,2,1,0:T(4,128)(2,1)S(1)}, u32[]{:S(2)}, u32[]{:S(2)}) collective-permute-start(bf16[2,5,4,6400]{3,2,1,0:T(4,128)(2,1)} %pad_maximum_fusion), channel_id=1, source_target_pairs={{0,48},{1,49},{2,50},{3,51},{4,52},{5,53},{6,54},{7,55},{8,56},{9,... | collective-permute-start | bytes 1536008 | tf_op jit(solution)/shard_map/ppermute | solution.py:377
  16.4 23.2 %collective-permute-start.11 = (bf16[2,5,4,6400]{3,2,1,0:T(4,128)(2,1)}, bf16[2,5,4,6400]{3,2,1,0:T(4,128)(2,1)S(1)}, u32[]{:S(2)}, u32[]{:S(2)}) collective-permute-start(bf16[2,5,4,6400]{3,2,1,0:T(4,128)(2,1)} %pad_maximum_fusion), channel_id=1, source_target_pairs={{0,32},{1,33},{2,34},{3,35},{4,36},{5,37},{6,38},{7,39},{8,40},{9,... | collective-permute-start | bytes 1536008 | tf_op jit(solution)/shard_map/ppermute | solution.py:377
  17.9 6.2 %collective-permute-start.2 = (bf16[416,256]{1,0:T(8,128)(2,1)S(1)}, bf16[416,256]{1,0:T(8,128)(2,1)S(1)}, u32[]{:S(2)}, u32[]{:S(2)}) collective-permute-start(bf16[416,256]{1,0:T(8,128)(2,1)S(1)} %pad_maximum_fusion.1.p0), channel_id=1, source_target_pairs={{0,12},{1,13},{2,14},{3,15},{4,0},{5,1},{6,2},{7,3},{8,4},{9,5},{1... | collective-permute-start | bytes 638984 | tf_op jit(solution)/shard_map/ppermute | solution.py:377
  20.1 10.1 %collective-permute-start.3 = (bf16[416,256]{1,0:T(8,128)(2,1)S(1)}, bf16[416,256]{1,0:T(8,128)(2,1)S(1)}, u32[]{:S(2)}, u32[]{:S(2)}) collective-permute-start(bf16[416,256]{1,0:T(8,128)(2,1)S(1)} %pad_maximum_fusion.1.p0), channel_id=1, source_target_pairs={{0,8},{1,9},{2,10},{3,11},{4,12},{5,13},{6,14},{7,15},{8,0},{9,1},... | collective-permute-start | bytes 638984 | tf_op jit(solution)/shard_map/ppermute | solution.py:377
  24.2 8.2 %collective-permute-start.4 = (bf16[416,256]{1,0:T(8,128)(2,1)S(1)}, bf16[416,256]{1,0:T(8,128)(2,1)S(1)}, u32[]{:S(2)}, u32[]{:S(2)}) collective-permute-start(bf16[416,256]{1,0:T(8,128)(2,1)S(1)} %pad_maximum_fusion.1.p0), channel_id=1, source_target_pairs={{0,1},{1,0},{2,3},{3,2},{4,5},{5,4},{6,7},{7,6},{8,9},{9,8},{10,11... | collective-permute-start | bytes 638984 | tf_op jit(solution)/shard_map/ppermute | solution.py:377
  30.2 2.4 %collective-permute-start.5 = (bf16[416,256]{1,0:T(8,128)(2,1)S(1)}, bf16[416,256]{1,0:T(8,128)(2,1)S(1)}, u32[]{:S(2)}, u32[]{:S(2)}) collective-permute-start(bf16[416,256]{1,0:T(8,128)(2,1)S(1)} %collective-permute-done.1.p1), channel_id=1, source_target_pairs={{0,1},{1,0},{2,3},{3,2},{4,5},{5,4},{6,7},{7,6},{8,9},{9,8},{10,11... | collective-permute-start | bytes 638984 | tf_op jit(solution)/shard_map/ppermute | solution.py:377
  30.8 10.4 %copy-start.1 = (f32[32,6]{0,1:T(8,128)S(1)}, f32[32,6]{0,1:T(8,128)}, u32[]{:S(2)}) copy-start(f32[32,6]{0,1:T(8,128)} %param.10) | copy-start | bytes 2308
  32.4 13.6 %collective-permute-start.6 = (bf16[416,256]{1,0:T(8,128)(2,1)S(1)}, bf16[416,256]{1,0:T(8,128)(2,1)S(1)}, u32[]{:S(2)}, u32[]{:S(2)}) collective-permute-start(bf16[416,256]{1,0:T(8,128)(2,1)S(1)} %collective-permute-done.2.p2), channel_id=1, source_target_pairs={{0,1},{1,0},{2,3},{3,2},{4,5},{5,4},{6,7},{7,6},{8,9},{9,8},{10,11... | collective-permute-start | bytes 638984 | tf_op jit(solution)/shard_map/ppermute | solution.py:377
  32.5 13.6 %collective-permute-start.7 = (bf16[416,256]{1,0:T(8,128)(2,1)S(1)}, bf16[416,256]{1,0:T(8,128)(2,1)S(1)}, u32[]{:S(2)}, u32[]{:S(2)}) collective-permute-start(bf16[416,256]{1,0:T(8,128)(2,1)S(1)} %collective-permute-done.3.p3), channel_id=1, source_target_pairs={{0,1},{1,0},{2,3},{3,2},{4,5},{5,4},{6,7},{7,6},{8,9},{9,8},{10,11... | collective-permute-start | bytes 638984 | tf_op jit(solution)/shard_map/ppermute | solution.py:377
  33.0 18.0 %collective-permute-start.13 = (bf16[2,5,4,6400]{3,2,1,0:T(4,128)(2,1)S(1)}, bf16[2,5,4,6400]{3,2,1,0:T(4,128)(2,1)S(1)}, u32[]{:S(2)}, u32[]{:S(2)}) collective-permute-start(bf16[2,5,4,6400]{3,2,1,0:T(4,128)(2,1)S(1)} %collective-permute-done.9.refs_1_), channel_id=1, source_target_pairs={{0,1},{1,0},{2,3},{3,2},{4,5},{5,4},{6,7},{7,6},{8,9},{9,8},{10,11... | collective-permute-start | bytes 1536008 | tf_op jit(solution)/shard_map/ppermute | solution.py:377
  33.1 17.9 %collective-permute-start.14 = (bf16[2,5,4,6400]{3,2,1,0:T(4,128)(2,1)S(1)}, bf16[2,5,4,6400]{3,2,1,0:T(4,128)(2,1)S(1)}, u32[]{:S(2)}, u32[]{:S(2)}) collective-permute-start(bf16[2,5,4,6400]{3,2,1,0:T(4,128)(2,1)S(1)} %collective-permute-done.10.refs_2_), channel_id=1, source_target_pairs={{0,1},{1,0},{2,3},{3,2},{4,5},{5,4},{6,7},{7,6},{8,9},{9,8},{10,11... | collective-permute-start | bytes 1536008 | tf_op jit(solution)/shard_map/ppermute | solution.py:377
  39.6 11.4 %collective-permute-start.15 = (bf16[2,5,4,6400]{3,2,1,0:T(4,128)(2,1)S(1)}, bf16[2,5,4,6400]{3,2,1,0:T(4,128)(2,1)S(1)}, u32[]{:S(2)}, u32[]{:S(2)}) collective-permute-start(bf16[2,5,4,6400]{3,2,1,0:T(4,128)(2,1)S(1)} %collective-permute-done.11.refs_3_), channel_id=1, source_target_pairs={{0,1},{1,0},{2,3},{3,2},{4,5},{5,4},{6,7},{7,6},{8,9},{9,8},{10,11... | collective-permute-start | bytes 1536008 | tf_op jit(solution)/shard_map/ppermute | solution.py:377
  46.0 5.0 %copy-start = (bf16[10,4,6400]{2,1,0:T(4,128)(2,1)S(1)}, bf16[10,4,6400]{2,1,0:T(4,128)(2,1)}, u32[]{:S(2)}) copy-start(bf16[10,4,6400]{2,1,0:T(4,128)(2,1)} %own.1) | copy-start | bytes 1536004
  46.0 5.0 %collective-permute-start.12 = (bf16[1,5,4,6400]{3,2,1,0:T(4,128)(2,1)S(1)}, bf16[1,5,4,6400]{3,2,1,0:T(4,128)(2,1)S(1)}, u32[]{:S(2)}, u32[]{:S(2)}) collective-permute-start(bf16[1,5,4,6400]{3,2,1,0:T(4,128)(2,1)S(1)} %collective-permute-done.8.refs_0_), channel_id=1, source_target_pairs={{0,1},{1,0},{2,3},{3,2},{4,5},{5,4},{6,7},{7,6},{8,9},{9,8},{10,11... | collective-permute-start | bytes 768008 | tf_op jit(solution)/shard_map/ppermute | solution.py:377

commit v3 on v2

--- a/solution.py
+++ b/solution.py
@@ -19,8 +19,8 @@
 QG = 8
 PLANES = 10
 HP = PLANES // 2
-PARTS = 4
-WHICH = (0, 1, 3, 5)
+PARTS = 5
+WHICH = (0, 1, 2, 3, 5)
 ROWS = 5
 HALF = KY // 2
 SHARE = ROWS * KY
@@ -32,7 +32,7 @@
 VLANES = FRONT + KX * KY + BACK
 WIN = 640
 STEP = 400
-UNROLL = 5
+UNROLL = 10
 VMEM_LIMIT = 28 * 1024 * 1024
 F32 = jnp.float32
 BF16 = jnp.bfloat16
@@ -48,6 +48,10 @@
 
 def anywhere():
     return pl.BlockSpec(memory_space=pl.ANY)
+
+
+def wrap(value, size):
+    return jnp.where(value >= size, value - size, value)
 
 
 def iota(shape, axis):
@@ -118,8 +122,14 @@
     return place, third, wide
 
 
-def phase_kernel(where_ref, lattice_ref, out_ref, out3_ref):
-    lattice = lattice_ref[...]
+def widen(lattice_ref, wide_ref):
+    wide_ref[...] = jnp.zeros((8, RW), jnp.int32)
+    wide_ref[:3, :NR] = lattice_ref[...]
+    return wide_ref[...]
+
+
+def phase_kernel(where_ref, lattice_ref, out_ref, out3_ref, wide_ref):
+    lattice = widen(lattice_ref, wide_ref)
     place, third, _ = order(lattice)
     vectors = lax.dot_general(lattice.astype(BF16), place, (((1,), (1,)), ((), ())), preferred_element_type=F32)
     n = PLANES * ROWS
@@ -158,58 +168,64 @@
         in_specs=[smem(), vmem()],
         out_specs=[vmem()] * 2,
         out_shape=[jax.ShapeDtypeStruct((POINTS, 512), BF16), jax.ShapeDtypeStruct((POINTS, 256), BF16)],
+        scratch_shapes=[pltpu.VMEM((8, RW), jnp.int32)],
         compiler_params=pltpu.CompilerParams(vmem_limit_bytes=VMEM_LIMIT),
         cost_estimate=pl.CostEstimate(flops=1_500_000_000, bytes_accessed=3_000_000, transcendentals=0),
         name="phases",
     )(where, lattice)
 
 
-def strength_kernel(table_ref, lattice_ref, p0, p1, p2, p3, ph_ref, ph3_ref, s_ref, off_ref, mixed_ref, g_ref, w_ref):
-    for slot in range(QG):
-        ref = (p0, p1, p2, p3)[slot // 2]
+def strength_kernel(table_ref, lattice_ref, *refs):
+    pays = refs[:8]
+    ph_ref, ph3_ref, s_ref, off_ref, mixed_ref, g_ref, w_ref, wide_ref = refs[8:]
+    for slot in range(2 * QG):
+        ref = pays[slot // 2]
         start = (slot % 2) * PAY
+        group, inner = slot // QG, slot % QG
         for part in range(2):
             for mode in range(NM):
                 source = start + part * CH + mode * 16
-                mixed_ref[part, mode * 128 + slot * 16 : mode * 128 + slot * 16 + 16, :] = ref[source : source + 16, :]
+                mixed_ref[group, part, mode * 128 + inner * 16 : mode * 128 + inner * 16 + 16, :] = ref[source : source + 16, :]
         line = ref[start + 2 * CH : start + 2 * CH + 16, :128].astype(F32)[:8]
-        small = line if slot == 0 else jnp.where(iota((8, 128), 1) >> 4 == slot, line, small)
-    off_ref[...] = small.astype(jnp.int32)
-    place, third, wide = order(lattice_ref[...])
+        small = line if inner == 0 else jnp.where(iota((8, 128), 1) >> 4 == inner, line, small)
+        if inner == QG - 1:
+            off_ref[group] = small.astype(jnp.int32)
+            level = jnp.where(iota((NBIN, 128), 0) == small[:1].astype(jnp.int32), 1.0, 0.0).astype(BF16)
+            table = table_ref[...]
+            weights = None
+            for _ in range(3):
+                piece = table.astype(BF16)
+                table = table - piece.astype(F32)
+                got = jnp.dot(piece, level, preferred_element_type=F32)
+                weights = got if weights is None else weights + got
+            w_ref[group, :NM, :] = weights
+    place, third, wide = order(widen(lattice_ref, wide_ref))
     general = third | wide
 
     def fill(first, count):
         span = count * 128
         rows = place[first * 128 : first * 128 + span]
         both = (((1,), (1,)), ((), ()))
-        real = lax.dot_general(rows, mixed_ref[0], both, preferred_element_type=F32)
-        imag = lax.dot_general(rows, mixed_ref[1], both, preferred_element_type=F32)
-        minus = (-imag).astype(BF16)
-        real = real.astype(BF16)
-        imag = imag.astype(BF16)
-        for t in range(count):
-            here = slice(t * 128, (t + 1) * 128)
-            low = (first + t) * 256
-            for mode in range(NM):
-                lanes = slice(mode * 128, (mode + 1) * 128)
-                left = slice(mode * 256, mode * 256 + 128)
-                right = slice(mode * 256 + 128, mode * 256 + 256)
-                g_ref[low : low + 128, left] = real[here, lanes]
-                g_ref[low : low + 128, right] = imag[here, lanes]
-                g_ref[low + 128 : low + 256, left] = minus[here, lanes]
-                g_ref[low + 128 : low + 256, right] = real[here, lanes]
+        for group in range(2):
+            real = lax.dot_general(rows, mixed_ref[group, 0], both, preferred_element_type=F32)
+            imag = lax.dot_general(rows, mixed_ref[group, 1], both, preferred_element_type=F32)
+            minus = (-imag).astype(BF16)
+            real = real.astype(BF16)
+            imag = imag.astype(BF16)
+            for t in range(count):
+                here = slice(t * 128, (t + 1) * 128)
+                low = (first + t) * 256
+                for mode in range(NM):
+                    lanes = slice(mode * 128, (mode + 1) * 128)
+                    left = slice(mode * 256, mode * 256 + 128)
+                    right = slice(mode * 256 + 128, mode * 256 + 256)
+                    g_ref[group, low : low + 128, left] = real[here, lanes]
+                    g_ref[group, low : low + 128, right] = imag[here, lanes]
+                    g_ref[group, low + 128 : low + 256, left] = minus[here, lanes]
+                    g_ref[group, low + 128 : low + 256, right] = real[here, lanes]
 
     fill(0, 2)
     pl.when(third)(lambda: fill(2, 1))
-    level = jnp.where(iota((NBIN, 128), 0) == small[:1].astype(jnp.int32), 1.0, 0.0).astype(BF16)
-    table = table_ref[...]
-    weights = None
-    for _ in range(3):
-        piece = table.astype(BF16)
-        table = table - piece.astype(F32)
-        got = jnp.dot(piece, level, preferred_element_type=F32)
-        weights = got if weights is None else weights + got
-    w_ref[:NM, :] = weights
 
     def square(x):
         return x[:, :128] * x[:, :128] + x[:, 128:] * x[:, 128:]
@@ -219,23 +235,24 @@
 
         def body(step, carry):
             rows = pl.ds(pl.multiple_of(step * STEP, STEP), STEP)
-            plus = minus = None
-            for mode in range(NM):
-                cols = slice(mode * 256, (mode + 1) * 256)
-                one = jnp.dot(ph_ref[rows, :256], g_ref[:256, cols], preferred_element_type=F32)
-                two = jnp.dot(ph_ref[rows, 256:], g_ref[256:512, cols], preferred_element_type=F32)
-                if full:
-                    three = jnp.dot(ph3_ref[rows, :], g_ref[512:, cols], preferred_element_type=F32)
-                    three = jnp.where(third, three, 0.0)
-                    sums, differences = one + two + three, one + sign * two - three
-                else:
-                    sums, differences = one + two, one - two
-                weight = w_ref[mode : mode + 1, :]
-                up, down = square(sums) * weight, square(differences) * weight
-                plus = up if plus is None else plus + up
-                minus = down if minus is None else minus + down
-            s_ref[0, rows, :] = plus
-            s_ref[1, rows, :] = minus
+            for group in range(2):
+                plus = minus = None
+                for mode in range(NM):
+                    cols = slice(mode * 256, (mode + 1) * 256)
+                    one = jnp.dot(ph_ref[rows, :256], g_ref[group, :256, cols], preferred_element_type=F32)
+                    two = jnp.dot(ph_ref[rows, 256:], g_ref[group, 256:512, cols], preferred_element_type=F32)
+                    if full:
+                        three = jnp.dot(ph3_ref[rows, :], g_ref[group, 512:, cols], preferred_element_type=F32)
+                        three = jnp.where(third, three, 0.0)
+                        sums, differences = one + two + three, one + sign * two - three
+                    else:
+                        sums, differences = one + two, one - two
+                    weight = w_ref[group, mode : mode + 1, :]
+                    up, down = square(sums) * weight, square(differences) * weight
+                    plus = up if plus is None else plus + up
+                    minus = down if minus is None else minus + down
+                s_ref[0, rows, group * 128 : (group + 1) * 128] = plus
+                s_ref[1, rows, group * 128 : (group + 1) * 128] = minus
             return carry
 
         lax.fori_loop(0, POINTS // STEP, body, 0)
@@ -247,29 +264,29 @@
 def strengths(table, lattice, pays, phases, phases3):
     return pl.pallas_call(
         strength_kernel,
-        in_specs=[vmem()] * 8,
+        in_specs=[vmem()] * 12,
         out_specs=[vmem()] * 2,
-        out_shape=[jax.ShapeDtypeStruct((2, POINTS, 128), F32), jax.ShapeDtypeStruct((8, 128), jnp.int32)],
+        out_shape=[jax.ShapeDtypeStruct((2, POINTS, 256), F32), jax.ShapeDtypeStruct((2, 8, 128), jnp.int32)],
         scratch_shapes=[
-            pltpu.VMEM((2, NM * 128, RW), BF16),
-            pltpu.VMEM((768, 2 * NM * 128), BF16),
-            pltpu.VMEM((8, 128), F32),
+            pltpu.VMEM((2, 2, NM * 128, RW), BF16),
+            pltpu.VMEM((2, 768, 2 * NM * 128), BF16),
+            pltpu.VMEM((2, 8, 128), F32),
+            pltpu.VMEM((8, RW), jnp.int32),
         ],
         compiler_params=pltpu.CompilerParams(vmem_limit_bytes=VMEM_LIMIT),
-        cost_estimate=pl.CostEstimate(flops=4_000_000_000, bytes_accessed=6_000_000, transcendentals=0),
+        cost_estimate=pl.CostEstimate(flops=1_000_000_000, bytes_accessed=1000, transcendentals=0),
         name="strengths",
     )(table, lattice, *pays, phases, phases3)
 
 
-def final_kernel(where_ref, off_a_ref, off_b_ref, own, *refs):
+def final_kernel(where_ref, offsets_ref, own, *refs):
     parts = refs[: 2 * PARTS]
-    sa_ref, sb_ref, out_ref, v_ref, arr_ref, off_ref, sem = refs[2 * PARTS :]
+    s_ref, out_ref, v_ref, arr_ref, off_ref, sem = refs[2 * PARTS :]
     slab = where_ref[0]
     core = where_ref[1]
     share = where_ref[2]
     copies = [
-        pltpu.make_async_copy(off_a_ref, off_ref.at[0], sem.at[0]),
-        pltpu.make_async_copy(off_b_ref, off_ref.at[1], sem.at[1]),
+        pltpu.make_async_copy(offsets_ref, off_ref, sem.at[0]),
     ]
 
     def bring(src, plane, count):
@@ -306,12 +323,12 @@
             qx = off_ref[slot // QG, 1, base]
             qy = off_ref[slot // QG, 1, base + 1]
             qz = off_ref[slot // QG, 1, base + 2]
-            plane = lax.rem(slab * PLANES + step + qz, KZ)
-            first = lax.rem(share * ROWS + qx, KX) * KY
+            plane = wrap(slab * PLANES + step + qz, KZ)
+            first = wrap(share * ROWS + qx, KX) * KY
             start = first + qy + (FRONT - KY)
             aligned = pl.multiple_of((start >> 7) * 128, 128)
             window = v_ref[plane, :, pl.ds(aligned, WIN)].astype(F32)
-            late = pltpu.roll(window, lax.rem(WIN - (start - aligned), WIN), 1)
+            late = pltpu.roll(window, wrap(WIN - (start - aligned), WIN), 1)
             early = pltpu.roll(late, WIN - KY, 1)
             arr_ref[lane, NB * slot : NB * (slot + 1), :] = jnp.where(ky + qy < KY, early[:, :512], late[:, :512])
         window = v_ref[slab * PLANES + step, :, pl.ds(home, WIN)].astype(F32)
@@ -325,7 +342,8 @@
             for upper in range(2):
                 rows = pl.ds(pl.multiple_of((step * ROWS + kx) * HALF, HALF), HALF)
                 here = slice((2 * kx + upper) * HALF, (2 * kx + upper + 1) * HALF)
-                terms.append(sa_ref[upper, rows, :] * diff[here, :128] + sb_ref[upper, rows, :] * diff[here, 128:])
+                product = s_ref[upper, rows, :] * diff[here]
+                terms.append(product[:, :128] + product[:, 128:])
         term = jnp.concatenate(terms, axis=0)
         result = None
         for _ in range(3):
@@ -345,10 +363,10 @@
     lax.fori_loop(0, PLANES // UNROLL, body, 0)
 
 
-def contract(where, off_a, off_b, own, parts, s_a, s_b):
+def contract(where, offsets, own, parts, strength):
     return pl.pallas_call(
         final_kernel,
-        in_specs=[smem()] + [anywhere()] * (3 + 2 * PARTS) + [vmem()] * 2,
+        in_specs=[smem()] + [anywhere()] * (2 + 2 * PARTS) + [vmem()],
         out_specs=vmem(),
         out_shape=jax.ShapeDtypeStruct((PLANES, NB, SHARE), F32),
         scratch_shapes=[
@@ -360,14 +378,13 @@
         compiler_params=pltpu.CompilerParams(vmem_limit_bytes=VMEM_LIMIT),
         cost_estimate=pl.CostEstimate(flops=2_000_000_000, bytes_accessed=9_000_000, transcendentals=0),
         name="contract",
-    )(where, off_a, off_b, own, *parts, s_a, s_b)
+    )(where, offsets, own, *parts, strength)
 
 
 def local(occupation, q_offsets, coupling, window_bins, lorentz_table, lattice):
     slab = lax.axis_index("ka")
     share = lax.axis_index("pb")
     core = share % 2
-    vectors = jnp.pad(lattice, ((0, 5), (0, RW - NR)))
 
     def place(ylo, x, z, yhi, c):
         return ((ylo * 4 + x) * 16) + z * 4 + yhi * 2 + c
@@ -380,25 +397,29 @@
         return move(array, lambda yl, x, z, yh, c: (yl, x, z, yh, 1 - c))
 
     pay = pack(q_offsets, window_bins, jnp.swapaxes(coupling[0], 1, 2))
-    pair = jnp.concatenate([pay, move(pay, lambda yl, x, z, yh, c: (1 - yl, x, z, 1 - yh, c))], axis=0)
+    half, pay = lax.optimization_barrier((lax.dynamic_slice_in_dim(occupation, core * HP, HP, 0)[None], pay))
+    along = [move(half, lambda yl, x, z, yh, c: (yl, (x + d) % 4, z, yh, c)) for d in (1, 3, 2)]
+    twin = move(pay, lambda yl, x, z, yh, c: (1 - yl, x, z, 1 - yh, c))
+    ylo, x = slab // 4, slab % 4
+    lines = [(ylo, 1), (ylo, 3), (ylo, 2), (1 - ylo, 0), (1 - ylo, 1), (1 - ylo, 3), (1 - ylo, 2)]
+    sources = [y * 4 + (x + 4 - d) % 4 for y, d in lines]
+    where = jnp.stack([slab, core, share] + sources).astype(jnp.int32)
+    pair = jnp.concatenate([pay, twin], axis=0)
+    pair, where = lax.optimization_barrier((pair, where))
+    phases, phases3 = make_phases(where, lattice)
     group = [pair] + [move(pair, lambda yl, x, z, yh, c: (yl, x, (z + d) % 4, yh, c)) for d in (1, 3, 2)]
     other = [core_swap(array) for array in group]
-    half = lax.dynamic_slice_in_dim(occupation, core * HP, HP, 0)[None]
-    beyond = move(half, lambda yl, x, z, yh, c: (1 - yl, x, z, yh, c))
-    both = jnp.concatenate([half, beyond], axis=0)
-    fetched = [beyond] + [move(both, lambda yl, x, z, yh, c: (yl, (x + d) % 4, z, yh, c)) for d in (1, 3, 2)]
+    near_in = jnp.concatenate([half, along[0]], axis=0)
+    far_in = jnp.concatenate(along[1:], axis=0)
+    near_in, far_in, phases = lax.optimization_barrier((near_in, far_in, phases))
+    near = move(near_in, lambda yl, x, z, yh, c: (1 - yl, x, z, yh, c))
+    far = move(far_in, lambda yl, x, z, yh, c: (1 - yl, x, z, 1 - yh, c))
+    table = lorentz_table.T
+    strength, offsets = strengths(table, lattice, group + other, phases, phases3)
+    near, far, strength = lax.optimization_barrier((near, far, strength))
+    fetched = along + [near, far]
     swapped = [core_swap(array) for array in fetched]
-    ylo, x = slab // 4, slab % 4
-    sources = [(1 - ylo) * 4 + x]
-    for d in (1, 3, 2):
-        sources += [ylo * 4 + (x + 4 - d) % 4, (1 - ylo) * 4 + (x + 4 - d) % 4]
-    where = jnp.stack([slab, core, share] + sources).astype(jnp.int32)
-
-    phases, phases3 = make_phases(where, vectors)
-    table = lorentz_table.T
-    s_a, off_a = strengths(table, vectors, group, phases, phases3)
-    s_b, off_b = strengths(table, vectors, other, phases, phases3)
-    return contract(where, off_a, off_b, occupation, fetched + swapped, s_a, s_b)
+    return contract(where, offsets, occupation, fetched + swapped, strength)
 
 
 def solution(mesh):

time: 59.5 us -> 52.8 us (0.89)
  starting transfers between devices: 28.7 us -> 21.6 us
  waiting for transfers between devices: 5.93 us -> 8.13 us
  Pallas kernels: 21.2 us -> 19.1 us
  local copies, waits for them, and re-layouts: 1.16 us -> 1.82 us
    ppermute x16 -> x18, starting transfers between devices: 28.7 us -> 21.6 us  [move(): lax.ppermute(array, ('ka', 'pb'), [(place(*at), place(*to(*at))) for at i...]
    ppermute x16 -> x18, waiting for transfers between devices: 5.93 us -> 8.13 us  [move(): lax.ppermute(array, ('ka', 'pb'), [(place(*at), place(*to(*at))) for at i...]
    pallas_call x3 -> x2, Pallas kernels: 17.8 us -> 15.8 us  [the longest x1 8.79 us: strengths(): pl.pallas_call(strength_kernel, in_specs=[vmem()] * 12, out_specs=[vmem()...]
    unnamed x6 -> x8, local copies, waits for them, and re-layouts: 0.01 us -> 0.7 us
    concatenate x2 -> x3, other arithmetic: 2.07 us -> 1.64 us  [the longest x1 0.91 us: local(): pair = jnp.concatenate([pay, twin], axis=0)]
  transfers between devices with their start and end apart: 16 -> 18, of which waited for: 2 -> 8; matrix products, arithmetic and copies ran while one was open for 4% -> 3% of each run, Pallas kernels for 22% -> 20%
where the time goes in v3:
time: 52.8 us; the launch traced here: 52.6 us
  starting transfers between devices  21.6 us (41%)
  Pallas kernels  19.1 us (36%)
  waiting for transfers between devices  8.13 us (15%)
  local copies, waits for them, and re-layouts  1.82 us (3%)
  other arithmetic  1.64 us (3%)
    ppermute x18, starting transfers between devices, move(): lax.ppermute(array, ('ka', 'pb'), [(place(*at), place(*to(*at))) for at i...  21.6 us
    pallas_call x1, Pallas kernels, strengths(): pl.pallas_call(strength_kernel, in_specs=[vmem()] * 12, out_specs=[vmem()...  8.79 us
    ppermute x18, waiting for transfers between devices, move(): lax.ppermute(array, ('ka', 'pb'), [(place(*at), place(*to(*at))) for at i...  8.13 us
    pallas_call x1, Pallas kernels, contract(): pl.pallas_call(final_kernel, in_specs=[smem()] + [anywhere()] * (2 + 2 *...  7 us
    pallas_call x1, Pallas kernels, pack(): pl.pallas_call(pack_kernel, in_specs=[smem(), smem(), vmem()], out_specs=...  1.7 us
    pallas_call x1, Pallas kernels, make_phases(): pl.pallas_call(phase_kernel, in_specs=[smem(), vmem()], out_specs=[vmem()...  1.64 us
  transfers between devices with their start and end apart: 18, of which 8 were waited for; matrix products, arithmetic and copies ran while one was open for 3% of the time, Pallas kernels for 20%

profile of v3, /device:TPU:1, one launch (start us, length us, event | category | flops | bytes accessed | tf_op | source)
XLA Modules:
  0.0 52.6 jit_solution(13900966853964826864)
XLA Ops:
  0.0 1.0 %dynamic-slice_bitcast_fusion = bf16[1,5,4,6400]{3,2,1,0:T(4,128)(2,1)S(1)} fusion(bf16[10,4,6400]{2,1,0:T(4,128)(2,1)} %own.1, s32[]{:T(128)S(6)} %select_n.41), kind=kLoop, calls=%fused_computation.2 | loop fusion | bytes 512004 | tf_op jit(solution)/shard_map/broadcast_in_dim | solution.py:400
  1.0 1.7 %pack.1 = bf16[208,256]{1,0:T(8,128)(2,1)} custom-call(s32[1,3]{1,0:T(1,128)} %off_ref.1, s32[1,16]{1,0:T(1,128)} %bins_ref.1, bf16[2,96,200]{2,1,0:T(8,128)(2,1)} %bitcast.17), custom_call_target="tpu_custom_call" | custom-call | tf_op jit(solution)/shard_map/pack/pallas_call | solution.py:80
  2.7 3.6 %collective-permute-start = (bf16[208,256]{1,0:T(8,128)(2,1)}, bf16[208,256]{1,0:T(8,128)(2,1)S(1)}, u32[]{:S(2)}, u32[]{:S(2)}) collective-permute-start(bf16[208,256]{1,0:T(8,128)(2,1)} %pack.1), channel_id=1, source_target_pairs={{0,66},{1,67},{2,64},{3,65},{4,70},{5,71},{6,68},{7,69},{8,74},{9,... | collective-permute-start | bytes 319496 | tf_op jit(solution)/shard_map/ppermute | solution.py:394
  6.3 2.7 %collective-permute-start.10 = (bf16[1,5,4,6400]{3,2,1,0:T(4,128)(2,1)S(1)}, bf16[1,5,4,6400]{3,2,1,0:T(4,128)(2,1)S(1)}, u32[]{:S(2)}, u32[]{:S(2)}) collective-permute-start(bf16[1,5,4,6400]{3,2,1,0:T(4,128)(2,1)S(1)} %dynamic-slice_bitcast_fusion), channel_id=1, source_target_pairs={{0,32},{1,33},{2,34},{3,35},{4,36},{5,37},{6,38},{7,39},{8,40},{9,... | collective-permute-start | bytes 768008 | tf_op jit(solution)/shard_map/ppermute | solution.py:394
  9.1 0.9 %collective-permute-start.9 = (bf16[1,5,4,6400]{3,2,1,0:T(4,128)(2,1)S(1)}, bf16[1,5,4,6400]{3,2,1,0:T(4,128)(2,1)S(1)}, u32[]{:S(2)}, u32[]{:S(2)}) collective-permute-start(bf16[1,5,4,6400]{3,2,1,0:T(4,128)(2,1)S(1)} %dynamic-slice_bitcast_fusion), channel_id=1, source_target_pairs={{0,48},{1,49},{2,50},{3,51},{4,52},{5,53},{6,54},{7,55},{8,56},{9,... | collective-permute-start | bytes 768008 | tf_op jit(solution)/shard_map/ppermute | solution.py:394
  9.9 0.6 %collective-permute-start.8 = (bf16[1,5,4,6400]{3,2,1,0:T(4,128)(2,1)S(1)}, bf16[1,5,4,6400]{3,2,1,0:T(4,128)(2,1)S(1)}, u32[]{:S(2)}, u32[]{:S(2)}) collective-permute-start(bf16[1,5,4,6400]{3,2,1,0:T(4,128)(2,1)S(1)} %dynamic-slice_bitcast_fusion), channel_id=1, source_target_pairs={{0,16},{1,17},{2,18},{3,19},{4,20},{5,21},{6,22},{7,23},{8,24},{9,... | collective-permute-start | bytes 768008 | tf_op jit(solution)/shard_map/ppermute | solution.py:394
  10.5 0.0 copy-start.1
  10.5 0.0 copy-start.3
  10.5 0.1 stack.43.where_ref
  10.6 0.0 collective-permute-done
  10.6 0.9 %pad_maximum_fusion.2.refs_0_ = bf16[416,256]{1,0:T(8,128)(2,1)S(1)} fusion(bf16[208,256]{1,0:T(8,128)(2,1)S(1)} %collective-permute-done, bf16[208,256]{1,0:T(8,128)(2,1)} %pack.1), kind=kLoop, calls=%fused_computation.3 | loop fusion | flops 425984 | bytes 425984 | tf_op jit(solution)/shard_map/concatenate | solution.py:407
  11.5 1.7 %collective-permute-start.1 = (bf16[416,256]{1,0:T(8,128)(2,1)S(1)}, bf16[416,256]{1,0:T(8,128)(2,1)S(1)}, u32[]{:S(2)}, u32[]{:S(2)}) collective-permute-start(bf16[416,256]{1,0:T(8,128)(2,1)S(1)} %pad_maximum_fusion.2.refs_0_), channel_id=1, source_target_pairs={{0,4},{1,5},{2,6},{3,7},{4,8},{5,9},{6,10},{7,11},{8,12},{9,13},{1... | collective-permute-start | bytes 638984 | tf_op jit(solution)/shard_map/ppermute | solution.py:394
  13.2 2.2 %collective-permute-start.2 = (bf16[416,256]{1,0:T(8,128)(2,1)S(1)}, bf16[416,256]{1,0:T(8,128)(2,1)S(1)}, u32[]{:S(2)}, u32[]{:S(2)}) collective-permute-start(bf16[416,256]{1,0:T(8,128)(2,1)S(1)} %pad_maximum_fusion.2.refs_0_), channel_id=1, source_target_pairs={{0,12},{1,13},{2,14},{3,15},{4,0},{5,1},{6,2},{7,3},{8,4},{9,5},{1... | collective-permute-start | bytes 638984 | tf_op jit(solution)/shard_map/ppermute | solution.py:394
  15.4 0.0 copy-start.2
  15.4 0.7 %copy-done.2 = s32[3,200]{1,0:T(4,128)S(1)} copy-done((s32[3,200]{1,0:T(4,128)S(1)}, s32[3,200]{1,0:T(4,128)}, u32[]{:S(2)}) %copy-start.2) | copy-done | bytes 2424
  16.1 1.6 %phases.1 = (bf16[2000,512]{1,0:T(8,128)(2,1)S(1)}, bf16[2000,256]{1,0:T(8,128)(2,1)S(1)}) custom-call(s32[10]{0:T(128)S(1)} %stack.43.where_ref, s32[3,200]{1,0:T(4,128)S(1)} %copy-done.2), custom_call_target="tpu_custom_call" | custom-call | flops 1500000000 | bytes 3000000 | tf_op jit(solution)/shard_map/phases/pallas_call | solution.py:166
  17.8 0.0 copy-start
  17.8 3.0 %collective-permute-done.8.refs_0_ = bf16[1,5,4,6400]{3,2,1,0:T(4,128)(2,1)S(1)} collective-permute-done((bf16[1,5,4,6400]{3,2,1,0:T(4,128)(2,1)S(1)}, bf16[1,5,4,6400]{3,2,1,0:T(4,128)(2,1)S(1)}, u32[]{:S(2)}, u32[]{:S(2)}) %collective-permute-start.8) | collective-permute-done | bytes 256032 | tf_op jit(solution)/shard_map/ppermute | solution.py:394
  20.8 3.6 %collective-permute-start.3 = (bf16[416,256]{1,0:T(8,128)(2,1)S(1)}, bf16[416,256]{1,0:T(8,128)(2,1)S(1)}, u32[]{:S(2)}, u32[]{:S(2)}) collective-permute-start(bf16[416,256]{1,0:T(8,128)(2,1)S(1)} %pad_maximum_fusion.2.refs_0_), channel_id=1, source_target_pairs={{0,8},{1,9},{2,10},{3,11},{4,12},{5,13},{6,14},{7,15},{8,0},{9,1},... | collective-permute-start | bytes 638984 | tf_op jit(solution)/shard_map/ppermute | solution.py:394
  24.4 0.4 pad_maximum_fusion
  24.8 0.0 collective-permute-done.10.refs_2_
  24.8 1.5 %collective-permute-start.4 = (bf16[416,256]{1,0:T(8,128)(2,1)S(1)}, bf16[416,256]{1,0:T(8,128)(2,1)S(1)}, u32[]{:S(2)}, u32[]{:S(2)}) collective-permute-start(bf16[416,256]{1,0:T(8,128)(2,1)S(1)} %pad_maximum_fusion.2.refs_0_), channel_id=1, source_target_pairs={{0,1},{1,0},{2,3},{3,2},{4,5},{5,4},{6,7},{7,6},{8,9},{9,8},{10,11... | collective-permute-start | bytes 638984 | tf_op jit(solution)/shard_map/ppermute | solution.py:394
  26.2 0.0 collective-permute-done.9.refs_1_
  26.2 0.4 pad_maximum_fusion.1
  26.6 0.1 collective-permute-start.11
  26.7 0.0 collective-permute-done.1.refs_1_
  26.7 0.6 %collective-permute-start.12 = (bf16[2,5,4,6400]{3,2,1,0:T(4,128)(2,1)S(1)}, bf16[2,5,4,6400]{3,2,1,0:T(4,128)(2,1)S(1)}, u32[]{:S(2)}, u32[]{:S(2)}) collective-permute-start(bf16[2,5,4,6400]{3,2,1,0:T(4,128)(2,1)S(1)} %pad_maximum_fusion.1), channel_id=1, source_target_pairs={{0,66},{1,67},{2,64},{3,65},{4,70},{5,71},{6,68},{7,69},{8,74},{9,... | collective-permute-start | bytes 1536008 | tf_op jit(solution)/shard_map/ppermute | solution.py:394
  27.3 0.0 collective-permute-done.2.refs_2_
  27.3 0.6 %collective-permute-start.5 = (bf16[416,256]{1,0:T(8,128)(2,1)S(1)}, bf16[416,256]{1,0:T(8,128)(2,1)S(1)}, u32[]{:S(2)}, u32[]{:S(2)}) collective-permute-start(bf16[416,256]{1,0:T(8,128)(2,1)S(1)} %collective-permute-done.1.refs_1_), channel_id=1, source_target_pairs={{0,1},{1,0},{2,3},{3,2},{4,5},{5,4},{6,7},{7,6},{8,9},{9,8},{10,11... | collective-permute-start | bytes 638984 | tf_op jit(solution)/shard_map/ppermute | solution.py:394
  27.9 1.0 %collective-permute-done.3.refs_3_ = bf16[416,256]{1,0:T(8,128)(2,1)S(1)} collective-permute-done((bf16[416,256]{1,0:T(8,128)(2,1)S(1)}, bf16[416,256]{1,0:T(8,128)(2,1)S(1)}, u32[]{:S(2)}, u32[]{:S(2)}) %collective-permute-start.3) | collective-permute-done | bytes 213024 | tf_op jit(solution)/shard_map/ppermute | solution.py:394
  28.9 1.7 %collective-permute-start.6 = (bf16[416,256]{1,0:T(8,128)(2,1)S(1)}, bf16[416,256]{1,0:T(8,128)(2,1)S(1)}, u32[]{:S(2)}, u32[]{:S(2)}) collective-permute-start(bf16[416,256]{1,0:T(8,128)(2,1)S(1)} %collective-permute-done.2.refs_2_), channel_id=1, source_target_pairs={{0,1},{1,0},{2,3},{3,2},{4,5},{5,4},{6,7},{7,6},{8,9},{9,8},{10,11... | collective-permute-start | bytes 638984 | tf_op jit(solution)/shard_map/ppermute | solution.py:394
  30.6 0.0 collective-permute-done.4.refs_4_
  30.6 0.0 collective-permute-start.7
  30.6 0.0 collective-permute-done.5.refs_5_
  30.6 1.1 %collective-permute-done.6.refs_6_ = bf16[416,256]{1,0:T(8,128)(2,1)S(1)} collective-permute-done((bf16[416,256]{1,0:T(8,128)(2,1)S(1)}, bf16[416,256]{1,0:T(8,128)(2,1)S(1)}, u32[]{:S(2)}, u32[]{:S(2)}) %collective-permute-start.6) | collective-permute-done | bytes 213024 | tf_op jit(solution)/shard_map/ppermute | solution.py:394
  31.7 0.4 collective-permute-done.7.refs_7_
  32.1 0.0 copy-done.1
  32.1 0.0 copy-done.3
  32.1 8.8 %strengths.1 = (f32[2,2000,256]{2,1,0:T(8,128)S(1)}, s32[2,8,128]{2,1,0:T(8,128)S(1)}) custom-call(f32[6,32]{1,0:T(8,128)S(1)} %bitcast.16, s32[3,200]{1,0:T(4,128)S(1)} %copy-done.3, bf16[416,256]{1,0:T(8,128)(2,1)S(1)} %pad_maximum_fusion.2.refs_0_, bf16[416,256]{1,0:T(8,128)(2,1)S(1)} %collective-permute-done.1.refs_1_, ...), custom_call_target="tpu_custom_call" | custom-call | flops 1000000000 | bytes 1000 | tf_op jit(solution)/shard_map/strengths/pallas_call | solution.py:265
  40.9 0.0 collective-permute-done.11.refs_3_
  40.9 0.3 collective-permute-done.12.refs_4_
  41.2 0.8 %collective-permute-start.16 = (bf16[2,5,4,6400]{3,2,1,0:T(4,128)(2,1)S(1)}, bf16[2,5,4,6400]{3,2,1,0:T(4,128)(2,1)S(1)}, u32[]{:S(2)}, u32[]{:S(2)}) collective-permute-start(bf16[2,5,4,6400]{3,2,1,0:T(4,128)(2,1)S(1)} %collective-permute-done.11.refs_3_), channel_id=1, source_target_pairs={{0,1},{1,0},{2,3},{3,2},{4,5},{5,4},{6,7},{7,6},{8,9},{9,8},{10,11... | collective-permute-start | bytes 1536008 | tf_op jit(solution)/shard_map/ppermute | solution.py:394
  42.1 0.0 collective-permute-start.17
  42.1 0.5 collective-permute-start.13
  42.6 0.0 collective-permute-start.14
  42.6 0.5 collective-permute-start.15
  43.1 1.6 %collective-permute-done.13.refs_5_ = bf16[1,5,4,6400]{3,2,1,0:T(4,128)(2,1)S(1)} collective-permute-done((bf16[1,5,4,6400]{3,2,1,0:T(4,128)(2,1)S(1)}, bf16[1,5,4,6400]{3,2,1,0:T(4,128)(2,1)S(1)}, u32[]{:S(2)}, u32[]{:S(2)}) %collective-permute-start.13) | collective-permute-done | bytes 256032 | tf_op jit(solution)/shard_map/ppermute | solution.py:394
  44.7 0.4 collective-permute-done.14.refs_6_
  45.0 0.4 collective-permute-done.15.refs_7_
  45.4 0.0 collective-permute-done.16.refs_8_
  45.4 0.0 collective-permute-done.17.refs_9_
  45.4 0.0 copy-done
  45.4 7.0 %contract.1 = f32[10,4,400]{2,1,0:T(4,128)} custom-call(s32[10]{0:T(128)S(1)} %stack.43.where_ref, s32[2,8,128]{2,1,0:T(8,128)S(1)} %get-tuple-element.26.offsets_ref, bf16[10,4,6400]{2,1,0:T(4,128)(2,1)S(1)} %copy-done, bf16[1,5,4,6400]{3,2,1,0:T(4,128)(2,1)S(1)} %collective-permute-done.8.refs_0_, ...), custom_call_target="tpu_custom_call" | custom-call | flops 2000000000 | bytes 9000000 | tf_op jit(solution)/shard_map/contract/pallas_call | solution.py:367
Async XLA Ops:
  2.7 7.9 %collective-permute-start = (bf16[208,256]{1,0:T(8,128)(2,1)}, bf16[208,256]{1,0:T(8,128)(2,1)S(1)}, u32[]{:S(2)}, u32[]{:S(2)}) collective-permute-start(bf16[208,256]{1,0:T(8,128)(2,1)} %pack.1), channel_id=1, source_target_pairs={{0,66},{1,67},{2,64},{3,65},{4,70},{5,71},{6,68},{7,69},{8,74},{9,... | collective-permute-start | bytes 319496 | tf_op jit(solution)/shard_map/ppermute | solution.py:394
  6.3 18.4 %collective-permute-start.10 = (bf16[1,5,4,6400]{3,2,1,0:T(4,128)(2,1)S(1)}, bf16[1,5,4,6400]{3,2,1,0:T(4,128)(2,1)S(1)}, u32[]{:S(2)}, u32[]{:S(2)}) collective-permute-start(bf16[1,5,4,6400]{3,2,1,0:T(4,128)(2,1)S(1)} %dynamic-slice_bitcast_fusion), channel_id=1, source_target_pairs={{0,32},{1,33},{2,34},{3,35},{4,36},{5,37},{6,38},{7,39},{8,40},{9,... | collective-permute-start | bytes 768008 | tf_op jit(solution)/shard_map/ppermute | solution.py:394
  9.1 17.2 %collective-permute-start.9 = (bf16[1,5,4,6400]{3,2,1,0:T(4,128)(2,1)S(1)}, bf16[1,5,4,6400]{3,2,1,0:T(4,128)(2,1)S(1)}, u32[]{:S(2)}, u32[]{:S(2)}) collective-permute-start(bf16[1,5,4,6400]{3,2,1,0:T(4,128)(2,1)S(1)} %dynamic-slice_bitcast_fusion), channel_id=1, source_target_pairs={{0,48},{1,49},{2,50},{3,51},{4,52},{5,53},{6,54},{7,55},{8,56},{9,... | collective-permute-start | bytes 768008 | tf_op jit(solution)/shard_map/ppermute | solution.py:394
  9.9 10.9 %collective-permute-start.8 = (bf16[1,5,4,6400]{3,2,1,0:T(4,128)(2,1)S(1)}, bf16[1,5,4,6400]{3,2,1,0:T(4,128)(2,1)S(1)}, u32[]{:S(2)}, u32[]{:S(2)}) collective-permute-start(bf16[1,5,4,6400]{3,2,1,0:T(4,128)(2,1)S(1)} %dynamic-slice_bitcast_fusion), channel_id=1, source_target_pairs={{0,16},{1,17},{2,18},{3,19},{4,20},{5,21},{6,22},{7,23},{8,24},{9,... | collective-permute-start | bytes 768008 | tf_op jit(solution)/shard_map/ppermute | solution.py:394
  10.5 21.5 %copy-start.1 = (f32[32,6]{0,1:T(8,128)S(1)}, f32[32,6]{0,1:T(8,128)}, u32[]{:S(2)}) copy-start(f32[32,6]{0,1:T(8,128)} %param.10) | copy-start | bytes 2308
  10.5 21.5 %copy-start.3 = (s32[3,200]{1,0:T(4,128)S(1)}, s32[3,200]{1,0:T(4,128)}, u32[]{:S(2)}) copy-start(s32[3,200]{1,0:T(4,128)} %lattice_ref.3) | copy-start | bytes 7204
  11.5 15.2 %collective-permute-start.1 = (bf16[416,256]{1,0:T(8,128)(2,1)S(1)}, bf16[416,256]{1,0:T(8,128)(2,1)S(1)}, u32[]{:S(2)}, u32[]{:S(2)}) collective-permute-start(bf16[416,256]{1,0:T(8,128)(2,1)S(1)} %pad_maximum_fusion.2.refs_0_), channel_id=1, source_target_pairs={{0,4},{1,5},{2,6},{3,7},{4,8},{5,9},{6,10},{7,11},{8,12},{9,13},{1... | collective-permute-start | bytes 638984 | tf_op jit(solution)/shard_map/ppermute | solution.py:394
  13.2 14.1 %collective-permute-start.2 = (bf16[416,256]{1,0:T(8,128)(2,1)S(1)}, bf16[416,256]{1,0:T(8,128)(2,1)S(1)}, u32[]{:S(2)}, u32[]{:S(2)}) collective-permute-start(bf16[416,256]{1,0:T(8,128)(2,1)S(1)} %pad_maximum_fusion.2.refs_0_), channel_id=1, source_target_pairs={{0,12},{1,13},{2,14},{3,15},{4,0},{5,1},{6,2},{7,3},{8,4},{9,5},{1... | collective-permute-start | bytes 638984 | tf_op jit(solution)/shard_map/ppermute | solution.py:394
  15.4 0.7 %copy-start.2 = (s32[3,200]{1,0:T(4,128)S(1)}, s32[3,200]{1,0:T(4,128)}, u32[]{:S(2)}) copy-start(s32[3,200]{1,0:T(4,128)} %lattice_ref.3) | copy-start | bytes 7204
  17.8 27.6 %copy-start = (bf16[10,4,6400]{2,1,0:T(4,128)(2,1)S(1)}, bf16[10,4,6400]{2,1,0:T(4,128)(2,1)}, u32[]{:S(2)}) copy-start(bf16[10,4,6400]{2,1,0:T(4,128)(2,1)} %own.1) | copy-start | bytes 1536004
  20.8 8.1 %collective-permute-start.3 = (bf16[416,256]{1,0:T(8,128)(2,1)S(1)}, bf16[416,256]{1,0:T(8,128)(2,1)S(1)}, u32[]{:S(2)}, u32[]{:S(2)}) collective-permute-start(bf16[416,256]{1,0:T(8,128)(2,1)S(1)} %pad_maximum_fusion.2.refs_0_), channel_id=1, source_target_pairs={{0,8},{1,9},{2,10},{3,11},{4,12},{5,13},{6,14},{7,15},{8,0},{9,1},... | collective-permute-start | bytes 638984 | tf_op jit(solution)/shard_map/ppermute | solution.py:394
  24.8 5.8 %collective-permute-start.4 = (bf16[416,256]{1,0:T(8,128)(2,1)S(1)}, bf16[416,256]{1,0:T(8,128)(2,1)S(1)}, u32[]{:S(2)}, u32[]{:S(2)}) collective-permute-start(bf16[416,256]{1,0:T(8,128)(2,1)S(1)} %pad_maximum_fusion.2.refs_0_), channel_id=1, source_target_pairs={{0,1},{1,0},{2,3},{3,2},{4,5},{5,4},{6,7},{7,6},{8,9},{9,8},{10,11... | collective-permute-start | bytes 638984 | tf_op jit(solution)/shard_map/ppermute | solution.py:394
  26.6 14.3 %collective-permute-start.11 = (bf16[2,5,4,6400]{3,2,1,0:T(4,128)(2,1)S(1)}, bf16[2,5,4,6400]{3,2,1,0:T(4,128)(2,1)S(1)}, u32[]{:S(2)}, u32[]{:S(2)}) collective-permute-start(bf16[2,5,4,6400]{3,2,1,0:T(4,128)(2,1)S(1)} %pad_maximum_fusion), channel_id=1, source_target_pairs={{0,64},{1,65},{2,66},{3,67},{4,68},{5,69},{6,70},{7,71},{8,72},{9,... | collective-permute-start | bytes 1536008 | tf_op jit(solution)/shard_map/ppermute | solution.py:394
  26.7 14.5 %collective-permute-start.12 = (bf16[2,5,4,6400]{3,2,1,0:T(4,128)(2,1)S(1)}, bf16[2,5,4,6400]{3,2,1,0:T(4,128)(2,1)S(1)}, u32[]{:S(2)}, u32[]{:S(2)}) collective-permute-start(bf16[2,5,4,6400]{3,2,1,0:T(4,128)(2,1)S(1)} %pad_maximum_fusion.1), channel_id=1, source_target_pairs={{0,66},{1,67},{2,64},{3,65},{4,70},{5,71},{6,68},{7,69},{8,74},{9,... | collective-permute-start | bytes 1536008 | tf_op jit(solution)/shard_map/ppermute | solution.py:394
  27.3 3.3 %collective-permute-start.5 = (bf16[416,256]{1,0:T(8,128)(2,1)S(1)}, bf16[416,256]{1,0:T(8,128)(2,1)S(1)}, u32[]{:S(2)}, u32[]{:S(2)}) collective-permute-start(bf16[416,256]{1,0:T(8,128)(2,1)S(1)} %collective-permute-done.1.refs_1_), channel_id=1, source_target_pairs={{0,1},{1,0},{2,3},{3,2},{4,5},{5,4},{6,7},{7,6},{8,9},{9,8},{10,11... | collective-permute-start | bytes 638984 | tf_op jit(solution)/shard_map/ppermute | solution.py:394
  28.9 2.8 %collective-permute-start.6 = (bf16[416,256]{1,0:T(8,128)(2,1)S(1)}, bf16[416,256]{1,0:T(8,128)(2,1)S(1)}, u32[]{:S(2)}, u32[]{:S(2)}) collective-permute-start(bf16[416,256]{1,0:T(8,128)(2,1)S(1)} %collective-permute-done.2.refs_2_), channel_id=1, source_target_pairs={{0,1},{1,0},{2,3},{3,2},{4,5},{5,4},{6,7},{7,6},{8,9},{9,8},{10,11... | collective-permute-start | bytes 638984 | tf_op jit(solution)/shard_map/ppermute | solution.py:394
  30.6 1.5 %collective-permute-start.7 = (bf16[416,256]{1,0:T(8,128)(2,1)S(1)}, bf16[416,256]{1,0:T(8,128)(2,1)S(1)}, u32[]{:S(2)}, u32[]{:S(2)}) collective-permute-start(bf16[416,256]{1,0:T(8,128)(2,1)S(1)} %collective-permute-done.3.refs_3_), channel_id=1, source_target_pairs={{0,1},{1,0},{2,3},{3,2},{4,5},{5,4},{6,7},{7,6},{8,9},{9,8},{10,11... | collective-permute-start | bytes 638984 | tf_op jit(solution)/shard_map/ppermute | solution.py:394
  41.2 4.2 %collective-permute-start.16 = (bf16[2,5,4,6400]{3,2,1,0:T(4,128)(2,1)S(1)}, bf16[2,5,4,6400]{3,2,1,0:T(4,128)(2,1)S(1)}, u32[]{:S(2)}, u32[]{:S(2)}) collective-permute-start(bf16[2,5,4,6400]{3,2,1,0:T(4,128)(2,1)S(1)} %collective-permute-done.11.refs_3_), channel_id=1, source_target_pairs={{0,1},{1,0},{2,3},{3,2},{4,5},{5,4},{6,7},{7,6},{8,9},{9,8},{10,11... | collective-permute-start | bytes 1536008 | tf_op jit(solution)/shard_map/ppermute | solution.py:394
  42.1 3.4 %collective-permute-start.17 = (bf16[2,5,4,6400]{3,2,1,0:T(4,128)(2,1)S(1)}, bf16[2,5,4,6400]{3,2,1,0:T(4,128)(2,1)S(1)}, u32[]{:S(2)}, u32[]{:S(2)}) collective-permute-start(bf16[2,5,4,6400]{3,2,1,0:T(4,128)(2,1)S(1)} %collective-permute-done.12.refs_4_), channel_id=1, source_target_pairs={{0,1},{1,0},{2,3},{3,2},{4,5},{5,4},{6,7},{7,6},{8,9},{9,8},{10,11... | collective-permute-start | bytes 1536008 | tf_op jit(solution)/shard_map/ppermute | solution.py:394
  42.1 2.6 %collective-permute-start.13 = (bf16[1,5,4,6400]{3,2,1,0:T(4,128)(2,1)S(1)}, bf16[1,5,4,6400]{3,2,1,0:T(4,128)(2,1)S(1)}, u32[]{:S(2)}, u32[]{:S(2)}) collective-permute-start(bf16[1,5,4,6400]{3,2,1,0:T(4,128)(2,1)S(1)} %collective-permute-done.8.refs_0_), channel_id=1, source_target_pairs={{0,1},{1,0},{2,3},{3,2},{4,5},{5,4},{6,7},{7,6},{8,9},{9,8},{10,11... | collective-permute-start | bytes 768008 | tf_op jit(solution)/shard_map/ppermute | solution.py:394
  42.6 2.5 %collective-permute-start.14 = (bf16[1,5,4,6400]{3,2,1,0:T(4,128)(2,1)S(1)}, bf16[1,5,4,6400]{3,2,1,0:T(4,128)(2,1)S(1)}, u32[]{:S(2)}, u32[]{:S(2)}) collective-permute-start(bf16[1,5,4,6400]{3,2,1,0:T(4,128)(2,1)S(1)} %collective-permute-done.9.refs_1_), channel_id=1, source_target_pairs={{0,1},{1,0},{2,3},{3,2},{4,5},{5,4},{6,7},{7,6},{8,9},{9,8},{10,11... | collective-permute-start | bytes 768008 | tf_op jit(solution)/shard_map/ppermute | solution.py:394
  42.6 2.8 %collective-permute-start.15 = (bf16[1,5,4,6400]{3,2,1,0:T(4,128)(2,1)S(1)}, bf16[1,5,4,6400]{3,2,1,0:T(4,128)(2,1)S(1)}, u32[]{:S(2)}, u32[]{:S(2)}) collective-permute-start(bf16[1,5,4,6400]{3,2,1,0:T(4,128)(2,1)S(1)} %collective-permute-done.10.refs_2_), channel_id=1, source_target_pairs={{0,1},{1,0},{2,3},{3,2},{4,5},{5,4},{6,7},{7,6},{8,9},{9,8},{10,11... | collective-permute-start | bytes 768008 | tf_op jit(solution)/shard_map/ppermute | solution.py:394

commit v4 on v3

--- a/solution.py
+++ b/solution.py
@@ -1,3 +1,4 @@
+import functools
 import math
 
 import jax
@@ -20,7 +21,7 @@
 PLANES = 10
 HP = PLANES // 2
 PARTS = 5
-WHICH = (0, 1, 2, 3, 5)
+WHICH = (0, 1, 2, 4, 6)
 ROWS = 5
 HALF = KY // 2
 SHARE = ROWS * KY
@@ -31,7 +32,7 @@
 BACK = 512
 VLANES = FRONT + KX * KY + BACK
 WIN = 640
-STEP = 400
+STEP = 1000
 UNROLL = 10
 VMEM_LIMIT = 28 * 1024 * 1024
 F32 = jnp.float32
@@ -175,10 +176,10 @@
     )(where, lattice)
 
 
-def strength_kernel(table_ref, lattice_ref, *refs):
-    pays = refs[:8]
-    ph_ref, ph3_ref, s_ref, off_ref, mixed_ref, g_ref, w_ref, wide_ref = refs[8:]
-    for slot in range(2 * QG):
+def strength_kernel(groups, table_ref, lattice_ref, *refs):
+    pays = refs[: 4 * groups]
+    ph_ref, ph3_ref, s_ref, off_ref, mixed_ref, g_ref, w_ref, wide_ref = refs[4 * groups :]
+    for slot in range(groups * QG):
         ref = pays[slot // 2]
         start = (slot % 2) * PAY
         group, inner = slot // QG, slot % QG
@@ -206,7 +207,7 @@
         span = count * 128
         rows = place[first * 128 : first * 128 + span]
         both = (((1,), (1,)), ((), ()))
-        for group in range(2):
+        for group in range(groups):
             real = lax.dot_general(rows, mixed_ref[group, 0], both, preferred_element_type=F32)
             imag = lax.dot_general(rows, mixed_ref[group, 1], both, preferred_element_type=F32)
             minus = (-imag).astype(BF16)
@@ -235,7 +236,7 @@
 
         def body(step, carry):
             rows = pl.ds(pl.multiple_of(step * STEP, STEP), STEP)
-            for group in range(2):
+            for group in range(groups):
                 plus = minus = None
                 for mode in range(NM):
                     cols = slice(mode * 256, (mode + 1) * 256)
@@ -261,32 +262,37 @@
     pl.when(general)(lambda: run(True))
 
 
-def strengths(table, lattice, pays, phases, phases3):
+def strengths(table, lattice, pays, phases, phases3, cost):
+    groups = len(pays) // 4
     return pl.pallas_call(
-        strength_kernel,
-        in_specs=[vmem()] * 12,
+        functools.partial(strength_kernel, groups),
+        in_specs=[vmem()] * (4 + len(pays)),
         out_specs=[vmem()] * 2,
-        out_shape=[jax.ShapeDtypeStruct((2, POINTS, 256), F32), jax.ShapeDtypeStruct((2, 8, 128), jnp.int32)],
+        out_shape=[
+            jax.ShapeDtypeStruct((2, POINTS, groups * 128), F32),
+            jax.ShapeDtypeStruct((groups, 8, 128), jnp.int32),
+        ],
         scratch_shapes=[
-            pltpu.VMEM((2, 2, NM * 128, RW), BF16),
-            pltpu.VMEM((2, 768, 2 * NM * 128), BF16),
-            pltpu.VMEM((2, 8, 128), F32),
+            pltpu.VMEM((groups, 2, NM * 128, RW), BF16),
+            pltpu.VMEM((groups, 768, 2 * NM * 128), BF16),
+            pltpu.VMEM((groups, 8, 128), F32),
             pltpu.VMEM((8, RW), jnp.int32),
         ],
         compiler_params=pltpu.CompilerParams(vmem_limit_bytes=VMEM_LIMIT),
-        cost_estimate=pl.CostEstimate(flops=1_000_000_000, bytes_accessed=1000, transcendentals=0),
+        cost_estimate=pl.CostEstimate(flops=cost, bytes_accessed=1000, transcendentals=0),
         name="strengths",
     )(table, lattice, *pays, phases, phases3)
 
 
-def final_kernel(where_ref, offsets_ref, own, *refs):
+def final_kernel(where_ref, off_a_ref, off_b_ref, own, *refs):
     parts = refs[: 2 * PARTS]
-    s_ref, out_ref, v_ref, arr_ref, off_ref, sem = refs[2 * PARTS :]
+    sa_ref, sb_ref, out_ref, v_ref, arr_ref, off_ref, sem = refs[2 * PARTS :]
     slab = where_ref[0]
     core = where_ref[1]
     share = where_ref[2]
     copies = [
-        pltpu.make_async_copy(offsets_ref, off_ref, sem.at[0]),
+        pltpu.make_async_copy(off_a_ref.at[0], off_ref.at[0], sem.at[0]),
+        pltpu.make_async_copy(off_b_ref.at[0], off_ref.at[1], sem.at[1]),
     ]
 
     def bring(src, plane, count):
@@ -342,8 +348,7 @@
             for upper in range(2):
                 rows = pl.ds(pl.multiple_of((step * ROWS + kx) * HALF, HALF), HALF)
                 here = slice((2 * kx + upper) * HALF, (2 * kx + upper + 1) * HALF)
-                product = s_ref[upper, rows, :] * diff[here]
-                terms.append(product[:, :128] + product[:, 128:])
+                terms.append(sa_ref[upper, rows, :] * diff[here, :128] + sb_ref[upper, rows, :] * diff[here, 128:])
         term = jnp.concatenate(terms, axis=0)
         result = None
         for _ in range(3):
@@ -363,10 +368,10 @@
     lax.fori_loop(0, PLANES // UNROLL, body, 0)
 
 
-def contract(where, offsets, own, parts, strength):
+def contract(where, off_a, off_b, own, parts, s_a, s_b):
     return pl.pallas_call(
         final_kernel,
-        in_specs=[smem()] + [anywhere()] * (2 + 2 * PARTS) + [vmem()],
+        in_specs=[smem()] + [anywhere()] * (3 + 2 * PARTS) + [vmem()] * 2,
         out_specs=vmem(),
         out_shape=jax.ShapeDtypeStruct((PLANES, NB, SHARE), F32),
         scratch_shapes=[
@@ -378,7 +383,7 @@
         compiler_params=pltpu.CompilerParams(vmem_limit_bytes=VMEM_LIMIT),
         cost_estimate=pl.CostEstimate(flops=2_000_000_000, bytes_accessed=9_000_000, transcendentals=0),
         name="contract",
-    )(where, offsets, own, *parts, strength)
+    )(where, off_a, off_b, own, *parts, s_a, s_b)
 
 
 def local(occupation, q_offsets, coupling, window_bins, lorentz_table, lattice):
@@ -396,30 +401,34 @@
     def core_swap(array):
         return move(array, lambda yl, x, z, yh, c: (yl, x, z, yh, 1 - c))
 
+    tie = lax.optimization_barrier
+    half = lax.dynamic_slice_in_dim(occupation, core * HP, HP, 0)[None]
+    beyond = move(half, lambda yl, x, z, yh, c: (1 - yl, x, z, yh, c))
     pay = pack(q_offsets, window_bins, jnp.swapaxes(coupling[0], 1, 2))
-    half, pay = lax.optimization_barrier((lax.dynamic_slice_in_dim(occupation, core * HP, HP, 0)[None], pay))
-    along = [move(half, lambda yl, x, z, yh, c: (yl, (x + d) % 4, z, yh, c)) for d in (1, 3, 2)]
+    early2 = move(half, lambda yl, x, z, yh, c: (yl, (x + 2) % 4, z, yh, c))
     twin = move(pay, lambda yl, x, z, yh, c: (1 - yl, x, z, 1 - yh, c))
     ylo, x = slab // 4, slab % 4
-    lines = [(ylo, 1), (ylo, 3), (ylo, 2), (1 - ylo, 0), (1 - ylo, 1), (1 - ylo, 3), (1 - ylo, 2)]
-    sources = [y * 4 + (x + 4 - d) % 4 for y, d in lines]
+    lines = [(1, 0), (0, 2), (0, 1), (1, 1), (0, 3), (1, 3), (1, 2)]
+    sources = [(ylo if y == 0 else 1 - ylo) * 4 + (x + 4 - d) % 4 for y, d in lines]
     where = jnp.stack([slab, core, share] + sources).astype(jnp.int32)
+    both = jnp.concatenate([half, beyond], axis=0)
+    phases, phases3 = make_phases(where, lattice)
+    twin, both, phases, phases3, early2 = tie((twin, both, phases, phases3, early2))
     pair = jnp.concatenate([pay, twin], axis=0)
-    pair, where = lax.optimization_barrier((pair, where))
-    phases, phases3 = make_phases(where, lattice)
     group = [pair] + [move(pair, lambda yl, x, z, yh, c: (yl, x, (z + d) % 4, yh, c)) for d in (1, 3, 2)]
-    other = [core_swap(array) for array in group]
-    near_in = jnp.concatenate([half, along[0]], axis=0)
-    far_in = jnp.concatenate(along[1:], axis=0)
-    near_in, far_in, phases = lax.optimization_barrier((near_in, far_in, phases))
-    near = move(near_in, lambda yl, x, z, yh, c: (1 - yl, x, z, yh, c))
-    far = move(far_in, lambda yl, x, z, yh, c: (1 - yl, x, z, 1 - yh, c))
+    late1 = move(both, lambda yl, x, z, yh, c: (yl, (x + 1) % 4, z, yh, c))
+    late3 = move(both, lambda yl, x, z, yh, c: (yl, (x + 3) % 4, z, yh, c))
+    late2 = move(beyond, lambda yl, x, z, yh, c: (yl, (x + 2) % 4, z, yh, c))
     table = lorentz_table.T
-    strength, offsets = strengths(table, lattice, group + other, phases, phases3)
-    near, far, strength = lax.optimization_barrier((near, far, strength))
-    fetched = along + [near, far]
+    first = [group[0], core_swap(group[0]), group[1], core_swap(group[1])]
+    s_a, off_a = strengths(table, lattice, first, phases, phases3, 1000)
+    phases, s_a = tie((phases, s_a))
+    second = [group[2], core_swap(group[2]), group[3], core_swap(group[3])]
+    s_b, off_b = strengths(table, lattice, second, phases, phases3, 1000)
+    late1, late3, late2, s_a = tie((late1, late3, late2, s_a))
+    fetched = [beyond, early2, late1, late3, late2]
     swapped = [core_swap(array) for array in fetched]
-    return contract(where, offsets, occupation, fetched + swapped, strength)
+    return contract(where, off_a, off_b, occupation, fetched + swapped, s_a, s_b)
 
 
 def solution(mesh):

time: 52.8 us -> 50.5 us (0.956)
  waiting for transfers between devices: 8.13 us -> 4.7 us
  starting transfers between devices: 21.6 us -> 24 us
  other arithmetic: 1.64 us -> 0.38 us
    ppermute x18, waiting for transfers between devices: 8.13 us -> 4.7 us  [move(): lax.ppermute(array, ('ka', 'pb'), [(place(*at), place(*to(*at))) for at i...]
    ppermute x18, starting transfers between devices: 21.6 us -> 24 us  [move(): lax.ppermute(array, ('ka', 'pb'), [(place(*at), place(*to(*at))) for at i...]
    concatenate x1, other arithmetic: 0.91 us -> 0.01 us  [local(): pair = jnp.concatenate([pay, twin], axis=0)]
    pallas_call x2 -> x3, Pallas kernels: 15.8 us -> 15.8 us  [the longest x2 8.81 us: strengths(): pl.pallas_call(functools.partial(strength_kernel, groups), in_specs=[vmem...]
  transfers between devices with their start and end apart: 18 -> 18, of which waited for: 8 -> 3; matrix products, arithmetic and copies ran while one was open for 3% -> 1% of each run, Pallas kernels for 20% -> 24%
where the time goes in v4:
time: 50.5 us; the launch traced here: 50.3 us
  starting transfers between devices  24 us (48%)
  Pallas kernels  19.2 us (38%)
  waiting for transfers between devices  4.7 us (9%)
  local copies, waits for them, and re-layouts  1.83 us (4%)
    ppermute x18, starting transfers between devices, move(): lax.ppermute(array, ('ka', 'pb'), [(place(*at), place(*to(*at))) for at i...  24 us
    pallas_call x2, Pallas kernels, strengths(): pl.pallas_call(functools.partial(strength_kernel, groups), in_specs=[vmem...  8.81 us
    pallas_call x1, Pallas kernels, contract(): pl.pallas_call(final_kernel, in_specs=[smem()] + [anywhere()] * (3 + 2 *...  7.02 us
    ppermute x18, waiting for transfers between devices, move(): lax.ppermute(array, ('ka', 'pb'), [(place(*at), place(*to(*at))) for at i...  4.7 us
    pallas_call x1, Pallas kernels, pack(): pl.pallas_call(pack_kernel, in_specs=[smem(), smem(), vmem()], out_specs=...  1.71 us
    pallas_call x1, Pallas kernels, make_phases(): pl.pallas_call(phase_kernel, in_specs=[smem(), vmem()], out_specs=[vmem()...  1.64 us
    broadcast_in_dim x1, local copies, waits for them, and re-layouts, local(): half = lax.dynamic_slice_in_dim(occupation, core * HP, HP, 0)[None]  1.04 us
  transfers between devices with their start and end apart: 18, of which 3 were waited for; matrix products, arithmetic and copies ran while one was open for 1% of the time, Pallas kernels for 24%

profile of v4, /device:TPU:1, one launch (start us, length us, event | category | flops | bytes accessed | tf_op | source)
XLA Modules:
  0.0 50.3 jit_solution(13535868465722260964)
XLA Ops:
  0.0 1.0 %dynamic-slice_bitcast_fusion = bf16[1,5,4,6400]{3,2,1,0:T(4,128)(2,1)S(1)} fusion(bf16[10,4,6400]{2,1,0:T(4,128)(2,1)} %own.1, s32[]{:T(128)S(6)} %select_n.47), kind=kLoop, calls=%fused_computation.1 | loop fusion | bytes 512004 | tf_op jit(solution)/shard_map/broadcast_in_dim | solution.py:405
  1.0 2.2 %collective-permute-start.1 = (bf16[1,5,4,6400]{3,2,1,0:T(4,128)(2,1)S(1)}, bf16[1,5,4,6400]{3,2,1,0:T(4,128)(2,1)S(1)}, u32[]{:S(2)}, u32[]{:S(2)}) collective-permute-start(bf16[1,5,4,6400]{3,2,1,0:T(4,128)(2,1)S(1)} %dynamic-slice_bitcast_fusion), channel_id=1, source_target_pairs={{0,64},{1,65},{2,66},{3,67},{4,68},{5,69},{6,70},{7,71},{8,72},{9,... | collective-permute-start | bytes 768008 | tf_op jit(solution)/shard_map/ppermute | solution.py:399
  3.2 2.7 %collective-permute-start.2 = (bf16[1,5,4,6400]{3,2,1,0:T(4,128)(2,1)S(1)}, bf16[1,5,4,6400]{3,2,1,0:T(4,128)(2,1)S(1)}, u32[]{:S(2)}, u32[]{:S(2)}) collective-permute-start(bf16[1,5,4,6400]{3,2,1,0:T(4,128)(2,1)S(1)} %dynamic-slice_bitcast_fusion), channel_id=1, source_target_pairs={{0,32},{1,33},{2,34},{3,35},{4,36},{5,37},{6,38},{7,39},{8,40},{9,... | collective-permute-start | bytes 768008 | tf_op jit(solution)/shard_map/ppermute | solution.py:399
  6.0 1.7 %pack.1 = bf16[208,256]{1,0:T(8,128)(2,1)} custom-call(s32[1,3]{1,0:T(1,128)} %off_ref.1, s32[1,16]{1,0:T(1,128)} %bins_ref.1, bf16[2,96,200]{2,1,0:T(8,128)(2,1)} %bitcast.18), custom_call_target="tpu_custom_call" | custom-call | tf_op jit(solution)/shard_map/pack/pallas_call | solution.py:81
  7.7 1.9 %collective-permute-start = (bf16[208,256]{1,0:T(8,128)(2,1)}, bf16[208,256]{1,0:T(8,128)(2,1)S(1)}, u32[]{:S(2)}, u32[]{:S(2)}) collective-permute-start(bf16[208,256]{1,0:T(8,128)(2,1)} %pack.1), channel_id=1, source_target_pairs={{0,66},{1,67},{2,64},{3,65},{4,70},{5,71},{6,68},{7,69},{8,74},{9,... | collective-permute-start | bytes 319496 | tf_op jit(solution)/shard_map/ppermute | solution.py:399
  9.6 0.1 stack.43.where_ref
  9.7 0.0 copy-start.2
  9.7 0.7 %copy-done.2 = s32[3,200]{1,0:T(4,128)S(1)} copy-done((s32[3,200]{1,0:T(4,128)S(1)}, s32[3,200]{1,0:T(4,128)}, u32[]{:S(2)}) %copy-start.2) | copy-done | bytes 2424
  10.4 0.0 copy-start.3
  10.4 0.0 copy-start.1
  10.4 1.6 %phases.1 = (bf16[2000,512]{1,0:T(8,128)(2,1)S(1)}, bf16[2000,256]{1,0:T(8,128)(2,1)S(1)}) custom-call(s32[10]{0:T(128)S(1)} %stack.43.where_ref, s32[3,200]{1,0:T(4,128)S(1)} %copy-done.2), custom_call_target="tpu_custom_call" | custom-call | flops 1500000000 | bytes 3000000 | tf_op jit(solution)/shard_map/phases/pallas_call | solution.py:167
  12.0 0.0 collective-permute-done.1.refs_0_
  12.0 0.4 pad_maximum_fusion
  12.4 0.5 %collective-permute-done = bf16[208,256]{1,0:T(8,128)(2,1)S(1)} collective-permute-done((bf16[208,256]{1,0:T(8,128)(2,1)}, bf16[208,256]{1,0:T(8,128)(2,1)S(1)}, u32[]{:S(2)}, u32[]{:S(2)}) %collective-permute-start) | collective-permute-done | bytes 106528 | tf_op jit(solution)/shard_map/ppermute | solution.py:399
  12.9 0.0 collective-permute-done.2.refs_1_
  12.9 0.0 copy-done.3
  13.0 1.7 %collective-permute-start.4 = (bf16[416,256]{1,0:T(8,128)(2,1)S(1)}, bf16[416,256]{1,0:T(8,128)(2,1)S(1)}, u32[]{:S(2)}, u32[]{:S(2)}) collective-permute-start(bf16[416,256]{1,0:T(8,128)(2,1)S(1)} %pad_maximum_fusion.1.refs_0_), channel_id=1, source_target_pairs={{0,4},{1,5},{2,6},{3,7},{4,8},{5,9},{6,10},{7,11},{8,12},{9,13},{1... | collective-permute-start | bytes 638984 | tf_op jit(solution)/shard_map/ppermute | solution.py:399
  14.7 0.2 collective-permute-start.10
  14.9 2.5 %collective-permute-start.11 = (bf16[2,5,4,6400]{3,2,1,0:T(4,128)(2,1)S(1)}, bf16[2,5,4,6400]{3,2,1,0:T(4,128)(2,1)S(1)}, u32[]{:S(2)}, u32[]{:S(2)}) collective-permute-start(bf16[2,5,4,6400]{3,2,1,0:T(4,128)(2,1)S(1)} %pad_maximum_fusion), channel_id=1, source_target_pairs={{0,48},{1,49},{2,50},{3,51},{4,52},{5,53},{6,54},{7,55},{8,56},{9,... | collective-permute-start | bytes 1536008 | tf_op jit(solution)/shard_map/ppermute | solution.py:399
  17.4 3.0 %collective-permute-start.3 = (bf16[416,256]{1,0:T(8,128)(2,1)S(1)}, bf16[416,256]{1,0:T(8,128)(2,1)S(1)}, u32[]{:S(2)}, u32[]{:S(2)}) collective-permute-start(bf16[416,256]{1,0:T(8,128)(2,1)S(1)} %pad_maximum_fusion.1.refs_0_), channel_id=1, source_target_pairs={{0,1},{1,0},{2,3},{3,2},{4,5},{5,4},{6,7},{7,6},{8,9},{9,8},{10,11... | collective-permute-start | bytes 638984 | tf_op jit(solution)/shard_map/ppermute | solution.py:399
  20.3 0.0 collective-permute-done.4.refs_2_
  20.3 2.7 %collective-permute-start.5 = (bf16[416,256]{1,0:T(8,128)(2,1)S(1)}, bf16[416,256]{1,0:T(8,128)(2,1)S(1)}, u32[]{:S(2)}, u32[]{:S(2)}) collective-permute-start(bf16[416,256]{1,0:T(8,128)(2,1)S(1)} %collective-permute-done.4.refs_2_), channel_id=1, source_target_pairs={{0,1},{1,0},{2,3},{3,2},{4,5},{5,4},{6,7},{7,6},{8,9},{9,8},{10,11... | collective-permute-start | bytes 638984 | tf_op jit(solution)/shard_map/ppermute | solution.py:399
  23.0 1.3 %collective-permute-start.12 = (bf16[1,5,4,6400]{3,2,1,0:T(4,128)(2,1)S(1)}, bf16[1,5,4,6400]{3,2,1,0:T(4,128)(2,1)S(1)}, u32[]{:S(2)}, u32[]{:S(2)}) collective-permute-start(bf16[1,5,4,6400]{3,2,1,0:T(4,128)(2,1)S(1)} %collective-permute-done.1.refs_0_), channel_id=1, source_target_pairs={{0,32},{1,33},{2,34},{3,35},{4,36},{5,37},{6,38},{7,39},{8,40},{9,... | collective-permute-start | bytes 768008 | tf_op jit(solution)/shard_map/ppermute | solution.py:399
  24.3 0.0 collective-permute-done.3.refs_1_
  24.3 1.5 %collective-permute-start.6 = (bf16[416,256]{1,0:T(8,128)(2,1)S(1)}, bf16[416,256]{1,0:T(8,128)(2,1)S(1)}, u32[]{:S(2)}, u32[]{:S(2)}) collective-permute-start(bf16[416,256]{1,0:T(8,128)(2,1)S(1)} %pad_maximum_fusion.1.refs_0_), channel_id=1, source_target_pairs={{0,12},{1,13},{2,14},{3,15},{4,0},{5,1},{6,2},{7,3},{8,4},{9,5},{1... | collective-permute-start | bytes 638984 | tf_op jit(solution)/shard_map/ppermute | solution.py:399
  25.8 0.0 collective-permute-done.5.refs_3_
  25.8 0.0 collective-permute-start.8
  25.8 0.0 copy-done.1
  25.8 4.4 %strengths.2 = (f32[2,2000,128]{2,1,0:T(8,128)S(1)}, s32[1,8,128]{2,1,0:T(8,128)S(1)}) custom-call(f32[6,32]{1,0:T(8,128)S(1)} %bitcast.16, s32[3,200]{1,0:T(4,128)S(1)} %copy-done.2, bf16[416,256]{1,0:T(8,128)(2,1)S(1)} %pad_maximum_fusion.1.refs_0_, bf16[416,256]{1,0:T(8,128)(2,1)S(1)} %collective-permute-done.3.refs_1_, ...), custom_call_target="tpu_custom_call" | custom-call | flops 1000 | bytes 1000 | tf_op jit(solution)/shard_map/strengths/pallas_call | solution.py:267
  30.2 0.0 copy-start
  30.2 2.6 %collective-permute-done.12.refs_4_ = bf16[1,5,4,6400]{3,2,1,0:T(4,128)(2,1)S(1)} collective-permute-done((bf16[1,5,4,6400]{3,2,1,0:T(4,128)(2,1)S(1)}, bf16[1,5,4,6400]{3,2,1,0:T(4,128)(2,1)S(1)}, u32[]{:S(2)}, u32[]{:S(2)}) %collective-permute-start.12) | collective-permute-done | bytes 256032 | tf_op jit(solution)/shard_map/ppermute | solution.py:399
  32.8 0.0 collective-permute-done.10.refs_2_
  32.8 0.0 collective-permute-done.11.refs_3_
  32.8 2.6 %collective-permute-start.15 = (bf16[2,5,4,6400]{3,2,1,0:T(4,128)(2,1)S(1)}, bf16[2,5,4,6400]{3,2,1,0:T(4,128)(2,1)S(1)}, u32[]{:S(2)}, u32[]{:S(2)}) collective-permute-start(bf16[2,5,4,6400]{3,2,1,0:T(4,128)(2,1)S(1)} %collective-permute-done.10.refs_2_), channel_id=1, source_target_pairs={{0,1},{1,0},{2,3},{3,2},{4,5},{5,4},{6,7},{7,6},{8,9},{9,8},{10,11... | collective-permute-start | bytes 1536008 | tf_op jit(solution)/shard_map/ppermute | solution.py:399
  35.5 0.0 collective-permute-start.16
  35.5 0.0 collective-permute-done.6.refs_0_
  35.5 0.5 %collective-permute-start.7 = (bf16[416,256]{1,0:T(8,128)(2,1)S(1)}, bf16[416,256]{1,0:T(8,128)(2,1)S(1)}, u32[]{:S(2)}, u32[]{:S(2)}) collective-permute-start(bf16[416,256]{1,0:T(8,128)(2,1)S(1)} %collective-permute-done.6.refs_0_), channel_id=1, source_target_pairs={{0,1},{1,0},{2,3},{3,2},{4,5},{5,4},{6,7},{7,6},{8,9},{9,8},{10,11... | collective-permute-start | bytes 638984 | tf_op jit(solution)/shard_map/ppermute | solution.py:399
  36.0 0.0 collective-permute-done.8.refs_2_
  36.0 0.3 collective-permute-start.9
  36.2 0.2 collective-permute-start.14
  36.5 1.5 %collective-permute-done.7.refs_1_ = bf16[416,256]{1,0:T(8,128)(2,1)S(1)} collective-permute-done((bf16[416,256]{1,0:T(8,128)(2,1)S(1)}, bf16[416,256]{1,0:T(8,128)(2,1)S(1)}, u32[]{:S(2)}, u32[]{:S(2)}) %collective-permute-start.7) | collective-permute-done | bytes 213024 | tf_op jit(solution)/shard_map/ppermute | solution.py:399
  38.0 0.4 collective-permute-start.13
  38.4 0.0 collective-permute-done.9.refs_3_
  38.4 0.3 collective-permute-start.17
  38.7 4.4 %strengths.3 = (f32[2,2000,128]{2,1,0:T(8,128)S(1)}, s32[1,8,128]{2,1,0:T(8,128)S(1)}) custom-call(f32[6,32]{1,0:T(8,128)S(1)} %bitcast.17, s32[3,200]{1,0:T(4,128)S(1)} %copy-done.2, bf16[416,256]{1,0:T(8,128)(2,1)S(1)} %collective-permute-done.6.refs_0_, bf16[416,256]{1,0:T(8,128)(2,1)S(1)} %collective-permute-done.7.refs_1_, ...), custom_call_target="tpu_custom_call" | custom-call | flops 1000 | bytes 1000 | tf_op jit(solution)/shard_map/strengths/pallas_call | solution.py:267
  43.1 0.0 collective-permute-done.13.refs_5_
  43.1 0.0 collective-permute-done.14.refs_6_
  43.1 0.0 collective-permute-done.17.refs_9_
  43.1 0.0 collective-permute-done.15.refs_7_
  43.1 0.0 collective-permute-done.16.refs_8_
  43.2 0.0 copy-done
  43.2 7.0 %contract.1 = f32[10,4,400]{2,1,0:T(4,128)} custom-call(s32[10]{0:T(128)S(1)} %stack.43.where_ref, s32[1,8,128]{2,1,0:T(8,128)S(1)} %get-tuple-element.27.off_a_ref, s32[1,8,128]{2,1,0:T(8,128)S(1)} %get-tuple-element.30.off_b_ref, bf16[10,4,6400]{2,1,0:T(4,128)(2,1)S(1)} %copy-done, bf16[1,5,4,6400]{3,2,1,0:T(4,128)(2,1)S(1)} %collective-permute-done.1.refs_0_, ...), custom_call_target="tpu_custom_call" | custom-call | flops 2000000000 | bytes 9000000 | tf_op jit(solution)/shard_map/contract/pallas_call | solution.py:372
  (1 shorter events, 0.0 us)
Async XLA Ops:
  1.0 11.0 %collective-permute-start.1 = (bf16[1,5,4,6400]{3,2,1,0:T(4,128)(2,1)S(1)}, bf16[1,5,4,6400]{3,2,1,0:T(4,128)(2,1)S(1)}, u32[]{:S(2)}, u32[]{:S(2)}) collective-permute-start(bf16[1,5,4,6400]{3,2,1,0:T(4,128)(2,1)S(1)} %dynamic-slice_bitcast_fusion), channel_id=1, source_target_pairs={{0,64},{1,65},{2,66},{3,67},{4,68},{5,69},{6,70},{7,71},{8,72},{9,... | collective-permute-start | bytes 768008 | tf_op jit(solution)/shard_map/ppermute | solution.py:399
  3.2 9.7 %collective-permute-start.2 = (bf16[1,5,4,6400]{3,2,1,0:T(4,128)(2,1)S(1)}, bf16[1,5,4,6400]{3,2,1,0:T(4,128)(2,1)S(1)}, u32[]{:S(2)}, u32[]{:S(2)}) collective-permute-start(bf16[1,5,4,6400]{3,2,1,0:T(4,128)(2,1)S(1)} %dynamic-slice_bitcast_fusion), channel_id=1, source_target_pairs={{0,32},{1,33},{2,34},{3,35},{4,36},{5,37},{6,38},{7,39},{8,40},{9,... | collective-permute-start | bytes 768008 | tf_op jit(solution)/shard_map/ppermute | solution.py:399
  7.7 5.2 %collective-permute-start = (bf16[208,256]{1,0:T(8,128)(2,1)}, bf16[208,256]{1,0:T(8,128)(2,1)S(1)}, u32[]{:S(2)}, u32[]{:S(2)}) collective-permute-start(bf16[208,256]{1,0:T(8,128)(2,1)} %pack.1), channel_id=1, source_target_pairs={{0,66},{1,67},{2,64},{3,65},{4,70},{5,71},{6,68},{7,69},{8,74},{9,... | collective-permute-start | bytes 319496 | tf_op jit(solution)/shard_map/ppermute | solution.py:399
  9.7 0.7 %copy-start.2 = (s32[3,200]{1,0:T(4,128)S(1)}, s32[3,200]{1,0:T(4,128)}, u32[]{:S(2)}) copy-start(s32[3,200]{1,0:T(4,128)} %lattice_ref.5) | copy-start | bytes 7204
  10.4 2.6 %copy-start.3 = (bf16[208,256]{1,0:T(8,128)(2,1)S(1)}, bf16[208,256]{1,0:T(8,128)(2,1)}, u32[]{:S(2)}) copy-start(bf16[208,256]{1,0:T(8,128)(2,1)} %pack.1) | copy-start | bytes 319492
  10.4 15.4 %copy-start.1 = (f32[32,6]{0,1:T(8,128)S(1)}, f32[32,6]{0,1:T(8,128)}, u32[]{:S(2)}) copy-start(f32[32,6]{0,1:T(8,128)} %param.10) | copy-start | bytes 2308
  13.0 7.3 %collective-permute-start.4 = (bf16[416,256]{1,0:T(8,128)(2,1)S(1)}, bf16[416,256]{1,0:T(8,128)(2,1)S(1)}, u32[]{:S(2)}, u32[]{:S(2)}) collective-permute-start(bf16[416,256]{1,0:T(8,128)(2,1)S(1)} %pad_maximum_fusion.1.refs_0_), channel_id=1, source_target_pairs={{0,4},{1,5},{2,6},{3,7},{4,8},{5,9},{6,10},{7,11},{8,12},{9,13},{1... | collective-permute-start | bytes 638984 | tf_op jit(solution)/shard_map/ppermute | solution.py:399
  14.7 18.1 %collective-permute-start.10 = (bf16[2,5,4,6400]{3,2,1,0:T(4,128)(2,1)S(1)}, bf16[2,5,4,6400]{3,2,1,0:T(4,128)(2,1)S(1)}, u32[]{:S(2)}, u32[]{:S(2)}) collective-permute-start(bf16[2,5,4,6400]{3,2,1,0:T(4,128)(2,1)S(1)} %pad_maximum_fusion), channel_id=1, source_target_pairs={{0,16},{1,17},{2,18},{3,19},{4,20},{5,21},{6,22},{7,23},{8,24},{9,... | collective-permute-start | bytes 1536008 | tf_op jit(solution)/shard_map/ppermute | solution.py:399
  14.9 18.0 %collective-permute-start.11 = (bf16[2,5,4,6400]{3,2,1,0:T(4,128)(2,1)S(1)}, bf16[2,5,4,6400]{3,2,1,0:T(4,128)(2,1)S(1)}, u32[]{:S(2)}, u32[]{:S(2)}) collective-permute-start(bf16[2,5,4,6400]{3,2,1,0:T(4,128)(2,1)S(1)} %pad_maximum_fusion), channel_id=1, source_target_pairs={{0,48},{1,49},{2,50},{3,51},{4,52},{5,53},{6,54},{7,55},{8,56},{9,... | collective-permute-start | bytes 1536008 | tf_op jit(solution)/shard_map/ppermute | solution.py:399
  17.4 6.9 %collective-permute-start.3 = (bf16[416,256]{1,0:T(8,128)(2,1)S(1)}, bf16[416,256]{1,0:T(8,128)(2,1)S(1)}, u32[]{:S(2)}, u32[]{:S(2)}) collective-permute-start(bf16[416,256]{1,0:T(8,128)(2,1)S(1)} %pad_maximum_fusion.1.refs_0_), channel_id=1, source_target_pairs={{0,1},{1,0},{2,3},{3,2},{4,5},{5,4},{6,7},{7,6},{8,9},{9,8},{10,11... | collective-permute-start | bytes 638984 | tf_op jit(solution)/shard_map/ppermute | solution.py:399
  20.3 5.5 %collective-permute-start.5 = (bf16[416,256]{1,0:T(8,128)(2,1)S(1)}, bf16[416,256]{1,0:T(8,128)(2,1)S(1)}, u32[]{:S(2)}, u32[]{:S(2)}) collective-permute-start(bf16[416,256]{1,0:T(8,128)(2,1)S(1)} %collective-permute-done.4.refs_2_), channel_id=1, source_target_pairs={{0,1},{1,0},{2,3},{3,2},{4,5},{5,4},{6,7},{7,6},{8,9},{9,8},{10,11... | collective-permute-start | bytes 638984 | tf_op jit(solution)/shard_map/ppermute | solution.py:399
  23.0 9.8 %collective-permute-start.12 = (bf16[1,5,4,6400]{3,2,1,0:T(4,128)(2,1)S(1)}, bf16[1,5,4,6400]{3,2,1,0:T(4,128)(2,1)S(1)}, u32[]{:S(2)}, u32[]{:S(2)}) collective-permute-start(bf16[1,5,4,6400]{3,2,1,0:T(4,128)(2,1)S(1)} %collective-permute-done.1.refs_0_), channel_id=1, source_target_pairs={{0,32},{1,33},{2,34},{3,35},{4,36},{5,37},{6,38},{7,39},{8,40},{9,... | collective-permute-start | bytes 768008 | tf_op jit(solution)/shard_map/ppermute | solution.py:399
  24.3 11.2 %collective-permute-start.6 = (bf16[416,256]{1,0:T(8,128)(2,1)S(1)}, bf16[416,256]{1,0:T(8,128)(2,1)S(1)}, u32[]{:S(2)}, u32[]{:S(2)}) collective-permute-start(bf16[416,256]{1,0:T(8,128)(2,1)S(1)} %pad_maximum_fusion.1.refs_0_), channel_id=1, source_target_pairs={{0,12},{1,13},{2,14},{3,15},{4,0},{5,1},{6,2},{7,3},{8,4},{9,5},{1... | collective-permute-start | bytes 638984 | tf_op jit(solution)/shard_map/ppermute | solution.py:399
  25.8 10.2 %collective-permute-start.8 = (bf16[416,256]{1,0:T(8,128)(2,1)S(1)}, bf16[416,256]{1,0:T(8,128)(2,1)S(1)}, u32[]{:S(2)}, u32[]{:S(2)}) collective-permute-start(bf16[416,256]{1,0:T(8,128)(2,1)S(1)} %pad_maximum_fusion.1.refs_0_), channel_id=1, source_target_pairs={{0,8},{1,9},{2,10},{3,11},{4,12},{5,13},{6,14},{7,15},{8,0},{9,1},... | collective-permute-start | bytes 638984 | tf_op jit(solution)/shard_map/ppermute | solution.py:399
  30.2 12.9 %copy-start = (bf16[10,4,6400]{2,1,0:T(4,128)(2,1)S(1)}, bf16[10,4,6400]{2,1,0:T(4,128)(2,1)}, u32[]{:S(2)}) copy-start(bf16[10,4,6400]{2,1,0:T(4,128)(2,1)} %own.1) | copy-start | bytes 1536004
  32.8 10.3 %collective-permute-start.15 = (bf16[2,5,4,6400]{3,2,1,0:T(4,128)(2,1)S(1)}, bf16[2,5,4,6400]{3,2,1,0:T(4,128)(2,1)S(1)}, u32[]{:S(2)}, u32[]{:S(2)}) collective-permute-start(bf16[2,5,4,6400]{3,2,1,0:T(4,128)(2,1)S(1)} %collective-permute-done.10.refs_2_), channel_id=1, source_target_pairs={{0,1},{1,0},{2,3},{3,2},{4,5},{5,4},{6,7},{7,6},{8,9},{9,8},{10,11... | collective-permute-start | bytes 1536008 | tf_op jit(solution)/shard_map/ppermute | solution.py:399
  35.5 7.7 %collective-permute-start.16 = (bf16[2,5,4,6400]{3,2,1,0:T(4,128)(2,1)S(1)}, bf16[2,5,4,6400]{3,2,1,0:T(4,128)(2,1)S(1)}, u32[]{:S(2)}, u32[]{:S(2)}) collective-permute-start(bf16[2,5,4,6400]{3,2,1,0:T(4,128)(2,1)S(1)} %collective-permute-done.11.refs_3_), channel_id=1, source_target_pairs={{0,1},{1,0},{2,3},{3,2},{4,5},{5,4},{6,7},{7,6},{8,9},{9,8},{10,11... | collective-permute-start | bytes 1536008 | tf_op jit(solution)/shard_map/ppermute | solution.py:399
  35.5 2.5 %collective-permute-start.7 = (bf16[416,256]{1,0:T(8,128)(2,1)S(1)}, bf16[416,256]{1,0:T(8,128)(2,1)S(1)}, u32[]{:S(2)}, u32[]{:S(2)}) collective-permute-start(bf16[416,256]{1,0:T(8,128)(2,1)S(1)} %collective-permute-done.6.refs_0_), channel_id=1, source_target_pairs={{0,1},{1,0},{2,3},{3,2},{4,5},{5,4},{6,7},{7,6},{8,9},{9,8},{10,11... | collective-permute-start | bytes 638984 | tf_op jit(solution)/shard_map/ppermute | solution.py:399
  36.0 2.4 %collective-permute-start.9 = (bf16[416,256]{1,0:T(8,128)(2,1)S(1)}, bf16[416,256]{1,0:T(8,128)(2,1)S(1)}, u32[]{:S(2)}, u32[]{:S(2)}) collective-permute-start(bf16[416,256]{1,0:T(8,128)(2,1)S(1)} %collective-permute-done.8.refs_2_), channel_id=1, source_target_pairs={{0,1},{1,0},{2,3},{3,2},{4,5},{5,4},{6,7},{7,6},{8,9},{9,8},{10,11... | collective-permute-start | bytes 638984 | tf_op jit(solution)/shard_map/ppermute | solution.py:399
  36.2 6.9 %collective-permute-start.14 = (bf16[1,5,4,6400]{3,2,1,0:T(4,128)(2,1)S(1)}, bf16[1,5,4,6400]{3,2,1,0:T(4,128)(2,1)S(1)}, u32[]{:S(2)}, u32[]{:S(2)}) collective-permute-start(bf16[1,5,4,6400]{3,2,1,0:T(4,128)(2,1)S(1)} %collective-permute-done.2.refs_1_), channel_id=1, source_target_pairs={{0,1},{1,0},{2,3},{3,2},{4,5},{5,4},{6,7},{7,6},{8,9},{9,8},{10,11... | collective-permute-start | bytes 768008 | tf_op jit(solution)/shard_map/ppermute | solution.py:399
  38.0 5.1 %collective-permute-start.13 = (bf16[1,5,4,6400]{3,2,1,0:T(4,128)(2,1)S(1)}, bf16[1,5,4,6400]{3,2,1,0:T(4,128)(2,1)S(1)}, u32[]{:S(2)}, u32[]{:S(2)}) collective-permute-start(bf16[1,5,4,6400]{3,2,1,0:T(4,128)(2,1)S(1)} %collective-permute-done.1.refs_0_), channel_id=1, source_target_pairs={{0,1},{1,0},{2,3},{3,2},{4,5},{5,4},{6,7},{7,6},{8,9},{9,8},{10,11... | collective-permute-start | bytes 768008 | tf_op jit(solution)/shard_map/ppermute | solution.py:399
  38.4 4.7 %collective-permute-start.17 = (bf16[1,5,4,6400]{3,2,1,0:T(4,128)(2,1)S(1)}, bf16[1,5,4,6400]{3,2,1,0:T(4,128)(2,1)S(1)}, u32[]{:S(2)}, u32[]{:S(2)}) collective-permute-start(bf16[1,5,4,6400]{3,2,1,0:T(4,128)(2,1)S(1)} %collective-permute-done.12.refs_4_), channel_id=1, source_target_pairs={{0,1},{1,0},{2,3},{3,2},{4,5},{5,4},{6,7},{7,6},{8,9},{9,8},{10,11... | collective-permute-start | bytes 768008 | tf_op jit(solution)/shard_map/ppermute | solution.py:399

commit v5 on v4

--- a/solution.py
+++ b/solution.py
@@ -34,7 +34,7 @@
 WIN = 640
 STEP = 1000
 UNROLL = 10
-VMEM_LIMIT = 28 * 1024 * 1024
+VMEM_LIMIT = 20 * 1024 * 1024
 F32 = jnp.float32
 BF16 = jnp.bfloat16
 

time: 50.5 us -> 50.5 us (level)
  no operation moved by 1% of the time
where the time goes in v5:
time: 50.5 us; the launch traced here: 50.3 us
  starting transfers between devices  24 us (48%)
  Pallas kernels  19.2 us (38%)
  waiting for transfers between devices  4.7 us (9%)
  local copies, waits for them, and re-layouts  1.83 us (4%)
    ppermute x18, starting transfers between devices, move(): lax.ppermute(array, ('ka', 'pb'), [(place(*at), place(*to(*at))) for at i...  24 us
    pallas_call x2, Pallas kernels, strengths(): pl.pallas_call(functools.partial(strength_kernel, groups), in_specs=[vmem...  8.81 us
    pallas_call x1, Pallas kernels, contract(): pl.pallas_call(final_kernel, in_specs=[smem()] + [anywhere()] * (3 + 2 *...  7.02 us
    ppermute x18, waiting for transfers between devices, move(): lax.ppermute(array, ('ka', 'pb'), [(place(*at), place(*to(*at))) for at i...  4.7 us
    pallas_call x1, Pallas kernels, pack(): pl.pallas_call(pack_kernel, in_specs=[smem(), smem(), vmem()], out_specs=...  1.71 us
    pallas_call x1, Pallas kernels, make_phases(): pl.pallas_call(phase_kernel, in_specs=[smem(), vmem()], out_specs=[vmem()...  1.64 us
    broadcast_in_dim x1, local copies, waits for them, and re-layouts, local(): half = lax.dynamic_slice_in_dim(occupation, core * HP, HP, 0)[None]  1.04 us
  transfers between devices with their start and end apart: 18, of which 3 were waited for; matrix products, arithmetic and copies ran while one was open for 1% of the time, Pallas kernels for 24%

profile of v5, /device:TPU:1, one launch (start us, length us, event | category | flops | bytes accessed | tf_op | source)
XLA Modules:
  0.0 50.3 jit_solution(8539049780581894987)
XLA Ops:
  0.0 1.0 %dynamic-slice_bitcast_fusion = bf16[1,5,4,6400]{3,2,1,0:T(4,128)(2,1)S(1)} fusion(bf16[10,4,6400]{2,1,0:T(4,128)(2,1)} %own.1, s32[]{:T(128)S(6)} %select_n.47), kind=kLoop, calls=%fused_computation.1 | loop fusion | bytes 512004 | tf_op jit(solution)/shard_map/broadcast_in_dim | solution.py:405
  1.0 2.2 %collective-permute-start.1 = (bf16[1,5,4,6400]{3,2,1,0:T(4,128)(2,1)S(1)}, bf16[1,5,4,6400]{3,2,1,0:T(4,128)(2,1)S(1)}, u32[]{:S(2)}, u32[]{:S(2)}) collective-permute-start(bf16[1,5,4,6400]{3,2,1,0:T(4,128)(2,1)S(1)} %dynamic-slice_bitcast_fusion), channel_id=1, source_target_pairs={{0,64},{1,65},{2,66},{3,67},{4,68},{5,69},{6,70},{7,71},{8,72},{9,... | collective-permute-start | bytes 768008 | tf_op jit(solution)/shard_map/ppermute | solution.py:399
  3.2 2.7 %collective-permute-start.2 = (bf16[1,5,4,6400]{3,2,1,0:T(4,128)(2,1)S(1)}, bf16[1,5,4,6400]{3,2,1,0:T(4,128)(2,1)S(1)}, u32[]{:S(2)}, u32[]{:S(2)}) collective-permute-start(bf16[1,5,4,6400]{3,2,1,0:T(4,128)(2,1)S(1)} %dynamic-slice_bitcast_fusion), channel_id=1, source_target_pairs={{0,32},{1,33},{2,34},{3,35},{4,36},{5,37},{6,38},{7,39},{8,40},{9,... | collective-permute-start | bytes 768008 | tf_op jit(solution)/shard_map/ppermute | solution.py:399
  6.0 1.7 %pack.1 = bf16[208,256]{1,0:T(8,128)(2,1)} custom-call(s32[1,3]{1,0:T(1,128)} %off_ref.1, s32[1,16]{1,0:T(1,128)} %bins_ref.1, bf16[2,96,200]{2,1,0:T(8,128)(2,1)} %bitcast.18), custom_call_target="tpu_custom_call" | custom-call | tf_op jit(solution)/shard_map/pack/pallas_call | solution.py:81
  7.7 1.9 %collective-permute-start = (bf16[208,256]{1,0:T(8,128)(2,1)}, bf16[208,256]{1,0:T(8,128)(2,1)S(1)}, u32[]{:S(2)}, u32[]{:S(2)}) collective-permute-start(bf16[208,256]{1,0:T(8,128)(2,1)} %pack.1), channel_id=1, source_target_pairs={{0,66},{1,67},{2,64},{3,65},{4,70},{5,71},{6,68},{7,69},{8,74},{9,... | collective-permute-start | bytes 319496 | tf_op jit(solution)/shard_map/ppermute | solution.py:399
  9.6 0.1 stack.43.where_ref
  9.7 0.0 copy-start.2
  9.7 0.7 %copy-done.2 = s32[3,200]{1,0:T(4,128)S(1)} copy-done((s32[3,200]{1,0:T(4,128)S(1)}, s32[3,200]{1,0:T(4,128)}, u32[]{:S(2)}) %copy-start.2) | copy-done | bytes 2424
  10.4 0.0 copy-start.3
  10.4 0.0 copy-start.1
  10.4 1.6 %phases.1 = (bf16[2000,512]{1,0:T(8,128)(2,1)S(1)}, bf16[2000,256]{1,0:T(8,128)(2,1)S(1)}) custom-call(s32[10]{0:T(128)S(1)} %stack.43.where_ref, s32[3,200]{1,0:T(4,128)S(1)} %copy-done.2), custom_call_target="tpu_custom_call" | custom-call | flops 1500000000 | bytes 3000000 | tf_op jit(solution)/shard_map/phases/pallas_call | solution.py:167
  12.0 0.0 collective-permute-done.1.refs_0_
  12.0 0.4 pad_maximum_fusion
  12.4 0.5 %collective-permute-done = bf16[208,256]{1,0:T(8,128)(2,1)S(1)} collective-permute-done((bf16[208,256]{1,0:T(8,128)(2,1)}, bf16[208,256]{1,0:T(8,128)(2,1)S(1)}, u32[]{:S(2)}, u32[]{:S(2)}) %collective-permute-start) | collective-permute-done | bytes 106528 | tf_op jit(solution)/shard_map/ppermute | solution.py:399
  12.9 0.0 collective-permute-done.2.refs_1_
  12.9 0.0 copy-done.3
  13.0 1.7 %collective-permute-start.4 = (bf16[416,256]{1,0:T(8,128)(2,1)S(1)}, bf16[416,256]{1,0:T(8,128)(2,1)S(1)}, u32[]{:S(2)}, u32[]{:S(2)}) collective-permute-start(bf16[416,256]{1,0:T(8,128)(2,1)S(1)} %pad_maximum_fusion.1.refs_0_), channel_id=1, source_target_pairs={{0,4},{1,5},{2,6},{3,7},{4,8},{5,9},{6,10},{7,11},{8,12},{9,13},{1... | collective-permute-start | bytes 638984 | tf_op jit(solution)/shard_map/ppermute | solution.py:399
  14.7 0.2 collective-permute-start.10
  14.9 2.5 %collective-permute-start.11 = (bf16[2,5,4,6400]{3,2,1,0:T(4,128)(2,1)S(1)}, bf16[2,5,4,6400]{3,2,1,0:T(4,128)(2,1)S(1)}, u32[]{:S(2)}, u32[]{:S(2)}) collective-permute-start(bf16[2,5,4,6400]{3,2,1,0:T(4,128)(2,1)S(1)} %pad_maximum_fusion), channel_id=1, source_target_pairs={{0,48},{1,49},{2,50},{3,51},{4,52},{5,53},{6,54},{7,55},{8,56},{9,... | collective-permute-start | bytes 1536008 | tf_op jit(solution)/shard_map/ppermute | solution.py:399
  17.4 3.0 %collective-permute-start.3 = (bf16[416,256]{1,0:T(8,128)(2,1)S(1)}, bf16[416,256]{1,0:T(8,128)(2,1)S(1)}, u32[]{:S(2)}, u32[]{:S(2)}) collective-permute-start(bf16[416,256]{1,0:T(8,128)(2,1)S(1)} %pad_maximum_fusion.1.refs_0_), channel_id=1, source_target_pairs={{0,1},{1,0},{2,3},{3,2},{4,5},{5,4},{6,7},{7,6},{8,9},{9,8},{10,11... | collective-permute-start | bytes 638984 | tf_op jit(solution)/shard_map/ppermute | solution.py:399
  20.3 0.0 collective-permute-done.4.refs_2_
  20.3 2.7 %collective-permute-start.5 = (bf16[416,256]{1,0:T(8,128)(2,1)S(1)}, bf16[416,256]{1,0:T(8,128)(2,1)S(1)}, u32[]{:S(2)}, u32[]{:S(2)}) collective-permute-start(bf16[416,256]{1,0:T(8,128)(2,1)S(1)} %collective-permute-done.4.refs_2_), channel_id=1, source_target_pairs={{0,1},{1,0},{2,3},{3,2},{4,5},{5,4},{6,7},{7,6},{8,9},{9,8},{10,11... | collective-permute-start | bytes 638984 | tf_op jit(solution)/shard_map/ppermute | solution.py:399
  23.0 1.3 %collective-permute-start.12 = (bf16[1,5,4,6400]{3,2,1,0:T(4,128)(2,1)S(1)}, bf16[1,5,4,6400]{3,2,1,0:T(4,128)(2,1)S(1)}, u32[]{:S(2)}, u32[]{:S(2)}) collective-permute-start(bf16[1,5,4,6400]{3,2,1,0:T(4,128)(2,1)S(1)} %collective-permute-done.1.refs_0_), channel_id=1, source_target_pairs={{0,32},{1,33},{2,34},{3,35},{4,36},{5,37},{6,38},{7,39},{8,40},{9,... | collective-permute-start | bytes 768008 | tf_op jit(solution)/shard_map/ppermute | solution.py:399
  24.3 0.0 collective-permute-done.3.refs_1_
  24.3 1.5 %collective-permute-start.6 = (bf16[416,256]{1,0:T(8,128)(2,1)S(1)}, bf16[416,256]{1,0:T(8,128)(2,1)S(1)}, u32[]{:S(2)}, u32[]{:S(2)}) collective-permute-start(bf16[416,256]{1,0:T(8,128)(2,1)S(1)} %pad_maximum_fusion.1.refs_0_), channel_id=1, source_target_pairs={{0,12},{1,13},{2,14},{3,15},{4,0},{5,1},{6,2},{7,3},{8,4},{9,5},{1... | collective-permute-start | bytes 638984 | tf_op jit(solution)/shard_map/ppermute | solution.py:399
  25.8 0.0 collective-permute-done.5.refs_3_
  25.8 0.0 collective-permute-start.8
  25.8 0.0 copy-done.1
  25.8 4.4 %strengths.2 = (f32[2,2000,128]{2,1,0:T(8,128)S(1)}, s32[1,8,128]{2,1,0:T(8,128)S(1)}) custom-call(f32[6,32]{1,0:T(8,128)S(1)} %bitcast.16, s32[3,200]{1,0:T(4,128)S(1)} %copy-done.2, bf16[416,256]{1,0:T(8,128)(2,1)S(1)} %pad_maximum_fusion.1.refs_0_, bf16[416,256]{1,0:T(8,128)(2,1)S(1)} %collective-permute-done.3.refs_1_, ...), custom_call_target="tpu_custom_call" | custom-call | flops 1000 | bytes 1000 | tf_op jit(solution)/shard_map/strengths/pallas_call | solution.py:267
  30.2 0.0 copy-start
  30.2 2.6 %collective-permute-done.12.refs_4_ = bf16[1,5,4,6400]{3,2,1,0:T(4,128)(2,1)S(1)} collective-permute-done((bf16[1,5,4,6400]{3,2,1,0:T(4,128)(2,1)S(1)}, bf16[1,5,4,6400]{3,2,1,0:T(4,128)(2,1)S(1)}, u32[]{:S(2)}, u32[]{:S(2)}) %collective-permute-start.12) | collective-permute-done | bytes 256032 | tf_op jit(solution)/shard_map/ppermute | solution.py:399
  32.8 0.0 collective-permute-done.10.refs_2_
  32.8 0.0 collective-permute-done.11.refs_3_
  32.8 2.6 %collective-permute-start.15 = (bf16[2,5,4,6400]{3,2,1,0:T(4,128)(2,1)S(1)}, bf16[2,5,4,6400]{3,2,1,0:T(4,128)(2,1)S(1)}, u32[]{:S(2)}, u32[]{:S(2)}) collective-permute-start(bf16[2,5,4,6400]{3,2,1,0:T(4,128)(2,1)S(1)} %collective-permute-done.10.refs_2_), channel_id=1, source_target_pairs={{0,1},{1,0},{2,3},{3,2},{4,5},{5,4},{6,7},{7,6},{8,9},{9,8},{10,11... | collective-permute-start | bytes 1536008 | tf_op jit(solution)/shard_map/ppermute | solution.py:399
  35.5 0.0 collective-permute-start.16
  35.5 0.0 collective-permute-done.6.refs_0_
  35.5 0.5 %collective-permute-start.7 = (bf16[416,256]{1,0:T(8,128)(2,1)S(1)}, bf16[416,256]{1,0:T(8,128)(2,1)S(1)}, u32[]{:S(2)}, u32[]{:S(2)}) collective-permute-start(bf16[416,256]{1,0:T(8,128)(2,1)S(1)} %collective-permute-done.6.refs_0_), channel_id=1, source_target_pairs={{0,1},{1,0},{2,3},{3,2},{4,5},{5,4},{6,7},{7,6},{8,9},{9,8},{10,11... | collective-permute-start | bytes 638984 | tf_op jit(solution)/shard_map/ppermute | solution.py:399
  36.0 0.0 collective-permute-done.8.refs_2_
  36.0 0.3 collective-permute-start.9
  36.2 0.2 collective-permute-start.14
  36.5 1.5 %collective-permute-done.7.refs_1_ = bf16[416,256]{1,0:T(8,128)(2,1)S(1)} collective-permute-done((bf16[416,256]{1,0:T(8,128)(2,1)S(1)}, bf16[416,256]{1,0:T(8,128)(2,1)S(1)}, u32[]{:S(2)}, u32[]{:S(2)}) %collective-permute-start.7) | collective-permute-done | bytes 213024 | tf_op jit(solution)/shard_map/ppermute | solution.py:399
  38.0 0.4 collective-permute-start.13
  38.4 0.0 collective-permute-done.9.refs_3_
  38.4 0.3 collective-permute-start.17
  38.7 4.4 %strengths.3 = (f32[2,2000,128]{2,1,0:T(8,128)S(1)}, s32[1,8,128]{2,1,0:T(8,128)S(1)}) custom-call(f32[6,32]{1,0:T(8,128)S(1)} %bitcast.17, s32[3,200]{1,0:T(4,128)S(1)} %copy-done.2, bf16[416,256]{1,0:T(8,128)(2,1)S(1)} %collective-permute-done.6.refs_0_, bf16[416,256]{1,0:T(8,128)(2,1)S(1)} %collective-permute-done.7.refs_1_, ...), custom_call_target="tpu_custom_call" | custom-call | flops 1000 | bytes 1000 | tf_op jit(solution)/shard_map/strengths/pallas_call | solution.py:267
  43.1 0.0 collective-permute-done.13.refs_5_
  43.1 0.0 collective-permute-done.14.refs_6_
  43.1 0.0 collective-permute-done.17.refs_9_
  43.1 0.0 collective-permute-done.15.refs_7_
  43.1 0.0 collective-permute-done.16.refs_8_
  43.2 0.0 copy-done
  43.2 7.0 %contract.1 = f32[10,4,400]{2,1,0:T(4,128)} custom-call(s32[10]{0:T(128)S(1)} %stack.43.where_ref, s32[1,8,128]{2,1,0:T(8,128)S(1)} %get-tuple-element.27.off_a_ref, s32[1,8,128]{2,1,0:T(8,128)S(1)} %get-tuple-element.30.off_b_ref, bf16[10,4,6400]{2,1,0:T(4,128)(2,1)S(1)} %copy-done, bf16[1,5,4,6400]{3,2,1,0:T(4,128)(2,1)S(1)} %collective-permute-done.1.refs_0_, ...), custom_call_target="tpu_custom_call" | custom-call | flops 2000000000 | bytes 9000000 | tf_op jit(solution)/shard_map/contract/pallas_call | solution.py:372
  (1 shorter events, 0.0 us)
Async XLA Ops:
  1.0 11.0 %collective-permute-start.1 = (bf16[1,5,4,6400]{3,2,1,0:T(4,128)(2,1)S(1)}, bf16[1,5,4,6400]{3,2,1,0:T(4,128)(2,1)S(1)}, u32[]{:S(2)}, u32[]{:S(2)}) collective-permute-start(bf16[1,5,4,6400]{3,2,1,0:T(4,128)(2,1)S(1)} %dynamic-slice_bitcast_fusion), channel_id=1, source_target_pairs={{0,64},{1,65},{2,66},{3,67},{4,68},{5,69},{6,70},{7,71},{8,72},{9,... | collective-permute-start | bytes 768008 | tf_op jit(solution)/shard_map/ppermute | solution.py:399
  3.2 9.7 %collective-permute-start.2 = (bf16[1,5,4,6400]{3,2,1,0:T(4,128)(2,1)S(1)}, bf16[1,5,4,6400]{3,2,1,0:T(4,128)(2,1)S(1)}, u32[]{:S(2)}, u32[]{:S(2)}) collective-permute-start(bf16[1,5,4,6400]{3,2,1,0:T(4,128)(2,1)S(1)} %dynamic-slice_bitcast_fusion), channel_id=1, source_target_pairs={{0,32},{1,33},{2,34},{3,35},{4,36},{5,37},{6,38},{7,39},{8,40},{9,... | collective-permute-start | bytes 768008 | tf_op jit(solution)/shard_map/ppermute | solution.py:399
  7.7 5.2 %collective-permute-start = (bf16[208,256]{1,0:T(8,128)(2,1)}, bf16[208,256]{1,0:T(8,128)(2,1)S(1)}, u32[]{:S(2)}, u32[]{:S(2)}) collective-permute-start(bf16[208,256]{1,0:T(8,128)(2,1)} %pack.1), channel_id=1, source_target_pairs={{0,66},{1,67},{2,64},{3,65},{4,70},{5,71},{6,68},{7,69},{8,74},{9,... | collective-permute-start | bytes 319496 | tf_op jit(solution)/shard_map/ppermute | solution.py:399
  9.7 0.7 %copy-start.2 = (s32[3,200]{1,0:T(4,128)S(1)}, s32[3,200]{1,0:T(4,128)}, u32[]{:S(2)}) copy-start(s32[3,200]{1,0:T(4,128)} %lattice_ref.5) | copy-start | bytes 7204
  10.4 2.6 %copy-start.3 = (bf16[208,256]{1,0:T(8,128)(2,1)S(1)}, bf16[208,256]{1,0:T(8,128)(2,1)}, u32[]{:S(2)}) copy-start(bf16[208,256]{1,0:T(8,128)(2,1)} %pack.1) | copy-start | bytes 319492
  10.4 15.4 %copy-start.1 = (f32[32,6]{0,1:T(8,128)S(1)}, f32[32,6]{0,1:T(8,128)}, u32[]{:S(2)}) copy-start(f32[32,6]{0,1:T(8,128)} %param.10) | copy-start | bytes 2308
  13.0 7.3 %collective-permute-start.4 = (bf16[416,256]{1,0:T(8,128)(2,1)S(1)}, bf16[416,256]{1,0:T(8,128)(2,1)S(1)}, u32[]{:S(2)}, u32[]{:S(2)}) collective-permute-start(bf16[416,256]{1,0:T(8,128)(2,1)S(1)} %pad_maximum_fusion.1.refs_0_), channel_id=1, source_target_pairs={{0,4},{1,5},{2,6},{3,7},{4,8},{5,9},{6,10},{7,11},{8,12},{9,13},{1... | collective-permute-start | bytes 638984 | tf_op jit(solution)/shard_map/ppermute | solution.py:399
  14.7 18.1 %collective-permute-start.10 = (bf16[2,5,4,6400]{3,2,1,0:T(4,128)(2,1)S(1)}, bf16[2,5,4,6400]{3,2,1,0:T(4,128)(2,1)S(1)}, u32[]{:S(2)}, u32[]{:S(2)}) collective-permute-start(bf16[2,5,4,6400]{3,2,1,0:T(4,128)(2,1)S(1)} %pad_maximum_fusion), channel_id=1, source_target_pairs={{0,16},{1,17},{2,18},{3,19},{4,20},{5,21},{6,22},{7,23},{8,24},{9,... | collective-permute-start | bytes 1536008 | tf_op jit(solution)/shard_map/ppermute | solution.py:399
  14.9 18.0 %collective-permute-start.11 = (bf16[2,5,4,6400]{3,2,1,0:T(4,128)(2,1)S(1)}, bf16[2,5,4,6400]{3,2,1,0:T(4,128)(2,1)S(1)}, u32[]{:S(2)}, u32[]{:S(2)}) collective-permute-start(bf16[2,5,4,6400]{3,2,1,0:T(4,128)(2,1)S(1)} %pad_maximum_fusion), channel_id=1, source_target_pairs={{0,48},{1,49},{2,50},{3,51},{4,52},{5,53},{6,54},{7,55},{8,56},{9,... | collective-permute-start | bytes 1536008 | tf_op jit(solution)/shard_map/ppermute | solution.py:399
  17.4 6.9 %collective-permute-start.3 = (bf16[416,256]{1,0:T(8,128)(2,1)S(1)}, bf16[416,256]{1,0:T(8,128)(2,1)S(1)}, u32[]{:S(2)}, u32[]{:S(2)}) collective-permute-start(bf16[416,256]{1,0:T(8,128)(2,1)S(1)} %pad_maximum_fusion.1.refs_0_), channel_id=1, source_target_pairs={{0,1},{1,0},{2,3},{3,2},{4,5},{5,4},{6,7},{7,6},{8,9},{9,8},{10,11... | collective-permute-start | bytes 638984 | tf_op jit(solution)/shard_map/ppermute | solution.py:399
  20.3 5.5 %collective-permute-start.5 = (bf16[416,256]{1,0:T(8,128)(2,1)S(1)}, bf16[416,256]{1,0:T(8,128)(2,1)S(1)}, u32[]{:S(2)}, u32[]{:S(2)}) collective-permute-start(bf16[416,256]{1,0:T(8,128)(2,1)S(1)} %collective-permute-done.4.refs_2_), channel_id=1, source_target_pairs={{0,1},{1,0},{2,3},{3,2},{4,5},{5,4},{6,7},{7,6},{8,9},{9,8},{10,11... | collective-permute-start | bytes 638984 | tf_op jit(solution)/shard_map/ppermute | solution.py:399
  23.0 9.8 %collective-permute-start.12 = (bf16[1,5,4,6400]{3,2,1,0:T(4,128)(2,1)S(1)}, bf16[1,5,4,6400]{3,2,1,0:T(4,128)(2,1)S(1)}, u32[]{:S(2)}, u32[]{:S(2)}) collective-permute-start(bf16[1,5,4,6400]{3,2,1,0:T(4,128)(2,1)S(1)} %collective-permute-done.1.refs_0_), channel_id=1, source_target_pairs={{0,32},{1,33},{2,34},{3,35},{4,36},{5,37},{6,38},{7,39},{8,40},{9,... | collective-permute-start | bytes 768008 | tf_op jit(solution)/shard_map/ppermute | solution.py:399
  24.3 11.2 %collective-permute-start.6 = (bf16[416,256]{1,0:T(8,128)(2,1)S(1)}, bf16[416,256]{1,0:T(8,128)(2,1)S(1)}, u32[]{:S(2)}, u32[]{:S(2)}) collective-permute-start(bf16[416,256]{1,0:T(8,128)(2,1)S(1)} %pad_maximum_fusion.1.refs_0_), channel_id=1, source_target_pairs={{0,12},{1,13},{2,14},{3,15},{4,0},{5,1},{6,2},{7,3},{8,4},{9,5},{1... | collective-permute-start | bytes 638984 | tf_op jit(solution)/shard_map/ppermute | solution.py:399
  25.8 10.2 %collective-permute-start.8 = (bf16[416,256]{1,0:T(8,128)(2,1)S(1)}, bf16[416,256]{1,0:T(8,128)(2,1)S(1)}, u32[]{:S(2)}, u32[]{:S(2)}) collective-permute-start(bf16[416,256]{1,0:T(8,128)(2,1)S(1)} %pad_maximum_fusion.1.refs_0_), channel_id=1, source_target_pairs={{0,8},{1,9},{2,10},{3,11},{4,12},{5,13},{6,14},{7,15},{8,0},{9,1},... | collective-permute-start | bytes 638984 | tf_op jit(solution)/shard_map/ppermute | solution.py:399
  30.2 12.9 %copy-start = (bf16[10,4,6400]{2,1,0:T(4,128)(2,1)S(1)}, bf16[10,4,6400]{2,1,0:T(4,128)(2,1)}, u32[]{:S(2)}) copy-start(bf16[10,4,6400]{2,1,0:T(4,128)(2,1)} %own.1) | copy-start | bytes 1536004
  32.8 10.3 %collective-permute-start.15 = (bf16[2,5,4,6400]{3,2,1,0:T(4,128)(2,1)S(1)}, bf16[2,5,4,6400]{3,2,1,0:T(4,128)(2,1)S(1)}, u32[]{:S(2)}, u32[]{:S(2)}) collective-permute-start(bf16[2,5,4,6400]{3,2,1,0:T(4,128)(2,1)S(1)} %collective-permute-done.10.refs_2_), channel_id=1, source_target_pairs={{0,1},{1,0},{2,3},{3,2},{4,5},{5,4},{6,7},{7,6},{8,9},{9,8},{10,11... | collective-permute-start | bytes 1536008 | tf_op jit(solution)/shard_map/ppermute | solution.py:399
  35.5 7.7 %collective-permute-start.16 = (bf16[2,5,4,6400]{3,2,1,0:T(4,128)(2,1)S(1)}, bf16[2,5,4,6400]{3,2,1,0:T(4,128)(2,1)S(1)}, u32[]{:S(2)}, u32[]{:S(2)}) collective-permute-start(bf16[2,5,4,6400]{3,2,1,0:T(4,128)(2,1)S(1)} %collective-permute-done.11.refs_3_), channel_id=1, source_target_pairs={{0,1},{1,0},{2,3},{3,2},{4,5},{5,4},{6,7},{7,6},{8,9},{9,8},{10,11... | collective-permute-start | bytes 1536008 | tf_op jit(solution)/shard_map/ppermute | solution.py:399
  35.5 2.5 %collective-permute-start.7 = (bf16[416,256]{1,0:T(8,128)(2,1)S(1)}, bf16[416,256]{1,0:T(8,128)(2,1)S(1)}, u32[]{:S(2)}, u32[]{:S(2)}) collective-permute-start(bf16[416,256]{1,0:T(8,128)(2,1)S(1)} %collective-permute-done.6.refs_0_), channel_id=1, source_target_pairs={{0,1},{1,0},{2,3},{3,2},{4,5},{5,4},{6,7},{7,6},{8,9},{9,8},{10,11... | collective-permute-start | bytes 638984 | tf_op jit(solution)/shard_map/ppermute | solution.py:399
  36.0 2.4 %collective-permute-start.9 = (bf16[416,256]{1,0:T(8,128)(2,1)S(1)}, bf16[416,256]{1,0:T(8,128)(2,1)S(1)}, u32[]{:S(2)}, u32[]{:S(2)}) collective-permute-start(bf16[416,256]{1,0:T(8,128)(2,1)S(1)} %collective-permute-done.8.refs_2_), channel_id=1, source_target_pairs={{0,1},{1,0},{2,3},{3,2},{4,5},{5,4},{6,7},{7,6},{8,9},{9,8},{10,11... | collective-permute-start | bytes 638984 | tf_op jit(solution)/shard_map/ppermute | solution.py:399
  36.2 6.9 %collective-permute-start.14 = (bf16[1,5,4,6400]{3,2,1,0:T(4,128)(2,1)S(1)}, bf16[1,5,4,6400]{3,2,1,0:T(4,128)(2,1)S(1)}, u32[]{:S(2)}, u32[]{:S(2)}) collective-permute-start(bf16[1,5,4,6400]{3,2,1,0:T(4,128)(2,1)S(1)} %collective-permute-done.2.refs_1_), channel_id=1, source_target_pairs={{0,1},{1,0},{2,3},{3,2},{4,5},{5,4},{6,7},{7,6},{8,9},{9,8},{10,11... | collective-permute-start | bytes 768008 | tf_op jit(solution)/shard_map/ppermute | solution.py:399
  38.0 5.1 %collective-permute-start.13 = (bf16[1,5,4,6400]{3,2,1,0:T(4,128)(2,1)S(1)}, bf16[1,5,4,6400]{3,2,1,0:T(4,128)(2,1)S(1)}, u32[]{:S(2)}, u32[]{:S(2)}) collective-permute-start(bf16[1,5,4,6400]{3,2,1,0:T(4,128)(2,1)S(1)} %collective-permute-done.1.refs_0_), channel_id=1, source_target_pairs={{0,1},{1,0},{2,3},{3,2},{4,5},{5,4},{6,7},{7,6},{8,9},{9,8},{10,11... | collective-permute-start | bytes 768008 | tf_op jit(solution)/shard_map/ppermute | solution.py:399
  38.4 4.7 %collective-permute-start.17 = (bf16[1,5,4,6400]{3,2,1,0:T(4,128)(2,1)S(1)}, bf16[1,5,4,6400]{3,2,1,0:T(4,128)(2,1)S(1)}, u32[]{:S(2)}, u32[]{:S(2)}) collective-permute-start(bf16[1,5,4,6400]{3,2,1,0:T(4,128)(2,1)S(1)} %collective-permute-done.12.refs_4_), channel_id=1, source_target_pairs={{0,1},{1,0},{2,3},{3,2},{4,5},{5,4},{6,7},{7,6},{8,9},{9,8},{10,11... | collective-permute-start | bytes 768008 | tf_op jit(solution)/shard_map/ppermute | solution.py:399
